TPU v7x, 512 devices: a whole 4x4x16 slice. The times are simulated.
512 devices in a mesh: row: 32 (over y, x, core), col: 16 (over z).
Axes of the slice: x: 4, y: 4, z: 16, core: 2. Of those that a mesh axis runs over, the one named last changes fastest.
Arguments:
- matrix: bfloat16 [16384, 16, 2, 512], P('row', 'col'), as said below
- inverses: float32 [2, 512, 512], replicated, as said below
Outputs:
- factored: bfloat16 [16384, 16, 2, 512], P('row', 'col')
Inputs may be any that keep to these rules, and one draw needn't show every extreme that they name: Entries off the diagonal of the whole matrix lie within [-6, 6]; its diagonal entries lie between 3.2 * sqrt(512) and 5 * sqrt(512). Each inverses[s] has diagonal entries between 0.7 and 1.3 times 1 / (4 sqrt(512)) and off-diagonal entries at most 0.4 / 2048 in magnitude.
All inputs are finite; a program needn't handle non-finite values.
Results may differ from a plain program's by a relative error of at most 0.0035.
Values may be sent and summed in bfloat16 or wider, within the bound.
No kernel may reach another device: no remote copies, remote signals or barrier semaphores. Data moves between devices by JAX's collectives and lax.ppermute only.
A program may use at most 64 MiB of HBM per device.

v0:
```python
import jax
import jax.numpy as jnp
from jax import lax
from jax.sharding import PartitionSpec as P

highest = lax.Precision.HIGHEST


def spread(value, axis, source):
    kept = jnp.where(lax.axis_index(axis) == source, value, 0).astype(value.dtype)
    return lax.psum(kept, axis)


def factor_panel(column, diagonal, approx):
    size_rows = column.shape[0]
    identity = jnp.eye(size_rows, dtype=jnp.float32)
    product = jnp.dot(diagonal, approx, precision=highest)
    inverse = jnp.dot(approx, 2.0 * identity - product, precision=highest).astype(jnp.bfloat16)
    return jnp.dot(column, inverse.astype(jnp.float32), precision=highest)


def panel_step(blocks, upper_rows, step_index, grid_row, col_count, inverses):
    local_index = step_index // col_count
    diagonal = upper_rows[local_index].astype(jnp.float32)
    lower_full = factor_panel(blocks[local_index], diagonal, inverses[step_index])
    return jnp.where(grid_row > step_index, lower_full, 0.0).astype(jnp.bfloat16)


def place_panel(blocks, lower_part, step_index, grid_row, grid_col, col_count):
    local_index = step_index // col_count
    owner = (grid_col == step_index % col_count) & (grid_row > step_index)
    fresh = list(blocks)
    fresh[local_index] = jnp.where(owner, lower_part.astype(jnp.float32), blocks[local_index])
    return fresh


def update_block(block, lower_recv, upper_piece, global_block, grid_row, step_index):
    active = (global_block > step_index) & (grid_row > step_index)
    change = jnp.dot(lower_recv, upper_piece, preferred_element_type=jnp.float32)
    return jnp.where(active, block - change, block)


def local(matrix, inverses):
    col_count = lax.axis_size("col")
    grid_row = lax.axis_index("row")
    grid_col = lax.axis_index("col")
    local_count = matrix.shape[2]
    blocks = [
        matrix[:, 0, local_block, :].astype(jnp.float32) for local_block in range(local_count)
    ]
    for step_index in range(2):
        upper_rows = spread(jnp.stack(blocks).astype(jnp.bfloat16), "row", step_index)
        lower_part = panel_step(blocks, upper_rows, step_index, grid_row, col_count, inverses)
        lower_recv = spread(lower_part, "col", step_index % col_count)
        blocks = place_panel(blocks, lower_part, step_index, grid_row, grid_col, col_count)
        blocks = [
            update_block(
                blocks[local_block],
                lower_recv,
                upper_rows[local_block],
                grid_col + col_count * local_block,
                grid_row,
                step_index,
            )
            for local_block in range(local_count)
        ]
    return jnp.stack(blocks, axis=1).astype(jnp.bfloat16)[:, None]


def solution(mesh):
    return jax.shard_map(
        local,
        mesh=mesh,
        in_specs=(P("row", "col", None, None), P()),
        out_specs=P("row", "col", None, None),
        check_vma=False,
    )
```

profile of v0, /device:TPU:1, one launch (start us, length us, event | category | flops | bytes accessed | tf_op | source)
XLA Modules:
  0.0 583.5 jit_solution(5877331499601619421)
XLA Ops:
  6.5 0.0 all-reduce.5.cloned.1.call-start
  6.5 3.4 fusion.16
  9.9 0.0 copy-start.3
  9.9 0.0 copy-start.1
  9.9 1.0 copy-done.3
  10.9 1.2 copy_bitcast_fusion
  12.2 2.4 maximum_select_fusion
  14.6 0.0 copy-done.1
  14.6 0.0 all-reduce.5.cloned.1.call-update
  14.6 0.0 all-reduce.7.cloned.1.call-start
  14.7 0.0 copy-start.4
  14.7 140.9 %all-reduce.5.cloned.1.call-done = bf16[2,512,512]{2,1,0:T(8,128)(2,1)} async-done(((bf16[2,512,512]{2,1,0:T(8,128)(2,1)}), bf16[2,512,512]{2,1,0:T(8,128)(2,1)}) %all-reduce.5.cloned.1.call-update) | async-done | bytes 1048592 | tf_op jit(solution)/shard_map/psum | solution.py:11
  155.6 0.0 copy-done
  155.6 2.1 select_subtract_fusion.1
  157.7 3.5 convolution_convert_fusion.1
  161.2 0.0 copy-done.4
  161.2 0.5 fusion.1
  161.7 0.8 copy-done.9
  162.5 0.8 select_bitcast_fusion
  163.3 0.0 all-reduce.7.cloned.1.call-update
  163.3 0.0 all-reduce.9.cloned.1.call-start
  163.4 2.1 copy.5
  165.5 125.2 %all-reduce.7.cloned.1.call-done = bf16[512,512]{0,1:T(8,128)(2,1)} async-done(((bf16[512,512]{0,1:T(8,128)(2,1)}), bf16[512,512]{0,1:T(8,128)(2,1)}) %all-reduce.7.cloned.1.call-update) | async-done | bytes 524304 | tf_op jit(solution)/shard_map/psum | solution.py:11
  290.7 2.3 subtract_select_fusion.3
  293.0 0.1 convert_bitcast_fusion.1
  293.1 0.0 copy-done.12
  293.1 0.5 subtract_select_fusion.2
  293.6 0.0 copy-start.5
  293.6 1.0 copy-done.5
  294.6 0.1 convert_bitcast_fusion
  294.7 1.1 maximum_select_fusion.1
  295.8 0.0 all-reduce.9.cloned.1.call-update
  295.8 0.2 all-reduce.11.cloned.1.call-start
  296.0 141.7 %all-reduce.9.cloned.1.call-done = bf16[2,512,512]{2,1,0:T(8,128)(2,1)} async-done(((bf16[2,512,512]{2,1,0:T(8,128)(2,1)}), bf16[2,512,512]{2,1,0:T(8,128)(2,1)}) %all-reduce.9.cloned.1.call-update) | async-done | bytes 1048592 | tf_op jit(solution)/shard_map/psum | solution.py:11
  437.7 2.1 select_subtract_fusion
  439.8 3.5 convolution_convert_fusion
  443.3 0.0 copy-start.6
  443.3 0.0 copy-start.7
  443.3 2.0 broadcast_select_fusion
  445.3 0.0 all-reduce.11.cloned.1.call-update
  445.4 127.4 %all-reduce.11.cloned.1.call-done = bf16[512,512]{1,0:T(8,128)(2,1)} async-done(((bf16[512,512]{1,0:T(8,128)(2,1)}), bf16[512,512]{1,0:T(8,128)(2,1)}) %all-reduce.11.cloned.1.call-update) | async-done | bytes 524304 | tf_op jit(solution)/shard_map/psum | solution.py:11
  572.7 0.0 copy-done.6
  572.7 1.6 fusion.4
  574.3 0.0 copy-done.8
  574.3 0.0 copy-done.10
  574.3 0.4 fusion.5
  574.8 0.1 pad_maximum_fusion
  574.9 2.0 copy.6
  (10 shorter events, 0.0 us)
Async XLA Ops:
  6.5 149.0 %all-reduce.5.cloned.1.call-start = ((), (), s32[]{:S(2)}) async-start(), calls=%async_computation | async-start | bytes 2097152 | tf_op jit(solution)/shard_map/psum | solution.py:11
  9.9 1.0 copy-start.3
  9.9 4.7 copy-start.1
  12.2 143.4 %copy-start = (f32[2,512,512]{2,1,0:T(8,128)S(1)}, f32[2,512,512]{2,1,0:T(8,128)}, u32[]{:S(2)}) copy-start(f32[2,512,512]{2,1,0:T(8,128)} %param.3) | copy-start | bytes 6291460
  14.6 276.1 %all-reduce.7.cloned.1.call-start = ((), (), s32[]{:S(2)}) async-start(), calls=%async_computation.1 | async-start | bytes 1048576 | tf_op jit(solution)/shard_map/psum | solution.py:11
  14.7 146.5 %copy-start.4 = (bf16[512,1,1,512]{3,2,1,0:T(2,128)(2,1)S(1)}, bf16[512,1,1,512]{3,2,1,0:T(2,128)(2,1)}, u32[]{:S(2)}) copy-start(bf16[512,1,1,512]{3,2,1,0:T(2,128)(2,1)} %copy-done.3) | copy-start | bytes 1572868
  161.7 0.8 copy-start.9
  163.3 274.3 %all-reduce.9.cloned.1.call-start = ((), (), s32[]{:S(2)}) async-start(), calls=%async_computation.2 | async-start | bytes 2097152 | tf_op jit(solution)/shard_map/psum | solution.py:11
  290.7 2.4 copy-start.2
  290.7 2.4 copy-start.11
  290.7 2.5 copy-start.12
  293.6 1.0 copy-start.5
  295.8 276.9 %all-reduce.11.cloned.1.call-start = ((), (), s32[]{:S(2)}) async-start(), calls=%async_computation.3 | async-start | bytes 1048576 | tf_op jit(solution)/shard_map/psum | solution.py:11
  443.3 129.5 %copy-start.6 = (f32[512,512]{1,0:T(8,128)S(1)}, f32[512,512]{1,0:T(8,128)}, u32[]{:S(2)}) copy-start(f32[512,512]{1,0:T(8,128)} %copy-done.5) | copy-start | bytes 3145732
  443.3 129.5 %copy-start.7 = (bf16[2,512,512]{2,1,0:T(8,128)(2,1)S(1)}, bf16[2,512,512]{2,1,0:T(8,128)(2,1)}, u32[]{:S(2)}) copy-start(bf16[2,512,512]{2,1,0:T(8,128)(2,1)} %all-reduce.9.cloned.1.call-done) | copy-start | bytes 3145732
  572.7 1.6 copy-start.8
  572.7 1.6 copy-start.10
Sparse Core Ops, SparseCore 0:
  14.7 140.7 all-reduce.4
  163.5 127.1 all-reduce.6
  295.9 141.7 all-reduce.8
  445.5 127.2 all-reduce.10
where the time goes:
time: 592 us; the launch traced here: 583 us
  waiting for transfers between devices  535 us (90%)
  matrix products  18.5 us (3%)
  between operations  13.4 us (2%)
  local copies, waits for them, and re-layouts  11.5 us (2%)
    psum x4, waiting for transfers between devices, spread(): return lax.psum(kept, axis)  535 us
  transfers between devices with their start and end apart: 4, of which 4 were waited for; matrix products, arithmetic and copies ran while one was open for 0% of the time, Pallas kernels for 0%

commit v1 on v0

v1 whole, which is shorter than its diff:
```python
import jax
import jax.numpy as jnp
from jax import lax
from jax.sharding import PartitionSpec as P

highest = lax.Precision.HIGHEST


def refined_inverse(diagonal, approx):
    identity = jnp.eye(diagonal.shape[0], dtype=jnp.float32)
    product = jnp.dot(diagonal.astype(jnp.float32), approx, precision=highest)
    return jnp.dot(approx, 2.0 * identity - product, precision=highest).astype(jnp.bfloat16)


def minus_product(base, left, right):
    return base.astype(jnp.float32) - jnp.dot(left, right, preferred_element_type=jnp.float32)


def panel_tree(panel, cols):
    held = panel
    col = lax.axis_index("col")
    reach = cols // 2
    while reach >= 2:
        step = 2 * reach
        pairs = [(s, (s - reach) % cols) for s in range(0, cols, step)]
        pairs += [(s + 1, (s + 1 + reach) % cols) for s in range(0, cols, step)]
        got = lax.ppermute(held, "col", pairs)
        holds = ((col - col % 2) % step) == 0
        held = jnp.where(holds, held, got)
        reach //= 2
    pairs = [(s, (s - 1) % cols) if s % 2 == 0 else (s, (s + 1) % cols) for s in range(cols)]
    other = lax.ppermute(held, "col", pairs)
    even = col % 2 == 0
    return jnp.where(even, held, other), jnp.where(even, other, held)


def spread_diagonal(piece, cols):
    col = lax.axis_index("col")
    quarter = cols // 4
    got = [
        lax.ppermute(piece, "col", [(0, quarter * k), (1, quarter * k + 1)]) for k in range(1, 4)
    ]
    held = jnp.where(col < 2, piece, got[0] + got[1] + got[2])
    groups = range(0, cols, 4)
    swap = lax.ppermute(held, "col", [p for g in groups for p in ((g, g + 1), (g + 1, g))])
    near = lax.ppermute(held, "col", [p for g in groups for p in ((g, g + 2), (g + 1, g + 3))])
    far = lax.ppermute(held, "col", [p for g in groups for p in ((g, g + 3), (g + 1, g + 2))])
    place = col % 4
    first = jnp.where(place == 0, held, jnp.where(place == 1, swap, jnp.where(place == 2, near, far)))
    second = jnp.where(place == 0, swap, jnp.where(place == 1, held, jnp.where(place == 2, far, near)))
    return jnp.stack([first, second])


def local(matrix, inverses):
    rows, cols = lax.axis_size("row"), lax.axis_size("col")
    row, col = lax.axis_index("row"), lax.axis_index("col")
    size = matrix.shape[0]
    chips = rows // 2
    part = size // chips
    same_core = [[2 * chip + core for chip in range(chips)] for core in range(2)]
    swap_core = [(r, r ^ 1) for r in range(rows)]
    core = row % 2

    with jax.named_scope("panels"):
        panel0, panel1 = panel_tree(matrix[:, 0, 0, :], cols)

    with jax.named_scope("scatter_rows"):
        dealt = lax.all_to_all(
            matrix, "row", 0, 0, tiled=True, axis_index_groups=same_core
        )[:part, 0]
    with jax.named_scope("gather_rows"):
        upper = lax.all_gather(dealt.reshape(part, -1), "row", axis=0, tiled=False)
        upper = upper.reshape(chips, 2, part, -1)
        upper0 = upper[:, 0].reshape(size, -1)
        raw1 = upper[:, 1].reshape(size, -1)
    with jax.named_scope("diagonal"):
        pieces = spread_diagonal(dealt[:, 0, :], cols)
        copies = jnp.broadcast_to(pieces[None], (chips,) + pieces.shape)
        mine = lax.all_to_all(copies, "row", 0, 0, tiled=True, axis_index_groups=same_core)
        other = lax.ppermute(mine, "row", swap_core)
        top = jnp.where(core == 0, mine, other)
        low = jnp.where(core == 0, other, mine)
        d00, d01 = (top[:, k].reshape(size, size) for k in range(2))
        d10, d11 = (low[:, k].reshape(size, size) for k in range(2))
    with jax.named_scope("inverses"):
        inverse0 = refined_inverse(d00, inverses[0])
        lower10 = jnp.dot(d10, inverse0, preferred_element_type=jnp.float32).astype(jnp.bfloat16)
        upper11 = minus_product(d11, lower10, d01).astype(jnp.bfloat16)
        inverse1 = refined_inverse(upper11, inverses[1])
    with jax.named_scope("update"):
        upper1 = minus_product(raw1, lower10, upper0).astype(jnp.bfloat16)
        lower0 = jnp.dot(panel0, inverse0, preferred_element_type=jnp.float32).astype(jnp.bfloat16)
        lower1 = jnp.dot(
            minus_product(panel1, lower0, d01), inverse1.astype(jnp.float32), precision=highest
        ).astype(jnp.bfloat16)
        zero = jnp.zeros_like(lower0)
        used0 = jnp.where(row > 0, lower0, zero)
        used1 = jnp.where(row > 1, lower1, zero)
        fresh = minus_product(matrix.reshape(size, -1), used0, upper0)
        fresh = fresh - jnp.dot(used1, upper1, preferred_element_type=jnp.float32)
        fresh = fresh.astype(jnp.bfloat16).reshape(size, 2, size)
        head = fresh[:, 0]
        head = jnp.where((col == 0) & (row > 0), lower0, head)
        head = jnp.where((col == 1) & (row > 1), lower1, head)
        return jnp.stack([head, fresh[:, 1]], axis=1)[:, None]


def solution(mesh):
    return jax.shard_map(
        local,
        mesh=mesh,
        in_specs=(P("row", "col", None, None), P()),
        out_specs=P("row", "col", None, None),
        check_vma=False,
    )
```

time: 592 us -> 161 us (0.27); the launches traced: 583 us -> 161 us
  waiting for transfers between devices: 535 us -> 39 us
  starting transfers between devices: 0.31 us -> 52.6 us
  blocking collectives: 0 us -> 21.8 us
    psum x4 -> x0, waiting for transfers between devices: 535 us -> none  [spread(): return lax.psum(kept, axis)]
    ppermute x0 -> x11, starting transfers between devices: none -> 48.9 us  [the longest x3 19.4 us: spread_diagonal(): lax.ppermute(piece, 'col', [(0, quarter * k), (1, quarter * k + 1)])]
    all_to_all x0 -> x1, blocking collectives: none -> 21.8 us  [local(): lax.all_to_all(matrix, 'row', 0, 0, tiled=True, axis_index_groups=same_core)]
    all_gather x0 -> x1, waiting for transfers between devices: none -> 15.3 us  [local(): upper = lax.all_gather(dealt.reshape(part, -1), 'row', axis=0, tiled=False)]
    ppermute x0 -> x11, waiting for transfers between devices: none -> 15.1 us  [the longest x3 11.9 us: panel_tree(): got = lax.ppermute(held, 'col', pairs)]
    all_to_all x0 -> x1, waiting for transfers between devices: none -> 8.62 us  [local(): lax.all_to_all(copies, 'row', 0, 0, tiled=True, axis_index_groups=same_core)]
    dot_general x10 -> x11, matrix products: 18.5 us -> 19.1 us  [the longest x2 7.04 us: refined_inverse(): jnp.dot(approx, 2.0 * identity - product, precision=highest)]
  transfers between devices with their start and end apart: 4 -> 13, of which waited for: 4 -> 6; matrix products, arithmetic and copies ran while one was open for 0% -> 11% of each run, Pallas kernels for 0% -> 0%
where the time goes in v1:
time: 161 us
  starting transfers between devices  52.6 us (33%)
  waiting for transfers between devices  39 us (24%)
  blocking collectives  21.8 us (14%)
  matrix products  19.1 us (12%)
  between operations  13.8 us (9%)
  local copies, waits for them, and re-layouts  12.5 us (8%)
  other arithmetic  1.78 us (1%)
    all_to_all x1, blocking collectives, local(): lax.all_to_all(matrix, 'row', 0, 0, tiled=True, axis_index_groups=same_core)  21.8 us
    ppermute x3, starting transfers between devices, spread_diagonal(): lax.ppermute(piece, 'col', [(0, quarter * k), (1, quarter * k + 1)])  19.4 us
    ppermute x3, starting transfers between devices, panel_tree(): got = lax.ppermute(held, 'col', pairs)  15.3 us
    all_gather x1, waiting for transfers between devices, local(): upper = lax.all_gather(dealt.reshape(part, -1), 'row', axis=0, tiled=False)  15.3 us
    ppermute x3, waiting for transfers between devices, panel_tree(): got = lax.ppermute(held, 'col', pairs)  11.9 us
    all_to_all x1, waiting for transfers between devices, local(): lax.all_to_all(copies, 'row', 0, 0, tiled=True, axis_index_groups=same_core)  8.62 us
    dot_general x2, matrix products, refined_inverse(): jnp.dot(approx, 2.0 * identity - product, precision=highest)  7.04 us
    ppermute x1, starting transfers between devices, local(): other = lax.ppermute(mine, 'row', swap_core)  6.78 us
  transfers between devices with their start and end apart: 13, of which 6 were waited for; matrix products, arithmetic and copies ran while one was open for 11% of the time, Pallas kernels for 0%

profile of v1, /device:TPU:1, one launch (start us, length us, event | category | flops | bytes accessed | tf_op | source)
XLA Modules:
  0.0 160.7 jit_solution(6710002178835805584)
XLA Ops:
  6.5 21.8 %all_to_all.10 = bf16[512,1,2,512]{3,2,1,0:T(2,128)(2,1)S(1)} all-to-all(bf16[512,1,2,512]{3,2,1,0:T(2,128)(2,1)} %param.2), channel_id=1, replica_groups={{0,32,64,96,128,160,192,224,256,288,320,352,384,416,448,480},{16,48,80,..., dimensions={0} | all-to-all | bytes 2097152 | tf_op jit(solution)/shard_map/scatter_rows/all_to_all | solution.py:68
  28.4 14.5 %collective-permute-start.6 = (bf16[32,512]{1,0:T(8,128)(2,1)S(1)}, bf16[32,512]{1,0:T(8,128)(2,1)S(1)}, u32[]{:S(2)}, u32[]{:S(2)}) collective-permute-start(bf16[32,512]{1,0:T(8,128)(2,1)S(1)} %slice_bitcast_fusion), channel_id=1, source_target_pairs={{0,12},{1,13},{16,28},{17,29},{32,44},{33,45},{48,60},{49,61},{64,... | collective-permute-start | bytes 98312 | tf_op jit(solution)/shard_map/diagonal/ppermute | solution.py:41
  42.9 3.7 %collective-permute-start.5 = (bf16[32,512]{1,0:T(8,128)(2,1)S(1)}, bf16[32,512]{1,0:T(8,128)(2,1)S(1)}, u32[]{:S(2)}, u32[]{:S(2)}) collective-permute-start(bf16[32,512]{1,0:T(8,128)(2,1)S(1)} %slice_bitcast_fusion), channel_id=1, source_target_pairs={{0,8},{1,9},{16,24},{17,25},{32,40},{33,41},{48,56},{49,57},{64,72... | collective-permute-start | bytes 98312 | tf_op jit(solution)/shard_map/diagonal/ppermute | solution.py:41
  46.6 1.3 collective-permute-start.4
  47.9 1.0 collective-permute-done.4
  48.9 1.3 collective-permute-start.9
  50.2 1.3 collective-permute-start.8
  51.5 2.6 %collective-permute-start.7 = (bf16[32,512]{1,0:T(8,128)(2,1)S(1)}, bf16[32,512]{1,0:T(8,128)(2,1)S(1)}, u32[]{:S(2)}, u32[]{:S(2)}) collective-permute-start(bf16[32,512]{1,0:T(8,128)(2,1)S(1)} %add_select_fusion), channel_id=1, source_target_pairs={{0,1},{1,0},{4,5},{5,4},{8,9},{9,8},{12,13},{13,12},{16,17},{17,16... | collective-permute-start | bytes 98312 | tf_op jit(solution)/shard_map/diagonal/ppermute | solution.py:45
  54.2 0.1 copy.37
  54.3 11.9 %collective-permute-start = (bf16[512,512]{1,0:T(8,128)(2,1)S(1)}, bf16[512,512]{1,0:T(8,128)(2,1)}, u32[]{:S(2)}, u32[]{:S(2)}) collective-permute-start(bf16[512,512]{1,0:T(8,128)(2,1)S(1)} %bitcast.81), channel_id=1, source_target_pairs={{0,8},{1,9},{16,24},{17,25},{32,40},{33,41},{48,56},{49,57},{64,72... | collective-permute-start | bytes 1572872 | tf_op jit(solution)/shard_map/panels/ppermute | solution.py:27
  66.2 1.1 broadcast_in_dim.12
  67.3 3.7 %all-to-all-start.1 = ((bf16[16,2,32,512]{3,2,1,0:T(8,128)(2,1)}), bf16[16,2,32,512]{3,2,1,0:T(8,128)(2,1)S(1)}, u32[]{:S(2)}, u32[]{:S(2)}) async-start(bf16[16,2,32,512]{3,2,1,0:T(8,128)(2,1)} %broadcast_in_dim.12), calls=%async_computation.1 | async-start | bytes 2097152 | tf_op jit(solution)/shard_map/diagonal/all_to_all | solution.py:79
  71.1 2.1 %collective-permute-done = bf16[512,512]{1,0:T(8,128)(2,1)} collective-permute-done((bf16[512,512]{1,0:T(8,128)(2,1)S(1)}, bf16[512,512]{1,0:T(8,128)(2,1)}, u32[]{:S(2)}, u32[]{:S(2)}) %collective-permute-start) | collective-permute-done | bytes 524320 | tf_op jit(solution)/shard_map/panels/ppermute | solution.py:27
  73.2 0.1 broadcast_select_fusion.2
  73.2 2.1 %collective-permute-start.1 = (bf16[512,512]{1,0:T(8,128)(2,1)S(1)}, bf16[512,512]{1,0:T(8,128)(2,1)}, u32[]{:S(2)}, u32[]{:S(2)}) collective-permute-start(bf16[512,512]{1,0:T(8,128)(2,1)S(1)} %broadcast_select_fusion.2), channel_id=1, source_target_pairs={{0,12},{8,4},{1,5},{9,13},{16,28},{24,20},{17,21},{25,29},{32,44},... | collective-permute-start | bytes 1572872 | tf_op jit(solution)/shard_map/panels/ppermute | solution.py:27
  75.3 0.7 squeeze.43
  76.0 8.6 %all-to-all-done.1 = bf16[16,2,32,512]{3,2,1,0:T(8,128)(2,1)S(1)} async-done(((bf16[16,2,32,512]{3,2,1,0:T(8,128)(2,1)}), bf16[16,2,32,512]{3,2,1,0:T(8,128)(2,1)S(1)}, u32[]{:S(2)}, u32[]{:S(2)}) %all-to-all-start.1) | async-done | bytes 1048608 | tf_op jit(solution)/shard_map/diagonal/all_to_all | solution.py:79
  84.6 6.8 %collective-permute-start.10 = (bf16[16,2,32,512]{3,2,1,0:T(8,128)(2,1)S(1)}, bf16[16,2,32,512]{3,2,1,0:T(8,128)(2,1)}, u32[]{:S(2)}, u32[]{:S(2)}) collective-permute-start(bf16[16,2,32,512]{3,2,1,0:T(8,128)(2,1)S(1)} %all-to-all-done.1), channel_id=1, source_target_pairs={{0,16},{16,0},{32,48},{48,32},{64,80},{80,64},{96,112},{112,96},{1... | collective-permute-start | bytes 3145736 | tf_op jit(solution)/shard_map/diagonal/ppermute | solution.py:80
  91.4 0.1 broadcast_select_fusion.3
  91.5 1.3 collective-permute-start.2
  92.9 1.6 %copy.32 = f32[64,8,2,512]{3,1,2,0:T(8,128)} copy(bf16[64,8,2,512]{3,2,1,0:T(2,128)(2,1)S(1)} %bitcast.69) | data formatting | bytes 3145728
  94.5 9.8 %collective-permute-done.2 = bf16[512,512]{1,0:T(8,128)(2,1)S(1)} collective-permute-done((bf16[512,512]{1,0:T(8,128)(2,1)S(1)}, bf16[512,512]{1,0:T(8,128)(2,1)S(1)}, u32[]{:S(2)}, u32[]{:S(2)}) %collective-permute-start.2) | collective-permute-done | bytes 524320 | tf_op jit(solution)/shard_map/panels/ppermute | solution.py:27
  104.4 2.1 %collective-permute-start.3 = (bf16[512,512]{1,0:T(8,128)(2,1)S(1)}, bf16[512,512]{1,0:T(8,128)(2,1)S(1)}, u32[]{:S(2)}, u32[]{:S(2)}) collective-permute-start(bf16[512,512]{1,0:T(8,128)(2,1)S(1)} %broadcast_select_fusion.4), channel_id=1, source_target_pairs={{0,15},{1,2},{2,1},{3,4},{4,3},{5,6},{6,5},{7,8},{8,7},{9,10},{10,... | collective-permute-start | bytes 1572872 | tf_op jit(solution)/shard_map/panels/ppermute | solution.py:32
  106.5 1.4 broadcast_select_fusion
  107.9 0.2 fusion.30
  108.1 1.4 copy-done.1
  109.5 1.1 select_subtract_fusion.1
  110.6 3.6 %convolution_convert_fusion.4 = bf16[512,512]{1,0:T(8,128)(2,1)S(1)} fusion(f32[512,512]{1,0:T(8,128)S(1)} %select_subtract_fusion.1, f32[2,512,512]{2,1,0:T(8,128)S(1)} %copy-done.1), kind=kOutput, calls=%fused_computation.9 | convolution fusion | flops 1610874880 | bytes 2621440 | tf_op jit(solution)/shard_map/inverses/dot_general | solution.py:12
  114.1 0.5 convolution_convert_fusion
  114.6 2.2 %collective-permute-done.3 = bf16[512,512]{1,0:T(8,128)(2,1)S(1)} collective-permute-done((bf16[512,512]{1,0:T(8,128)(2,1)S(1)}, bf16[512,512]{1,0:T(8,128)(2,1)S(1)}, u32[]{:S(2)}, u32[]{:S(2)}) %collective-permute-start.3) | collective-permute-done | bytes 524320 | tf_op jit(solution)/shard_map/panels/ppermute | solution.py:32
  116.8 0.5 convolution_convert_fusion.1
  117.3 0.4 fusion.32
  117.7 0.4 fusion.33
  118.2 1.1 select_subtract_fusion
  119.2 3.5 %convolution_convert_fusion.3 = bf16[512,512]{1,0:T(8,128)(2,1)S(1)} fusion(f32[512,512]{1,0:T(8,128)S(1)} %select_subtract_fusion, f32[2,512,512]{2,1,0:T(8,128)S(1)} %copy-done.1), kind=kOutput, calls=%fused_computation.8 | convolution fusion | flops 1610874880 | bytes 2621440 | tf_op jit(solution)/shard_map/inverses/dot_general | solution.py:12
  122.7 1.0 convolution_convert_fusion.2
  123.8 15.3 %all-gather.2.cloned.1.call-done = bf16[32,32,1024]{2,1,0:T(8,128)(2,1)} async-done(((bf16[1,32,1024]{2,1,0:T(8,128)(2,1)}), bf16[32,32,1024]{2,1,0:T(8,128)(2,1)}) %all-gather.2.cloned.1.call-update) | async-done | bytes 2097168 | tf_op jit(solution)/shard_map/gather_rows/all_gather | solution.py:72
  139.1 2.8 %fusion.28 = (bf16[16,1,32,1024]{3,2,1,0:T(8,128)(2,1)}, bf16[16,1,32,1024]{3,2,1,0:T(8,128)(2,1)S(1)}) fusion(bf16[16,2,32,1024]{3,2,1,0:T(8,128)(2,1)} %bitcast.76), kind=kLoop, calls=%fused_computation.52 | loop fusion | bytes 4194304 | tf_op jit(solution)/shard_map/gather_rows/slice | solution.py:75
  141.8 2.1 %fusion.16 = f32[512,1024]{1,0:T(8,128)} fusion(bf16[512,1024]{1,0:T(8,128)(2,1)S(1)} %bitcast.73, bf16[512,512]{1,0:T(8,128)(2,1)S(1)} %convolution_convert_fusion.1, pred[]{:T(512)S(6)} %gt.9), kind=kOutput, calls=%fused_computation.31 | convolution fusion | flops 537133056 | bytes 3670017 | tf_op jit(solution)/shard_map/update/dot_general | solution.py:16
  143.9 5.1 %subtract_convert_fusion = bf16[512,1024]{1,0:T(8,128)(2,1)} fusion(f32[512,1024]{1,0:T(8,128)} %bitcast.75, f32[512,1024]{1,0:T(8,128)} %fusion.16, bf16[512,1024]{1,0:T(8,128)(2,1)} %bitcast.80, bf16[512,512]{1,0:T(8,128)(2,1)S(1)} %convolution_convert_fusion, bf16[512,1024]{1,0:T(8,128)(2,1)S(1)} %bitcast.74, ...), kind=kOutput, calls=%fused_computation.2 | convolution fusion | flops 1077149696 | bytes 8388609 | tf_op jit(solution)/shard_map/update/dot_general | solution.py:100
  149.0 1.5 copy.22
  150.5 0.1 fusion.29
  150.5 0.2 copy.29
  150.8 0.2 copy.30
  151.0 0.6 copy-done.3
  151.6 0.1 fusion.14
  151.7 0.1 maximum_bitcast_fusion
  151.8 2.0 %copy.25 = bf16[512,1,2,512]{3,2,1,0:T(2,128)(2,1)} copy(bf16[512,1,2,512]{3,0,2,1:T(8,128)(2,1)S(1)} %maximum_bitcast_fusion) | data formatting | bytes 2097152 | tf_op jit(solution)/shard_map/update/broadcast_in_dim | solution.py:105
  (22 shorter events, 0.2 us)
Async XLA Ops:
  6.5 47.6 %copy-start = (bf16[512,1,2,512]{3,2,1,0:T(2,128)(2,1)S(1)}, bf16[512,1,2,512]{3,2,1,0:T(2,128)(2,1)}, u32[]{:S(2)}) copy-start(bf16[512,1,2,512]{3,2,1,0:T(2,128)(2,1)} %param.2) | copy-start | bytes 3145732
  28.4 19.5 %collective-permute-start.6 = (bf16[32,512]{1,0:T(8,128)(2,1)S(1)}, bf16[32,512]{1,0:T(8,128)(2,1)S(1)}, u32[]{:S(2)}, u32[]{:S(2)}) collective-permute-start(bf16[32,512]{1,0:T(8,128)(2,1)S(1)} %slice_bitcast_fusion), channel_id=1, source_target_pairs={{0,12},{1,13},{16,28},{17,29},{32,44},{33,45},{48,60},{49,61},{64,... | collective-permute-start | bytes 98312 | tf_op jit(solution)/shard_map/diagonal/ppermute | solution.py:41
  42.9 5.0 %collective-permute-start.5 = (bf16[32,512]{1,0:T(8,128)(2,1)S(1)}, bf16[32,512]{1,0:T(8,128)(2,1)S(1)}, u32[]{:S(2)}, u32[]{:S(2)}) collective-permute-start(bf16[32,512]{1,0:T(8,128)(2,1)S(1)} %slice_bitcast_fusion), channel_id=1, source_target_pairs={{0,8},{1,9},{16,24},{17,25},{32,40},{33,41},{48,56},{49,57},{64,72... | collective-permute-start | bytes 98312 | tf_op jit(solution)/shard_map/diagonal/ppermute | solution.py:41
  46.6 2.3 %collective-permute-start.4 = (bf16[32,512]{1,0:T(8,128)(2,1)S(1)}, bf16[32,512]{1,0:T(8,128)(2,1)S(1)}, u32[]{:S(2)}, u32[]{:S(2)}) collective-permute-start(bf16[32,512]{1,0:T(8,128)(2,1)S(1)} %slice_bitcast_fusion), channel_id=1, source_target_pairs={{0,4},{1,5},{16,20},{17,21},{32,36},{33,37},{48,52},{49,53},{64,68... | collective-permute-start | bytes 98312 | tf_op jit(solution)/shard_map/diagonal/ppermute | solution.py:41
  48.9 17.3 %collective-permute-start.9 = (bf16[32,512]{1,0:T(8,128)(2,1)S(1)}, bf16[32,512]{1,0:T(8,128)(2,1)S(1)}, u32[]{:S(2)}, u32[]{:S(2)}) collective-permute-start(bf16[32,512]{1,0:T(8,128)(2,1)S(1)} %add_select_fusion), channel_id=1, source_target_pairs={{0,3},{1,2},{4,7},{5,6},{8,11},{9,10},{12,15},{13,14},{16,19},{17,... | collective-permute-start | bytes 98312 | tf_op jit(solution)/shard_map/diagonal/ppermute | solution.py:47
  50.2 16.0 %collective-permute-start.8 = (bf16[32,512]{1,0:T(8,128)(2,1)S(1)}, bf16[32,512]{1,0:T(8,128)(2,1)S(1)}, u32[]{:S(2)}, u32[]{:S(2)}) collective-permute-start(bf16[32,512]{1,0:T(8,128)(2,1)S(1)} %add_select_fusion), channel_id=1, source_target_pairs={{0,2},{1,3},{4,6},{5,7},{8,10},{9,11},{12,14},{13,15},{16,18},{17,... | collective-permute-start | bytes 98312 | tf_op jit(solution)/shard_map/diagonal/ppermute | solution.py:46
  51.5 14.7 %collective-permute-start.7 = (bf16[32,512]{1,0:T(8,128)(2,1)S(1)}, bf16[32,512]{1,0:T(8,128)(2,1)S(1)}, u32[]{:S(2)}, u32[]{:S(2)}) collective-permute-start(bf16[32,512]{1,0:T(8,128)(2,1)S(1)} %add_select_fusion), channel_id=1, source_target_pairs={{0,1},{1,0},{4,5},{5,4},{8,9},{9,8},{12,13},{13,12},{16,17},{17,16... | collective-permute-start | bytes 98312 | tf_op jit(solution)/shard_map/diagonal/ppermute | solution.py:45
  54.3 18.9 %collective-permute-start = (bf16[512,512]{1,0:T(8,128)(2,1)S(1)}, bf16[512,512]{1,0:T(8,128)(2,1)}, u32[]{:S(2)}, u32[]{:S(2)}) collective-permute-start(bf16[512,512]{1,0:T(8,128)(2,1)S(1)} %bitcast.81), channel_id=1, source_target_pairs={{0,8},{1,9},{16,24},{17,25},{32,40},{33,41},{48,56},{49,57},{64,72... | collective-permute-start | bytes 1572872 | tf_op jit(solution)/shard_map/panels/ppermute | solution.py:27
  67.3 17.3 %all-to-all-start.1 = ((bf16[16,2,32,512]{3,2,1,0:T(8,128)(2,1)}), bf16[16,2,32,512]{3,2,1,0:T(8,128)(2,1)S(1)}, u32[]{:S(2)}, u32[]{:S(2)}) async-start(bf16[16,2,32,512]{3,2,1,0:T(8,128)(2,1)} %broadcast_in_dim.12), calls=%async_computation.1 | async-start | bytes 2097152 | tf_op jit(solution)/shard_map/diagonal/all_to_all | solution.py:79
  71.0 68.1 %all-gather.2.cloned.1.call-start = ((), (), s32[]{:S(2)}) async-start(), calls=%async_computation.2 | async-start | bytes 2162688 | tf_op jit(solution)/shard_map/gather_rows/all_gather | solution.py:72
  73.2 18.2 %collective-permute-start.1 = (bf16[512,512]{1,0:T(8,128)(2,1)S(1)}, bf16[512,512]{1,0:T(8,128)(2,1)}, u32[]{:S(2)}, u32[]{:S(2)}) collective-permute-start(bf16[512,512]{1,0:T(8,128)(2,1)S(1)} %broadcast_select_fusion.2), channel_id=1, source_target_pairs={{0,12},{8,4},{1,5},{9,13},{16,28},{24,20},{17,21},{25,29},{32,44},... | collective-permute-start | bytes 1572872 | tf_op jit(solution)/shard_map/panels/ppermute | solution.py:27
  84.6 21.9 %collective-permute-start.10 = (bf16[16,2,32,512]{3,2,1,0:T(8,128)(2,1)S(1)}, bf16[16,2,32,512]{3,2,1,0:T(8,128)(2,1)}, u32[]{:S(2)}, u32[]{:S(2)}) collective-permute-start(bf16[16,2,32,512]{3,2,1,0:T(8,128)(2,1)S(1)} %all-to-all-done.1), channel_id=1, source_target_pairs={{0,16},{16,0},{32,48},{48,32},{64,80},{80,64},{96,112},{112,96},{1... | collective-permute-start | bytes 3145736 | tf_op jit(solution)/shard_map/diagonal/ppermute | solution.py:80
  91.5 12.8 %collective-permute-start.2 = (bf16[512,512]{1,0:T(8,128)(2,1)S(1)}, bf16[512,512]{1,0:T(8,128)(2,1)S(1)}, u32[]{:S(2)}, u32[]{:S(2)}) collective-permute-start(bf16[512,512]{1,0:T(8,128)(2,1)S(1)} %broadcast_select_fusion.3), channel_id=1, source_target_pairs={{0,14},{4,2},{8,6},{12,10},{1,3},{5,7},{9,11},{13,15},{16,30},{20,... | collective-permute-start | bytes 1572872 | tf_op jit(solution)/shard_map/panels/ppermute | solution.py:27
  104.4 12.4 %collective-permute-start.3 = (bf16[512,512]{1,0:T(8,128)(2,1)S(1)}, bf16[512,512]{1,0:T(8,128)(2,1)S(1)}, u32[]{:S(2)}, u32[]{:S(2)}) collective-permute-start(bf16[512,512]{1,0:T(8,128)(2,1)S(1)} %broadcast_select_fusion.4), channel_id=1, source_target_pairs={{0,15},{1,2},{2,1},{3,4},{4,3},{5,6},{6,5},{7,8},{8,7},{9,10},{10,... | collective-permute-start | bytes 1572872 | tf_op jit(solution)/shard_map/panels/ppermute | solution.py:32
  107.9 1.6 copy-start.1
  123.8 20.1 %copy-start.2 = (bf16[512,512]{1,0:T(8,128)(2,1)}, bf16[512,512]{1,0:T(8,128)(2,1)S(1)}, u32[]{:S(2)}) copy-start(bf16[512,512]{1,0:T(8,128)(2,1)S(1)} %convolution_convert_fusion.2) | copy-start | bytes 1572868
  150.5 1.0 copy-start.3
Sparse Core Ops, SparseCore 0:
  76.1 62.8 all-gather.1

commit v2 on v1

--- a/solution.py
+++ b/solution.py
@@ -16,21 +16,19 @@
     return base.astype(jnp.float32) - jnp.dot(left, right, preferred_element_type=jnp.float32)
 
 
-def panel_tree(panel, cols):
-    held = panel
+def panel_step(held, reach, cols):
     col = lax.axis_index("col")
-    reach = cols // 2
-    while reach >= 2:
-        step = 2 * reach
-        pairs = [(s, (s - reach) % cols) for s in range(0, cols, step)]
-        pairs += [(s + 1, (s + 1 + reach) % cols) for s in range(0, cols, step)]
-        got = lax.ppermute(held, "col", pairs)
-        holds = ((col - col % 2) % step) == 0
-        held = jnp.where(holds, held, got)
-        reach //= 2
+    step = 2 * reach
+    pairs = [(s, (s - reach) % cols) for s in range(0, cols, step)]
+    pairs += [(s + 1, (s + 1 + reach) % cols) for s in range(0, cols, step)]
+    got = lax.ppermute(held, "col", pairs)
+    return jnp.where((col - col % 2) % step == 0, held, got)
+
+
+def panel_pair(held, cols):
+    even = lax.axis_index("col") % 2 == 0
     pairs = [(s, (s - 1) % cols) if s % 2 == 0 else (s, (s + 1) % cols) for s in range(cols)]
     other = lax.ppermute(held, "col", pairs)
-    even = col % 2 == 0
     return jnp.where(even, held, other), jnp.where(even, other, held)
 
 
@@ -61,27 +59,41 @@
     swap_core = [(r, r ^ 1) for r in range(rows)]
     core = row % 2
 
+    def gather_part(piece):
+        copies = jnp.broadcast_to(piece[None], (chips,) + piece.shape)
+        return lax.all_to_all(copies, "row", 0, 0, tiled=True, axis_index_groups=same_core)
+
     with jax.named_scope("panels"):
-        panel0, panel1 = panel_tree(matrix[:, 0, 0, :], cols)
-
+        held = panel_step(matrix[:, 0, 0, :], 8, cols)
     with jax.named_scope("scatter_rows"):
         dealt = lax.all_to_all(
             matrix, "row", 0, 0, tiled=True, axis_index_groups=same_core
         )[:part, 0]
-    with jax.named_scope("gather_rows"):
-        upper = lax.all_gather(dealt.reshape(part, -1), "row", axis=0, tiled=False)
-        upper = upper.reshape(chips, 2, part, -1)
-        upper0 = upper[:, 0].reshape(size, -1)
-        raw1 = upper[:, 1].reshape(size, -1)
+    dealt, held = lax.optimization_barrier((dealt, held))
+    with jax.named_scope("panels"):
+        held = panel_step(held, 4, cols)
     with jax.named_scope("diagonal"):
         pieces = spread_diagonal(dealt[:, 0, :], cols)
-        copies = jnp.broadcast_to(pieces[None], (chips,) + pieces.shape)
-        mine = lax.all_to_all(copies, "row", 0, 0, tiled=True, axis_index_groups=same_core)
+        pieces, held = lax.optimization_barrier((pieces, held))
+    with jax.named_scope("panels"):
+        held = panel_step(held, 2, cols)
+    with jax.named_scope("diagonal"):
+        mine = gather_part(pieces)
+        mine, held = lax.optimization_barrier((mine, held))
+    with jax.named_scope("panels"):
+        panel0, panel1 = panel_pair(held, cols)
+    with jax.named_scope("diagonal"):
         other = lax.ppermute(mine, "row", swap_core)
         top = jnp.where(core == 0, mine, other)
         low = jnp.where(core == 0, other, mine)
         d00, d01 = (top[:, k].reshape(size, size) for k in range(2))
         d10, d11 = (low[:, k].reshape(size, size) for k in range(2))
+    with jax.named_scope("gather_rows"):
+        own_rows = gather_part(dealt.reshape(part, -1)).reshape(size, -1)
+        own_rows, panel0, panel1 = lax.optimization_barrier((own_rows, panel0, panel1))
+        other_rows = lax.ppermute(own_rows, "row", swap_core)
+        upper0 = jnp.where(core == 0, own_rows, other_rows)
+        raw1 = jnp.where(core == 0, other_rows, own_rows)
     with jax.named_scope("inverses"):
         inverse0 = refined_inverse(d00, inverses[0])
         lower10 = jnp.dot(d10, inverse0, preferred_element_type=jnp.float32).astype(jnp.bfloat16)

time: 161 us -> 148 us (0.919)
  the two profiles are of different devices: /device:TPU:1 before, /device:TPU:99 now
where the time goes in v2:
time: 148 us; the launch traced here: 147 us
  waiting for transfers between devices  72.8 us (49%)
  starting transfers between devices  39.1 us (26%)
  matrix products  18.8 us (13%)
  local copies, waits for them, and re-layouts  11.1 us (8%)
  other arithmetic  4.84 us (3%)
    ppermute x1, waiting for transfers between devices, spread_diagonal(): lax.ppermute(held, 'col', [p for g in groups for p in ((g, g + 3), (g + 1...  22.7 us
    all_to_all x1, waiting for transfers between devices, local(): lax.all_to_all(matrix, 'row', 0, 0, tiled=True, axis_index_groups=same_core)  13.9 us
    all_to_all x2, starting transfers between devices, gather_part(): lax.all_to_all(copies, 'row', 0, 0, tiled=True, axis_index_groups=same_core)  13.3 us
    ppermute x1, waiting for transfers between devices, panel_pair(): other = lax.ppermute(held, 'col', pairs)  12.7 us
    ppermute x3, waiting for transfers between devices, panel_step(): got = lax.ppermute(held, 'col', pairs)  12.3 us
    ppermute x1, waiting for transfers between devices, spread_diagonal(): lax.ppermute(held, 'col', [p for g in groups for p in ((g, g + 2), (g + 1...  11.2 us
    all_to_all x1, starting transfers between devices, local(): lax.all_to_all(matrix, 'row', 0, 0, tiled=True, axis_index_groups=same_core)  7.05 us
    dot_general x2, matrix products, refined_inverse(): jnp.dot(approx, 2.0 * identity - product, precision=highest)  6.98 us
  transfers between devices with their start and end apart: 15, of which 5 were waited for; matrix products, arithmetic and copies ran while one was open for 14% of the time, Pallas kernels for 0%

profile of v2, /device:TPU:99, one launch (start us, length us, event | category | flops | bytes accessed | tf_op | source)
XLA Modules:
  0.0 147.3 jit_solution(8902344530562416301)
XLA Ops:
  0.0 7.0 %all-to-all-start = ((bf16[512,1,2,512]{3,2,1,0:T(2,128)(2,1)}), bf16[512,1,2,512]{3,2,1,0:T(2,128)(2,1)S(1)}, u32[]{:S(2)}, u32[]{:S(2)}) async-start(bf16[512,1,2,512]{3,2,1,0:T(2,128)(2,1)} %param.2), calls=%async_computation | async-start | bytes 2097152 | tf_op jit(solution)/shard_map/scatter_rows/all_to_all | solution.py:69
  7.1 0.1 copy.34
  7.2 0.7 collective-permute-start
  8.0 13.9 %all-to-all-done = bf16[512,1,2,512]{3,2,1,0:T(2,128)(2,1)S(1)} async-done(((bf16[512,1,2,512]{3,2,1,0:T(2,128)(2,1)}), bf16[512,1,2,512]{3,2,1,0:T(2,128)(2,1)S(1)}, u32[]{:S(2)}, u32[]{:S(2)}) %all-to-all-start) | async-done | bytes 1048608 | tf_op jit(solution)/shard_map/scatter_rows/all_to_all | solution.py:69
  22.0 0.7 collective-permute-start.3
  22.7 0.7 collective-permute-start.2
  23.4 0.7 collective-permute-start.1
  24.1 0.7 collective-permute-start.7
  24.8 1.3 collective-permute-start.6
  26.1 1.3 collective-permute-start.5
  27.4 0.7 collective-permute-start.4
  28.1 22.7 %collective-permute-done.6 = bf16[32,512]{1,0:T(8,128)(2,1)S(1)} collective-permute-done((bf16[32,512]{1,0:T(8,128)(2,1)S(1)}, bf16[32,512]{1,0:T(8,128)(2,1)S(1)}, u32[]{:S(2)}, u32[]{:S(2)}) %collective-permute-start.6) | collective-permute-done | bytes 32800 | tf_op jit(solution)/shard_map/diagonal/ppermute | solution.py:45
  50.9 11.2 %collective-permute-done.5 = bf16[32,512]{1,0:T(8,128)(2,1)S(1)} collective-permute-done((bf16[32,512]{1,0:T(8,128)(2,1)S(1)}, bf16[32,512]{1,0:T(8,128)(2,1)S(1)}, u32[]{:S(2)}, u32[]{:S(2)}) %collective-permute-start.5) | collective-permute-done | bytes 32800 | tf_op jit(solution)/shard_map/diagonal/ppermute | solution.py:44
  62.1 1.1 broadcast_in_dim.21
  63.2 6.6 %all-to-all-start.2 = ((bf16[16,2,32,512]{3,2,1,0:T(8,128)(2,1)}), bf16[16,2,32,512]{3,2,1,0:T(8,128)(2,1)S(1)}, u32[]{:S(2)}, u32[]{:S(2)}) async-start(bf16[16,2,32,512]{3,2,1,0:T(8,128)(2,1)} %broadcast_in_dim.21), calls=%async_computation.2 | async-start | bytes 2097152 | tf_op jit(solution)/shard_map/diagonal/all_to_all | solution.py:64
  69.9 1.3 collective-permute-start.8
  71.2 12.3 %collective-permute-done.8 = bf16[512,512]{1,0:T(8,128)(2,1)S(1)} collective-permute-done((bf16[512,512]{1,0:T(8,128)(2,1)S(1)}, bf16[512,512]{1,0:T(8,128)(2,1)S(1)}, u32[]{:S(2)}, u32[]{:S(2)}) %collective-permute-start.8) | collective-permute-done | bytes 524320 | tf_op jit(solution)/shard_map/panels/ppermute | solution.py:24
  83.4 0.9 broadcast_select_fusion.3
  84.3 5.5 %collective-permute-start.10 = (bf16[16,2,32,512]{3,2,1,0:T(8,128)(2,1)S(1)}, bf16[16,2,32,512]{3,2,1,0:T(8,128)(2,1)}, u32[]{:S(2)}, u32[]{:S(2)}) collective-permute-start(bf16[16,2,32,512]{3,2,1,0:T(8,128)(2,1)S(1)} %all-to-all-done.2), channel_id=1, source_target_pairs={{0,16},{16,0},{32,48},{48,32},{64,80},{80,64},{96,112},{112,96},{1... | collective-permute-start | bytes 3145736 | tf_op jit(solution)/shard_map/diagonal/ppermute | solution.py:86
  89.8 1.1 broadcast_in_dim.20
  90.9 6.7 %all-to-all-start.1 = ((bf16[16,32,1024]{2,1,0:T(8,128)(2,1)}), bf16[16,32,1024]{2,1,0:T(8,128)(2,1)S(1)}, u32[]{:S(2)}, u32[]{:S(2)}) async-start(bf16[16,32,1024]{2,1,0:T(8,128)(2,1)} %broadcast_in_dim.20), calls=%async_computation.1 | async-start | bytes 2097152 | tf_op jit(solution)/shard_map/gather_rows/all_to_all | solution.py:64
  97.5 1.9 %collective-permute-start.9 = (bf16[512,512]{1,0:T(8,128)(2,1)}, bf16[512,512]{1,0:T(8,128)(2,1)}, u32[]{:S(2)}, u32[]{:S(2)}) collective-permute-start(bf16[512,512]{1,0:T(8,128)(2,1)} %broadcast_select_fusion.3), channel_id=1, source_target_pairs={{0,15},{1,2},{2,1},{3,4},{4,3},{5,6},{6,5},{7,8},{8,7},{9,10},{10,... | collective-permute-start | bytes 1572872 | tf_op jit(solution)/shard_map/panels/ppermute | solution.py:31
  99.5 1.7 %copy.29 = f32[64,8,2,512]{3,1,2,0:T(8,128)} copy(bf16[64,8,2,512]{3,2,1,0:T(2,128)(2,1)S(1)} %bitcast.65) | data formatting | bytes 3145728
  101.2 12.7 %collective-permute-done.9 = bf16[512,512]{1,0:T(8,128)(2,1)} collective-permute-done((bf16[512,512]{1,0:T(8,128)(2,1)}, bf16[512,512]{1,0:T(8,128)(2,1)}, u32[]{:S(2)}, u32[]{:S(2)}) %collective-permute-start.9) | collective-permute-done | bytes 524320 | tf_op jit(solution)/shard_map/panels/ppermute | solution.py:31
  113.9 2.2 %broadcast_select_fusion.5 = (bf16[512,512]{1,0:T(8,128)(2,1)}, bf16[512,512]{1,0:T(8,128)(2,1)}) fusion(bf16[512,512]{1,0:T(8,128)(2,1)} %collective-permute-done.9, bf16[512,512]{1,0:T(8,128)(2,1)} %broadcast_select_fusion.3, pred[]{:T(512)S(6)} %eq.54), kind=kLoop, calls=%fused_computation.40 | loop fusion | flops 524288 | bytes 2097153 | tf_op jit(solution)/shard_map/panels/jit(_where)/select_n | solution.py:32
  116.1 3.5 %collective-permute-start.11 = (bf16[512,1024]{1,0:T(8,128)(2,1)S(1)}, bf16[512,1024]{1,0:T(8,128)(2,1)S(1)}, u32[]{:S(2)}, u32[]{:S(2)}) collective-permute-start(bf16[512,1024]{1,0:T(8,128)(2,1)S(1)} %bitcast.68), channel_id=1, source_target_pairs={{0,16},{16,0},{32,48},{48,32},{64,80},{80,64},{96,112},{112,96},{1... | collective-permute-start | bytes 3145736 | tf_op jit(solution)/shard_map/gather_rows/ppermute | solution.py:94
  119.6 1.4 broadcast_select_fusion.1
  121.0 0.2 fusion.28
  121.2 1.4 copy-done.1
  122.6 1.1 select_subtract_fusion.1
  123.7 3.5 %convolution_convert_fusion.4 = bf16[512,512]{1,0:T(8,128)(2,1)S(1)} fusion(f32[512,512]{1,0:T(8,128)S(1)} %select_subtract_fusion.1, f32[2,512,512]{2,1,0:T(8,128)S(1)} %copy-done.1), kind=kOutput, calls=%fused_computation.8 | convolution fusion | flops 1610874880 | bytes 2621440 | tf_op jit(solution)/shard_map/inverses/dot_general | solution.py:12
  127.2 0.5 convolution_convert_fusion.1
  127.7 0.5 convolution_convert_fusion
  128.2 0.8 copy-done.7
  129.0 0.4 fusion.31
  129.4 0.4 fusion.30
  129.8 1.1 select_subtract_fusion
  130.9 3.5 %convolution_convert_fusion.3 = bf16[512,512]{1,0:T(8,128)(2,1)S(1)} fusion(f32[512,512]{1,0:T(8,128)S(1)} %select_subtract_fusion, f32[2,512,512]{2,1,0:T(8,128)S(1)} %copy-done.1), kind=kOutput, calls=%fused_computation.7 | convolution fusion | flops 1610874880 | bytes 2621440 | tf_op jit(solution)/shard_map/inverses/dot_general | solution.py:12
  134.5 1.9 %convolution_convert_fusion.2 = bf16[512,512]{1,0:T(8,128)(2,1)} fusion(bf16[512,512]{1,0:T(8,128)(2,1)S(1)} %convolution_convert_fusion.3, f32[512,512]{1,0:T(8,128)S(1)} %fusion.30, bf16[512,512]{1,0:T(8,128)(2,1)S(1)} %copy-done.4), kind=kOutput, calls=%fused_computation.6 | convolution fusion | flops 1611399168 | bytes 2621440 | tf_op jit(solution)/shard_map/update/dot_general | solution.py:105
  136.3 0.7 fusion.18
  137.1 0.3 copy-done.8
  137.3 0.4 copy-done.6
  137.7 5.3 %subtract_convert_fusion = bf16[512,1024]{1,0:T(8,128)(2,1)} fusion(f32[512,1024]{1,0:T(8,128)} %bitcast.72, f32[512,1024]{1,0:T(8,128)S(1)} %fusion.18, bf16[512,1024]{1,0:T(8,128)(2,1)} %copy-done.8, bf16[512,1024]{1,0:T(8,128)(2,1)} %bitcast.69, pred[]{:T(512)S(6)} %eq.61, bf16[512,512]{1,0:T(8,128)(2,1)S(1)} %copy-done.6, pred[]{:T(512)S(6)} %gt.8, ...), kind=kOutput, calls=%fused_computation | convolution fusion | flops 1078198272 | bytes 8388610 | tf_op jit(solution)/shard_map/update/dot_general | solution.py:112
  143.0 1.5 %copy.20 = bf16[512,1024]{0,1:T(8,128)(2,1)S(1)} copy(bf16[512,1024]{1,0:T(8,128)(2,1)} %subtract_convert_fusion) | data formatting | bytes 2097152 | tf_op jit(solution)/shard_map/update/convert_element_type | solution.py:113
  144.6 0.2 copy.26
  144.8 0.2 copy.27
  145.1 0.1 maximum_bitcast_fusion
  145.2 2.0 %copy.23 = bf16[512,1,2,512]{3,2,1,0:T(2,128)(2,1)} copy(bf16[512,1,2,512]{3,0,2,1:T(8,128)(2,1)S(1)} %maximum_bitcast_fusion) | data formatting | bytes 2097152 | tf_op jit(solution)/shard_map/update/broadcast_in_dim | solution.py:117
  (35 shorter events, 0.4 us)
Async XLA Ops:
  0.0 7.1 %copy-start = (bf16[512,1,2,512]{3,2,1,0:T(2,128)(2,1)S(1)}, bf16[512,1,2,512]{3,2,1,0:T(2,128)(2,1)}, u32[]{:S(2)}) copy-start(bf16[512,1,2,512]{3,2,1,0:T(2,128)(2,1)} %param.2) | copy-start | bytes 3145732
  0.0 22.0 %all-to-all-start = ((bf16[512,1,2,512]{3,2,1,0:T(2,128)(2,1)}), bf16[512,1,2,512]{3,2,1,0:T(2,128)(2,1)S(1)}, u32[]{:S(2)}, u32[]{:S(2)}) async-start(bf16[512,1,2,512]{3,2,1,0:T(2,128)(2,1)} %param.2), calls=%async_computation | async-start | bytes 2097152 | tf_op jit(solution)/shard_map/scatter_rows/all_to_all | solution.py:69
  7.2 0.7 collective-permute-start
  22.0 2.7 %collective-permute-start.3 = (bf16[32,512]{1,0:T(8,128)(2,1)S(1)}, bf16[32,512]{1,0:T(8,128)(2,1)S(1)}, u32[]{:S(2)}, u32[]{:S(2)}) collective-permute-start(bf16[32,512]{1,0:T(8,128)(2,1)S(1)} %slice_bitcast_fusion), channel_id=1, source_target_pairs={{0,12},{1,13},{16,28},{17,29},{32,44},{33,45},{48,60},{49,61},{64,... | collective-permute-start | bytes 98312 | tf_op jit(solution)/shard_map/diagonal/ppermute | solution.py:39
  22.7 2.1 %collective-permute-start.2 = (bf16[32,512]{1,0:T(8,128)(2,1)S(1)}, bf16[32,512]{1,0:T(8,128)(2,1)S(1)}, u32[]{:S(2)}, u32[]{:S(2)}) collective-permute-start(bf16[32,512]{1,0:T(8,128)(2,1)S(1)} %slice_bitcast_fusion), channel_id=1, source_target_pairs={{0,8},{1,9},{16,24},{17,25},{32,40},{33,41},{48,56},{49,57},{64,72... | collective-permute-start | bytes 98312 | tf_op jit(solution)/shard_map/diagonal/ppermute | solution.py:39
  23.4 1.4 collective-permute-start.1
  24.1 38.0 %collective-permute-start.7 = (bf16[512,512]{1,0:T(8,128)(2,1)S(1)}, bf16[512,512]{1,0:T(8,128)(2,1)S(1)}, u32[]{:S(2)}, u32[]{:S(2)}) collective-permute-start(bf16[512,512]{1,0:T(8,128)(2,1)S(1)} %broadcast_select_fusion.7), channel_id=1, source_target_pairs={{0,12},{8,4},{1,5},{9,13},{16,28},{24,20},{17,21},{25,29},{32,44},... | collective-permute-start | bytes 1572872 | tf_op jit(solution)/shard_map/panels/ppermute | solution.py:24
  24.8 26.0 %collective-permute-start.6 = (bf16[32,512]{1,0:T(8,128)(2,1)S(1)}, bf16[32,512]{1,0:T(8,128)(2,1)S(1)}, u32[]{:S(2)}, u32[]{:S(2)}) collective-permute-start(bf16[32,512]{1,0:T(8,128)(2,1)S(1)} %add_select_fusion), channel_id=1, source_target_pairs={{0,3},{1,2},{4,7},{5,6},{8,11},{9,10},{12,15},{13,14},{16,19},{17,... | collective-permute-start | bytes 98312 | tf_op jit(solution)/shard_map/diagonal/ppermute | solution.py:45
  26.1 35.9 %collective-permute-start.5 = (bf16[32,512]{1,0:T(8,128)(2,1)S(1)}, bf16[32,512]{1,0:T(8,128)(2,1)S(1)}, u32[]{:S(2)}, u32[]{:S(2)}) collective-permute-start(bf16[32,512]{1,0:T(8,128)(2,1)S(1)} %add_select_fusion), channel_id=1, source_target_pairs={{0,2},{1,3},{4,6},{5,7},{8,10},{9,11},{12,14},{13,15},{16,18},{17,... | collective-permute-start | bytes 98312 | tf_op jit(solution)/shard_map/diagonal/ppermute | solution.py:44
  27.4 34.6 %collective-permute-start.4 = (bf16[32,512]{1,0:T(8,128)(2,1)S(1)}, bf16[32,512]{1,0:T(8,128)(2,1)S(1)}, u32[]{:S(2)}, u32[]{:S(2)}) collective-permute-start(bf16[32,512]{1,0:T(8,128)(2,1)S(1)} %add_select_fusion), channel_id=1, source_target_pairs={{0,1},{1,0},{4,5},{5,4},{8,9},{9,8},{12,13},{13,12},{16,17},{17,16... | collective-permute-start | bytes 98312 | tf_op jit(solution)/shard_map/diagonal/ppermute | solution.py:43
  63.2 21.1 %all-to-all-start.2 = ((bf16[16,2,32,512]{3,2,1,0:T(8,128)(2,1)}), bf16[16,2,32,512]{3,2,1,0:T(8,128)(2,1)S(1)}, u32[]{:S(2)}, u32[]{:S(2)}) async-start(bf16[16,2,32,512]{3,2,1,0:T(8,128)(2,1)} %broadcast_in_dim.21), calls=%async_computation.2 | async-start | bytes 2097152 | tf_op jit(solution)/shard_map/diagonal/all_to_all | solution.py:64
  69.9 13.6 %collective-permute-start.8 = (bf16[512,512]{1,0:T(8,128)(2,1)S(1)}, bf16[512,512]{1,0:T(8,128)(2,1)S(1)}, u32[]{:S(2)}, u32[]{:S(2)}) collective-permute-start(bf16[512,512]{1,0:T(8,128)(2,1)S(1)} %broadcast_select_fusion.4), channel_id=1, source_target_pairs={{0,14},{4,2},{8,6},{12,10},{1,3},{5,7},{9,11},{13,15},{16,30},{20,... | collective-permute-start | bytes 1572872 | tf_op jit(solution)/shard_map/panels/ppermute | solution.py:24
  84.3 35.3 %collective-permute-start.10 = (bf16[16,2,32,512]{3,2,1,0:T(8,128)(2,1)S(1)}, bf16[16,2,32,512]{3,2,1,0:T(8,128)(2,1)}, u32[]{:S(2)}, u32[]{:S(2)}) collective-permute-start(bf16[16,2,32,512]{3,2,1,0:T(8,128)(2,1)S(1)} %all-to-all-done.2), channel_id=1, source_target_pairs={{0,16},{16,0},{32,48},{48,32},{64,80},{80,64},{96,112},{112,96},{1... | collective-permute-start | bytes 3145736 | tf_op jit(solution)/shard_map/diagonal/ppermute | solution.py:86
  90.9 25.2 %all-to-all-start.1 = ((bf16[16,32,1024]{2,1,0:T(8,128)(2,1)}), bf16[16,32,1024]{2,1,0:T(8,128)(2,1)S(1)}, u32[]{:S(2)}, u32[]{:S(2)}) async-start(bf16[16,32,1024]{2,1,0:T(8,128)(2,1)} %broadcast_in_dim.20), calls=%async_computation.1 | async-start | bytes 2097152 | tf_op jit(solution)/shard_map/gather_rows/all_to_all | solution.py:64
  97.5 16.3 %collective-permute-start.9 = (bf16[512,512]{1,0:T(8,128)(2,1)}, bf16[512,512]{1,0:T(8,128)(2,1)}, u32[]{:S(2)}, u32[]{:S(2)}) collective-permute-start(bf16[512,512]{1,0:T(8,128)(2,1)} %broadcast_select_fusion.3), channel_id=1, source_target_pairs={{0,15},{1,2},{2,1},{3,4},{4,3},{5,6},{6,5},{7,8},{8,7},{9,10},{10,... | collective-permute-start | bytes 1572872 | tf_op jit(solution)/shard_map/panels/ppermute | solution.py:31
  116.1 4.9 %copy-start.2 = (bf16[16,32,1024]{2,1,0:T(8,128)(2,1)}, bf16[16,32,1024]{2,1,0:T(8,128)(2,1)S(1)}, u32[]{:S(2)}) copy-start(bf16[16,32,1024]{2,1,0:T(8,128)(2,1)S(1)} %all-to-all-done.1) | copy-start | bytes 3145732
  116.1 20.2 %collective-permute-start.11 = (bf16[512,1024]{1,0:T(8,128)(2,1)S(1)}, bf16[512,1024]{1,0:T(8,128)(2,1)S(1)}, u32[]{:S(2)}, u32[]{:S(2)}) collective-permute-start(bf16[512,1024]{1,0:T(8,128)(2,1)S(1)} %bitcast.68), channel_id=1, source_target_pairs={{0,16},{16,0},{32,48},{48,32},{64,80},{80,64},{96,112},{112,96},{1... | collective-permute-start | bytes 3145736 | tf_op jit(solution)/shard_map/gather_rows/ppermute | solution.py:94
  121.0 1.6 %copy-start.1 = (f32[2,512,512]{2,1,0:T(8,128)S(1)}, f32[2,512,512]{2,1,0:T(8,128)}, u32[]{:S(2)}) copy-start(f32[2,512,512]{2,1,0:T(8,128)} %param.3) | copy-start | bytes 6291460
  122.6 4.6 %copy-start.5 = (bf16[512,512]{1,0:T(8,128)(2,1)S(1)}, bf16[512,512]{1,0:T(8,128)(2,1)}, u32[]{:S(2)}) copy-start(bf16[512,512]{1,0:T(8,128)(2,1)} %get-tuple-element.20) | copy-start | bytes 1572868
  128.1 0.8 copy-start.7
  130.9 3.5 %copy-start.4 = (bf16[512,512]{1,0:T(8,128)(2,1)S(1)}, bf16[512,512]{1,0:T(8,128)(2,1)}, u32[]{:S(2)}) copy-start(bf16[512,512]{1,0:T(8,128)(2,1)} %get-tuple-element.19) | copy-start | bytes 1572868
  130.9 5.4 %copy-start.3 = (bf16[16,32,1024]{2,1,0:T(8,128)(2,1)S(1)}, bf16[16,32,1024]{2,1,0:T(8,128)(2,1)}, u32[]{:S(2)}) copy-start(bf16[16,32,1024]{2,1,0:T(8,128)(2,1)} %copy-done.2) | copy-start | bytes 3145732
  136.3 1.4 copy-start.6
  136.3 1.0 copy-start.8

commit v3 on v2

--- a/solution.py
+++ b/solution.py
@@ -16,13 +16,13 @@
     return base.astype(jnp.float32) - jnp.dot(left, right, preferred_element_type=jnp.float32)
 
 
-def panel_step(held, reach, cols):
+def panel_step(held, level, cols):
+    tree = [[(0, 10)], [(0, 4), (10, 6)], [(0, 14), (4, 2), (6, 8), (10, 12)]][level]
+    pairs = tree + [((1 - s) % cols, (1 - t) % cols) for s, t in tree]
+    got = lax.ppermute(held, "col", pairs)
     col = lax.axis_index("col")
-    step = 2 * reach
-    pairs = [(s, (s - reach) % cols) for s in range(0, cols, step)]
-    pairs += [(s + 1, (s + 1 + reach) % cols) for s in range(0, cols, step)]
-    got = lax.ppermute(held, "col", pairs)
-    return jnp.where((col - col % 2) % step == 0, held, got)
+    arrives = jnp.any(jnp.stack([col == t for _, t in pairs]))
+    return jnp.where(arrives, got, held)
 
 
 def panel_pair(held, cols):
@@ -64,17 +64,23 @@
         return lax.all_to_all(copies, "row", 0, 0, tiled=True, axis_index_groups=same_core)
 
     with jax.named_scope("panels"):
-        held = panel_step(matrix[:, 0, 0, :], 8, cols)
+        held = panel_step(matrix[:, 0, 0, :], 0, cols)
     with jax.named_scope("scatter_rows"):
         dealt = lax.all_to_all(
             matrix, "row", 0, 0, tiled=True, axis_index_groups=same_core
         )[:part, 0]
     dealt, held = lax.optimization_barrier((dealt, held))
     with jax.named_scope("panels"):
-        held = panel_step(held, 4, cols)
+        held = panel_step(held, 1, cols)
+    with jax.named_scope("gather_rows"):
+        own_rows = gather_part(dealt.reshape(part, -1)).reshape(size, -1)
     with jax.named_scope("diagonal"):
         pieces = spread_diagonal(dealt[:, 0, :], cols)
-        pieces, held = lax.optimization_barrier((pieces, held))
+        pieces, held, own_rows = lax.optimization_barrier((pieces, held, own_rows))
+    with jax.named_scope("gather_rows"):
+        other_rows = lax.ppermute(own_rows, "row", swap_core)
+        upper0 = jnp.where(core == 0, own_rows, other_rows)
+        raw1 = jnp.where(core == 0, other_rows, own_rows)
     with jax.named_scope("panels"):
         held = panel_step(held, 2, cols)
     with jax.named_scope("diagonal"):
@@ -88,12 +94,6 @@
         low = jnp.where(core == 0, other, mine)
         d00, d01 = (top[:, k].reshape(size, size) for k in range(2))
         d10, d11 = (low[:, k].reshape(size, size) for k in range(2))
-    with jax.named_scope("gather_rows"):
-        own_rows = gather_part(dealt.reshape(part, -1)).reshape(size, -1)
-        own_rows, panel0, panel1 = lax.optimization_barrier((own_rows, panel0, panel1))
-        other_rows = lax.ppermute(own_rows, "row", swap_core)
-        upper0 = jnp.where(core == 0, own_rows, other_rows)
-        raw1 = jnp.where(core == 0, other_rows, own_rows)
     with jax.named_scope("inverses"):
         inverse0 = refined_inverse(d00, inverses[0])
         lower10 = jnp.dot(d10, inverse0, preferred_element_type=jnp.float32).astype(jnp.bfloat16)

time: 148 us -> 136 us (0.919)
  the two profiles are of different devices: /device:TPU:99 before, /device:TPU:1 now
where the time goes in v3:
time: 136 us; the launch traced here: 135 us
  starting transfers between devices  67.7 us (50%)
  waiting for transfers between devices  32.2 us (24%)
  matrix products  18.7 us (14%)
  local copies, waits for them, and re-layouts  11 us (8%)
  other arithmetic  4.46 us (3%)
    ppermute x3, starting transfers between devices, panel_step(): got = lax.ppermute(held, 'col', pairs)  18 us
    ppermute x3, waiting for transfers between devices, panel_step(): got = lax.ppermute(held, 'col', pairs)  15.8 us
    ppermute x1, starting transfers between devices, local(): other = lax.ppermute(mine, 'row', swap_core)  13.7 us
    all_to_all x2, starting transfers between devices, gather_part(): lax.all_to_all(copies, 'row', 0, 0, tiled=True, axis_index_groups=same_core)  12.9 us
    all_to_all x1, starting transfers between devices, local(): lax.all_to_all(matrix, 'row', 0, 0, tiled=True, axis_index_groups=same_core)  7.72 us
    dot_general x2, matrix products, refined_inverse(): jnp.dot(approx, 2.0 * identity - product, precision=highest)  6.97 us
    ppermute x1, waiting for transfers between devices, panel_pair(): other = lax.ppermute(held, 'col', pairs)  6.66 us
    ppermute x3, starting transfers between devices, spread_diagonal(): lax.ppermute(piece, 'col', [(0, quarter * k), (1, quarter * k + 1)])  6.16 us
  transfers between devices with their start and end apart: 15, of which 7 were waited for; matrix products, arithmetic and copies ran while one was open for 13% of the time, Pallas kernels for 0%

profile of v3, /device:TPU:1, one launch (start us, length us, event | category | flops | bytes accessed | tf_op | source)
XLA Modules:
  0.0 134.6 jit_solution(4287307519309782536)
XLA Ops:
  0.0 7.7 %all-to-all-start = ((bf16[512,1,2,512]{3,2,1,0:T(2,128)(2,1)}), bf16[512,1,2,512]{3,2,1,0:T(2,128)(2,1)S(1)}, u32[]{:S(2)}, u32[]{:S(2)}) async-start(bf16[512,1,2,512]{3,2,1,0:T(2,128)(2,1)} %param.2), calls=%async_computation | async-start | bytes 2097152 | tf_op jit(solution)/shard_map/scatter_rows/all_to_all | solution.py:69
  7.9 14.6 %collective-permute-start = (bf16[512,512]{1,0:T(8,128)(2,1)S(1)}, bf16[512,512]{1,0:T(8,128)(2,1)S(1)}, u32[]{:S(2)}, u32[]{:S(2)}) collective-permute-start(bf16[512,512]{1,0:T(8,128)(2,1)S(1)} %bitcast.78), channel_id=1, source_target_pairs={{0,10},{1,7},{16,26},{17,23},{32,42},{33,39},{48,58},{49,55},{64,7... | collective-permute-start | bytes 1572872 | tf_op jit(solution)/shard_map/panels/ppermute | solution.py:22
  22.5 10.2 %collective-permute-done = bf16[512,512]{1,0:T(8,128)(2,1)S(1)} collective-permute-done((bf16[512,512]{1,0:T(8,128)(2,1)S(1)}, bf16[512,512]{1,0:T(8,128)(2,1)S(1)}, u32[]{:S(2)}, u32[]{:S(2)}) %collective-permute-start) | collective-permute-done | bytes 524320 | tf_op jit(solution)/shard_map/panels/ppermute | solution.py:22
  32.9 1.1 broadcast_in_dim.20
  34.0 6.4 %all-to-all-start.1 = ((bf16[16,32,1024]{2,1,0:T(8,128)(2,1)}), bf16[16,32,1024]{2,1,0:T(8,128)(2,1)S(1)}, u32[]{:S(2)}, u32[]{:S(2)}) async-start(bf16[16,32,1024]{2,1,0:T(8,128)(2,1)} %broadcast_in_dim.20), calls=%async_computation.1 | async-start | bytes 2097152 | tf_op jit(solution)/shard_map/gather_rows/all_to_all | solution.py:64
  40.3 1.3 collective-permute-start.3
  41.6 3.6 %collective-permute-start.2 = (bf16[32,512]{1,0:T(8,128)(2,1)S(1)}, bf16[32,512]{1,0:T(8,128)(2,1)S(1)}, u32[]{:S(2)}, u32[]{:S(2)}) collective-permute-start(bf16[32,512]{1,0:T(8,128)(2,1)S(1)} %slice_bitcast_fusion), channel_id=1, source_target_pairs={{0,8},{1,9},{16,24},{17,25},{32,40},{33,41},{48,56},{49,57},{64,72... | collective-permute-start | bytes 98312 | tf_op jit(solution)/shard_map/diagonal/ppermute | solution.py:39
  45.2 1.3 collective-permute-start.1
  46.5 1.3 collective-permute-start.7
  47.9 1.3 collective-permute-start.6
  49.2 1.3 collective-permute-start.5
  50.5 2.6 %collective-permute-start.4 = (bf16[32,512]{1,0:T(8,128)(2,1)S(1)}, bf16[32,512]{1,0:T(8,128)(2,1)S(1)}, u32[]{:S(2)}, u32[]{:S(2)}) collective-permute-start(bf16[32,512]{1,0:T(8,128)(2,1)S(1)} %add_select_fusion), channel_id=1, source_target_pairs={{0,1},{1,0},{4,5},{5,4},{8,9},{9,8},{12,13},{13,12},{16,17},{17,16... | collective-permute-start | bytes 98312 | tf_op jit(solution)/shard_map/diagonal/ppermute | solution.py:43
  53.2 5.8 %collective-permute-done.6 = bf16[32,512]{1,0:T(8,128)(2,1)S(1)} collective-permute-done((bf16[32,512]{1,0:T(8,128)(2,1)S(1)}, bf16[32,512]{1,0:T(8,128)(2,1)S(1)}, u32[]{:S(2)}, u32[]{:S(2)}) %collective-permute-start.6) | collective-permute-done | bytes 32800 | tf_op jit(solution)/shard_map/diagonal/ppermute | solution.py:45
  59.0 0.7 collective-permute-done.5
  59.7 0.7 collective-permute-done.4
  60.4 0.9 broadcast_select_fusion.4
  61.3 1.2 broadcast_in_dim.21
  62.5 6.6 %all-to-all-start.2 = ((bf16[16,2,32,512]{3,2,1,0:T(8,128)(2,1)}), bf16[16,2,32,512]{3,2,1,0:T(8,128)(2,1)S(1)}, u32[]{:S(2)}, u32[]{:S(2)}) async-start(bf16[16,2,32,512]{3,2,1,0:T(8,128)(2,1)} %broadcast_in_dim.21), calls=%async_computation.2 | async-start | bytes 2097152 | tf_op jit(solution)/shard_map/diagonal/all_to_all | solution.py:64
  69.1 2.1 %collective-permute-start.8 = (bf16[512,512]{1,0:T(8,128)(2,1)}, bf16[512,512]{1,0:T(8,128)(2,1)}, u32[]{:S(2)}, u32[]{:S(2)}) collective-permute-start(bf16[512,512]{1,0:T(8,128)(2,1)} %broadcast_select_fusion.4), channel_id=1, source_target_pairs={{0,14},{4,2},{6,8},{10,12},{1,3},{13,15},{11,9},{7,5},{16,30},{20,... | collective-permute-start | bytes 1572872 | tf_op jit(solution)/shard_map/panels/ppermute | solution.py:22
  71.2 5.6 %collective-permute-done.8 = bf16[512,512]{1,0:T(8,128)(2,1)} collective-permute-done((bf16[512,512]{1,0:T(8,128)(2,1)}, bf16[512,512]{1,0:T(8,128)(2,1)}, u32[]{:S(2)}, u32[]{:S(2)}) %collective-permute-start.8) | collective-permute-done | bytes 524320 | tf_op jit(solution)/shard_map/panels/ppermute | solution.py:22
  76.8 1.9 %broadcast_select_fusion.3 = bf16[512,512]{1,0:T(8,128)(2,1)} fusion(bf16[512,512]{1,0:T(8,128)(2,1)} %collective-permute-done.8, bf16[512,512]{1,0:T(8,128)(2,1)} %broadcast_select_fusion.4, pred[]{:T(512)S(6)} %reduce_or.55), kind=kLoop, calls=%fused_computation.40 | loop fusion | flops 262144 | bytes 1572865 | tf_op jit(solution)/shard_map/panels/jit(_where)/select_n | solution.py:25
  78.8 2.5 %all-to-all-done.2 = bf16[16,2,32,512]{3,2,1,0:T(8,128)(2,1)S(1)} async-done(((bf16[16,2,32,512]{3,2,1,0:T(8,128)(2,1)}), bf16[16,2,32,512]{3,2,1,0:T(8,128)(2,1)S(1)}, u32[]{:S(2)}, u32[]{:S(2)}) %all-to-all-start.2) | async-done | bytes 1048608 | tf_op jit(solution)/shard_map/diagonal/all_to_all | solution.py:64
  81.3 13.7 %collective-permute-start.10 = (bf16[16,2,32,512]{3,2,1,0:T(8,128)(2,1)S(1)}, bf16[16,2,32,512]{3,2,1,0:T(8,128)(2,1)}, u32[]{:S(2)}, u32[]{:S(2)}) collective-permute-start(bf16[16,2,32,512]{3,2,1,0:T(8,128)(2,1)S(1)} %all-to-all-done.2), channel_id=1, source_target_pairs={{0,16},{16,0},{32,48},{48,32},{64,80},{80,64},{96,112},{112,96},{1... | collective-permute-start | bytes 3145736 | tf_op jit(solution)/shard_map/diagonal/ppermute | solution.py:92
  95.0 1.7 %copy.29 = f32[64,8,2,512]{3,1,2,0:T(8,128)} copy(bf16[64,8,2,512]{3,2,1,0:T(2,128)(2,1)S(1)} %bitcast.64) | data formatting | bytes 3145728
  96.7 1.9 %collective-permute-start.11 = (bf16[512,1024]{1,0:T(8,128)(2,1)S(1)}, bf16[512,1024]{1,0:T(8,128)(2,1)S(1)}, u32[]{:S(2)}, u32[]{:S(2)}) collective-permute-start(bf16[512,1024]{1,0:T(8,128)(2,1)S(1)} %bitcast.67), channel_id=1, source_target_pairs={{0,16},{16,0},{32,48},{48,32},{64,80},{80,64},{96,112},{112,96},{1... | collective-permute-start | bytes 3145736 | tf_op jit(solution)/shard_map/gather_rows/ppermute | solution.py:81
  98.6 2.1 %collective-permute-start.9 = (bf16[512,512]{1,0:T(8,128)(2,1)}, bf16[512,512]{1,0:T(8,128)(2,1)S(1)}, u32[]{:S(2)}, u32[]{:S(2)}) collective-permute-start(bf16[512,512]{1,0:T(8,128)(2,1)} %broadcast_select_fusion.3), channel_id=1, source_target_pairs={{0,15},{1,2},{2,1},{3,4},{4,3},{5,6},{6,5},{7,8},{8,7},{9,10},{10,... | collective-permute-start | bytes 1572872 | tf_op jit(solution)/shard_map/panels/ppermute | solution.py:31
  100.7 1.4 %broadcast_select_fusion.1 = (bf16[16,2,32,512]{3,2,1,0:T(8,128)(2,1)S(1)}, bf16[16,2,32,512]{3,2,1,0:T(8,128)(2,1)S(1)}) fusion(bf16[16,2,32,512]{3,2,1,0:T(8,128)(2,1)} %collective-permute-done.10, bf16[16,2,32,512]{3,2,1,0:T(8,128)(2,1)S(1)} %all-to-all-done.2, pred[]{:T(512)S(6)} %eq.99), kind=kLoop, calls=%fused_computation.23 | loop fusion | flops 1048576 | bytes 4194305 | tf_op jit(solution)/shard_map/diagonal/jit(_where)/select_n | solution.py:94
  102.1 0.2 fusion.32
  102.3 1.4 %copy-done.1 = f32[2,512,512]{2,1,0:T(8,128)S(1)} copy-done((f32[2,512,512]{2,1,0:T(8,128)S(1)}, f32[2,512,512]{2,1,0:T(8,128)}, u32[]{:S(2)}) %copy-start.1) | copy-done | bytes 2097176
  103.7 1.1 select_subtract_fusion.1
  104.8 3.5 %convolution_convert_fusion.4 = bf16[512,512]{1,0:T(8,128)(2,1)S(1)} fusion(f32[512,512]{1,0:T(8,128)S(1)} %select_subtract_fusion.1, f32[2,512,512]{2,1,0:T(8,128)S(1)} %copy-done.1), kind=kOutput, calls=%fused_computation.8 | convolution fusion | flops 1610874880 | bytes 2621440 | tf_op jit(solution)/shard_map/inverses/dot_general | solution.py:12
  108.3 6.7 %collective-permute-done.9 = bf16[512,512]{1,0:T(8,128)(2,1)S(1)} collective-permute-done((bf16[512,512]{1,0:T(8,128)(2,1)}, bf16[512,512]{1,0:T(8,128)(2,1)S(1)}, u32[]{:S(2)}, u32[]{:S(2)}) %collective-permute-start.9) | collective-permute-done | bytes 524320 | tf_op jit(solution)/shard_map/panels/ppermute | solution.py:31
  114.9 0.5 convolution_convert_fusion.1
  115.4 0.4 fusion.34
  115.8 0.5 convolution_convert_fusion
  116.3 0.4 fusion.35
  116.8 0.4 copy-done.4
  117.1 1.1 select_subtract_fusion
  118.2 3.5 %convolution_convert_fusion.3 = bf16[512,512]{1,0:T(8,128)(2,1)S(1)} fusion(f32[512,512]{1,0:T(8,128)S(1)} %select_subtract_fusion, f32[2,512,512]{2,1,0:T(8,128)S(1)} %copy-done.1), kind=kOutput, calls=%fused_computation.7 | convolution fusion | flops 1610874880 | bytes 2621440 | tf_op jit(solution)/shard_map/inverses/dot_general | solution.py:12
  121.8 0.7 fusion.18
  122.5 0.2 copy-done.8
  122.7 1.9 %convolution_convert_fusion.2 = bf16[512,512]{1,0:T(8,128)(2,1)} fusion(bf16[512,512]{1,0:T(8,128)(2,1)S(1)} %convolution_convert_fusion.3, f32[512,512]{1,0:T(8,128)S(1)} %fusion.34, bf16[512,512]{1,0:T(8,128)(2,1)S(1)} %collective-permute-done.9, bf16[512,512]{1,0:T(8,128)(2,1)S(1)} %copy-done.6, pred[]{:T(512)S(6)} %eq.80), kind=kOutput, calls=%fused_computation.6 | convolution fusion | flops 1611661312 | bytes 3145729 | tf_op jit(solution)/shard_map/update/dot_general | solution.py:105
  124.6 5.2 %subtract_convert_fusion = bf16[512,1024]{1,0:T(8,128)(2,1)} fusion(f32[512,1024]{1,0:T(8,128)} %bitcast.71, f32[512,1024]{1,0:T(8,128)S(1)} %fusion.18, bf16[512,1024]{1,0:T(8,128)(2,1)} %copy-done.8, bf16[512,1024]{1,0:T(8,128)(2,1)} %bitcast.68, pred[]{:T(512)S(6)} %eq.99, bf16[512,512]{1,0:T(8,128)(2,1)} %convolution_convert_fusion.2, pred[]{:T(512)S(6)} %gt.8, ...), kind=kOutput, calls=%fused_computation | convolution fusion | flops 1078198272 | bytes 8388610 | tf_op jit(solution)/shard_map/update/dot_general | solution.py:112
  129.8 1.5 %copy.20 = bf16[512,1024]{0,1:T(8,128)(2,1)S(1)} copy(bf16[512,1024]{1,0:T(8,128)(2,1)} %subtract_convert_fusion) | data formatting | bytes 2097152 | tf_op jit(solution)/shard_map/update/convert_element_type | solution.py:113
  131.3 0.2 copy.26
  131.6 0.2 copy.27
  131.8 0.6 copy-done.7
  132.6 2.0 %copy.23 = bf16[512,1,2,512]{3,2,1,0:T(2,128)(2,1)} copy(bf16[512,1,2,512]{3,0,2,1:T(8,128)(2,1)S(1)} %maximum_bitcast_fusion) | data formatting | bytes 2097152 | tf_op jit(solution)/shard_map/update/broadcast_in_dim | solution.py:117
  (34 shorter events, 0.6 us)
Async XLA Ops:
  0.0 7.7 %copy-start = (bf16[512,1,2,512]{3,2,1,0:T(2,128)(2,1)S(1)}, bf16[512,1,2,512]{3,2,1,0:T(2,128)(2,1)}, u32[]{:S(2)}) copy-start(bf16[512,1,2,512]{3,2,1,0:T(2,128)(2,1)} %param.2) | copy-start | bytes 3145732
  0.0 32.8 %all-to-all-start = ((bf16[512,1,2,512]{3,2,1,0:T(2,128)(2,1)}), bf16[512,1,2,512]{3,2,1,0:T(2,128)(2,1)S(1)}, u32[]{:S(2)}, u32[]{:S(2)}) async-start(bf16[512,1,2,512]{3,2,1,0:T(2,128)(2,1)} %param.2), calls=%async_computation | async-start | bytes 2097152 | tf_op jit(solution)/shard_map/scatter_rows/all_to_all | solution.py:69
  7.9 24.8 %collective-permute-start = (bf16[512,512]{1,0:T(8,128)(2,1)S(1)}, bf16[512,512]{1,0:T(8,128)(2,1)S(1)}, u32[]{:S(2)}, u32[]{:S(2)}) collective-permute-start(bf16[512,512]{1,0:T(8,128)(2,1)S(1)} %bitcast.78), channel_id=1, source_target_pairs={{0,10},{1,7},{16,26},{17,23},{32,42},{33,39},{48,58},{49,55},{64,7... | collective-permute-start | bytes 1572872 | tf_op jit(solution)/shard_map/panels/ppermute | solution.py:22
  34.0 27.4 %all-to-all-start.1 = ((bf16[16,32,1024]{2,1,0:T(8,128)(2,1)}), bf16[16,32,1024]{2,1,0:T(8,128)(2,1)S(1)}, u32[]{:S(2)}, u32[]{:S(2)}) async-start(bf16[16,32,1024]{2,1,0:T(8,128)(2,1)} %broadcast_in_dim.20), calls=%async_computation.1 | async-start | bytes 2097152 | tf_op jit(solution)/shard_map/gather_rows/all_to_all | solution.py:64
  40.3 7.5 %collective-permute-start.3 = (bf16[32,512]{1,0:T(8,128)(2,1)S(1)}, bf16[32,512]{1,0:T(8,128)(2,1)S(1)}, u32[]{:S(2)}, u32[]{:S(2)}) collective-permute-start(bf16[32,512]{1,0:T(8,128)(2,1)S(1)} %slice_bitcast_fusion), channel_id=1, source_target_pairs={{0,12},{1,13},{16,28},{17,29},{32,44},{33,45},{48,60},{49,61},{64,... | collective-permute-start | bytes 98312 | tf_op jit(solution)/shard_map/diagonal/ppermute | solution.py:39
  41.6 6.2 %collective-permute-start.2 = (bf16[32,512]{1,0:T(8,128)(2,1)S(1)}, bf16[32,512]{1,0:T(8,128)(2,1)S(1)}, u32[]{:S(2)}, u32[]{:S(2)}) collective-permute-start(bf16[32,512]{1,0:T(8,128)(2,1)S(1)} %slice_bitcast_fusion), channel_id=1, source_target_pairs={{0,8},{1,9},{16,24},{17,25},{32,40},{33,41},{48,56},{49,57},{64,72... | collective-permute-start | bytes 98312 | tf_op jit(solution)/shard_map/diagonal/ppermute | solution.py:39
  45.2 2.7 %collective-permute-start.1 = (bf16[32,512]{1,0:T(8,128)(2,1)S(1)}, bf16[32,512]{1,0:T(8,128)(2,1)S(1)}, u32[]{:S(2)}, u32[]{:S(2)}) collective-permute-start(bf16[32,512]{1,0:T(8,128)(2,1)S(1)} %slice_bitcast_fusion), channel_id=1, source_target_pairs={{0,4},{1,5},{16,20},{17,21},{32,36},{33,37},{48,52},{49,53},{64,68... | collective-permute-start | bytes 98312 | tf_op jit(solution)/shard_map/diagonal/ppermute | solution.py:39
  46.5 13.9 %collective-permute-start.7 = (bf16[512,512]{1,0:T(8,128)(2,1)S(1)}, bf16[512,512]{1,0:T(8,128)(2,1)S(1)}, u32[]{:S(2)}, u32[]{:S(2)}) collective-permute-start(bf16[512,512]{1,0:T(8,128)(2,1)S(1)} %broadcast_select_fusion.5), channel_id=1, source_target_pairs={{0,4},{10,6},{1,13},{7,11},{16,20},{26,22},{17,29},{23,27},{32,36}... | collective-permute-start | bytes 1572872 | tf_op jit(solution)/shard_map/panels/ppermute | solution.py:22
  47.9 11.1 %collective-permute-start.6 = (bf16[32,512]{1,0:T(8,128)(2,1)S(1)}, bf16[32,512]{1,0:T(8,128)(2,1)S(1)}, u32[]{:S(2)}, u32[]{:S(2)}) collective-permute-start(bf16[32,512]{1,0:T(8,128)(2,1)S(1)} %add_select_fusion), channel_id=1, source_target_pairs={{0,3},{1,2},{4,7},{5,6},{8,11},{9,10},{12,15},{13,14},{16,19},{17,... | collective-permute-start | bytes 98312 | tf_op jit(solution)/shard_map/diagonal/ppermute | solution.py:45
  49.2 10.5 %collective-permute-start.5 = (bf16[32,512]{1,0:T(8,128)(2,1)S(1)}, bf16[32,512]{1,0:T(8,128)(2,1)S(1)}, u32[]{:S(2)}, u32[]{:S(2)}) collective-permute-start(bf16[32,512]{1,0:T(8,128)(2,1)S(1)} %add_select_fusion), channel_id=1, source_target_pairs={{0,2},{1,3},{4,6},{5,7},{8,10},{9,11},{12,14},{13,15},{16,18},{17,... | collective-permute-start | bytes 98312 | tf_op jit(solution)/shard_map/diagonal/ppermute | solution.py:44
  50.5 9.9 %collective-permute-start.4 = (bf16[32,512]{1,0:T(8,128)(2,1)S(1)}, bf16[32,512]{1,0:T(8,128)(2,1)S(1)}, u32[]{:S(2)}, u32[]{:S(2)}) collective-permute-start(bf16[32,512]{1,0:T(8,128)(2,1)S(1)} %add_select_fusion), channel_id=1, source_target_pairs={{0,1},{1,0},{4,5},{5,4},{8,9},{9,8},{12,13},{13,12},{16,17},{17,16... | collective-permute-start | bytes 98312 | tf_op jit(solution)/shard_map/diagonal/ppermute | solution.py:43
  61.3 35.4 %copy-start.2 = (bf16[16,32,1024]{2,1,0:T(8,128)(2,1)}, bf16[16,32,1024]{2,1,0:T(8,128)(2,1)S(1)}, u32[]{:S(2)}) copy-start(bf16[16,32,1024]{2,1,0:T(8,128)(2,1)S(1)} %all-to-all-done.1) | copy-start | bytes 3145732
  62.5 18.8 %all-to-all-start.2 = ((bf16[16,2,32,512]{3,2,1,0:T(8,128)(2,1)}), bf16[16,2,32,512]{3,2,1,0:T(8,128)(2,1)S(1)}, u32[]{:S(2)}, u32[]{:S(2)}) async-start(bf16[16,2,32,512]{3,2,1,0:T(8,128)(2,1)} %broadcast_in_dim.21), calls=%async_computation.2 | async-start | bytes 2097152 | tf_op jit(solution)/shard_map/diagonal/all_to_all | solution.py:64
  69.1 7.7 %collective-permute-start.8 = (bf16[512,512]{1,0:T(8,128)(2,1)}, bf16[512,512]{1,0:T(8,128)(2,1)}, u32[]{:S(2)}, u32[]{:S(2)}) collective-permute-start(bf16[512,512]{1,0:T(8,128)(2,1)} %broadcast_select_fusion.4), channel_id=1, source_target_pairs={{0,14},{4,2},{6,8},{10,12},{1,3},{13,15},{11,9},{7,5},{16,30},{20,... | collective-permute-start | bytes 1572872 | tf_op jit(solution)/shard_map/panels/ppermute | solution.py:22
  81.3 19.4 %collective-permute-start.10 = (bf16[16,2,32,512]{3,2,1,0:T(8,128)(2,1)S(1)}, bf16[16,2,32,512]{3,2,1,0:T(8,128)(2,1)}, u32[]{:S(2)}, u32[]{:S(2)}) collective-permute-start(bf16[16,2,32,512]{3,2,1,0:T(8,128)(2,1)S(1)} %all-to-all-done.2), channel_id=1, source_target_pairs={{0,16},{16,0},{32,48},{48,32},{64,80},{80,64},{96,112},{112,96},{1... | collective-permute-start | bytes 3145736 | tf_op jit(solution)/shard_map/diagonal/ppermute | solution.py:92
  96.7 25.0 %collective-permute-start.11 = (bf16[512,1024]{1,0:T(8,128)(2,1)S(1)}, bf16[512,1024]{1,0:T(8,128)(2,1)S(1)}, u32[]{:S(2)}, u32[]{:S(2)}) collective-permute-start(bf16[512,1024]{1,0:T(8,128)(2,1)S(1)} %bitcast.67), channel_id=1, source_target_pairs={{0,16},{16,0},{32,48},{48,32},{64,80},{80,64},{96,112},{112,96},{1... | collective-permute-start | bytes 3145736 | tf_op jit(solution)/shard_map/gather_rows/ppermute | solution.py:81
  98.6 16.3 %collective-permute-start.9 = (bf16[512,512]{1,0:T(8,128)(2,1)}, bf16[512,512]{1,0:T(8,128)(2,1)S(1)}, u32[]{:S(2)}, u32[]{:S(2)}) collective-permute-start(bf16[512,512]{1,0:T(8,128)(2,1)} %broadcast_select_fusion.3), channel_id=1, source_target_pairs={{0,15},{1,2},{2,1},{3,4},{4,3},{5,6},{6,5},{7,8},{8,7},{9,10},{10,... | collective-permute-start | bytes 1572872 | tf_op jit(solution)/shard_map/panels/ppermute | solution.py:31
  102.1 1.6 %copy-start.1 = (f32[2,512,512]{2,1,0:T(8,128)S(1)}, f32[2,512,512]{2,1,0:T(8,128)}, u32[]{:S(2)}) copy-start(f32[2,512,512]{2,1,0:T(8,128)} %param.3) | copy-start | bytes 6291460
  103.7 11.2 %copy-start.6 = (bf16[512,512]{1,0:T(8,128)(2,1)S(1)}, bf16[512,512]{1,0:T(8,128)(2,1)}, u32[]{:S(2)}) copy-start(bf16[512,512]{1,0:T(8,128)(2,1)} %broadcast_select_fusion.3) | copy-start | bytes 1572868
  116.3 0.8 copy-start.4
  118.2 3.5 %copy-start.3 = (bf16[16,32,1024]{2,1,0:T(8,128)(2,1)S(1)}, bf16[16,32,1024]{2,1,0:T(8,128)(2,1)}, u32[]{:S(2)}) copy-start(bf16[16,32,1024]{2,1,0:T(8,128)(2,1)} %copy-done.2) | copy-start | bytes 3145732
  121.7 1.0 copy-start.8
  122.7 1.9 %copy-start.5 = (bf16[512,512]{1,0:T(8,128)(2,1)S(1)}, bf16[512,512]{1,0:T(8,128)(2,1)}, u32[]{:S(2)}) copy-start(bf16[512,512]{1,0:T(8,128)(2,1)} %copy-done.4) | copy-start | bytes 1572868
  131.3 1.0 copy-start.7

commit v4 on v3

v4 whole, which is shorter than its diff:
```python
import jax
import jax.numpy as jnp
from jax import lax
from jax.experimental import pallas as pl
from jax.experimental.pallas import tpu as pltpu
from jax.sharding import PartitionSpec as P

whole = pl.BlockSpec(memory_space=pltpu.VMEM)
params = pltpu.CompilerParams(vmem_limit_bytes=48 * 1024 * 1024)


def product(left, right):
    return jnp.dot(left, right, preferred_element_type=jnp.float32)


def two_parts(value):
    high = value.astype(jnp.bfloat16)
    return high, (value - high.astype(jnp.float32)).astype(jnp.bfloat16)


def refined_inverse(diagonal, approx):
    size = diagonal.shape[0]
    high, low = two_parts(approx)
    row_ids = lax.broadcasted_iota(jnp.int32, (size, size), 0)
    col_ids = lax.broadcasted_iota(jnp.int32, (size, size), 1)
    twice = jnp.where(row_ids == col_ids, 2.0, 0.0)
    rest_high, rest_low = two_parts(twice - (product(diagonal, high) + product(diagonal, low)))
    small = product(high, rest_low) + product(low, rest_high)
    return (product(high, rest_high) + small).astype(jnp.bfloat16)


def upper_kernel(
    own_diag, other_diag, own_rows, other_rows, approx,
    inverse0_ref, inverse1_ref, corner_ref, upper0_ref, upper1_ref,
):
    first = lax.axis_index("row") % 2 == 0
    size = inverse0_ref.shape[0]

    def block(row, col):
        own, other = own_diag[:, col], other_diag[:, col]
        picked = jnp.where(first, own, other) if row == 0 else jnp.where(first, other, own)
        return picked.reshape(size, size)

    inverse0 = refined_inverse(block(0, 0), approx[0])
    inverse0_ref[...] = inverse0
    corner = block(0, 1)
    corner_ref[...] = corner
    lower10 = product(block(1, 0), inverse0).astype(jnp.bfloat16)
    upper11 = (block(1, 1).astype(jnp.float32) - product(lower10, corner)).astype(jnp.bfloat16)
    inverse1_ref[...] = refined_inverse(upper11, approx[1])
    upper0 = jnp.where(first, own_rows[...], other_rows[...])
    upper0_ref[...] = upper0
    raw1 = jnp.where(first, other_rows[...], own_rows[...])
    upper1_ref[...] = (raw1.astype(jnp.float32) - product(lower10, upper0)).astype(jnp.bfloat16)


def update_kernel(
    held, other, block, inverse0, inverse1, corner, upper0, upper1, out,
):
    row, col = lax.axis_index("row"), lax.axis_index("col")
    even = col % 2 == 0
    size = inverse0.shape[0]
    half = size // 2
    for part in range(2):
        rows = pl.ds(part * half, half)
        panel0 = jnp.where(even, held[rows], other[rows])
        panel1 = jnp.where(even, other[rows], held[rows])
        lower0 = product(panel0, inverse0[...]).astype(jnp.bfloat16)
        rest = panel1.astype(jnp.float32) - product(lower0, corner[...])
        rest_high, rest_low = two_parts(rest)
        lower1 = product(rest_high, inverse1[...]) + product(rest_low, inverse1[...])
        lower1 = lower1.astype(jnp.bfloat16)
        used0 = jnp.where(row > 0, lower0, jnp.zeros_like(lower0))
        used1 = jnp.where(row > 1, lower1, jnp.zeros_like(lower1))
        fresh = block[rows].astype(jnp.float32) - product(used0, upper0[...])
        out[rows] = (fresh - product(used1, upper1[...])).astype(jnp.bfloat16)

        @pl.when((col == 0) & (row > 0))
        def _():
            out[rows, pl.ds(0, size)] = lower0

        @pl.when((col == 1) & (row > 1))
        def _():
            out[rows, pl.ds(0, size)] = lower1


def local_call(kernel, count, shapes):
    return pl.pallas_call(
        kernel,
        out_shape=[jax.ShapeDtypeStruct(shape, jnp.bfloat16) for shape in shapes],
        in_specs=[whole] * count,
        out_specs=[whole] * len(shapes),
        compiler_params=params,
    )


def panel_step(held, level, cols):
    tree = [[(0, 10)], [(0, 4), (10, 6)], [(0, 14), (4, 2), (6, 8), (10, 12)]][level]
    pairs = tree + [((1 - s) % cols, (1 - t) % cols) for s, t in tree]
    got = lax.ppermute(held, "col", pairs)
    col = lax.axis_index("col")
    arrives = jnp.any(jnp.stack([col == t for _, t in pairs]))
    return jnp.where(arrives, got, held)


def panel_pair(held, cols):
    pairs = [(s, (s - 1) % cols) if s % 2 == 0 else (s, (s + 1) % cols) for s in range(cols)]
    return lax.ppermute(held, "col", pairs)


def spread_diagonal(piece, cols):
    col = lax.axis_index("col")
    quarter = cols // 4
    got = [
        lax.ppermute(piece, "col", [(0, quarter * k), (1, quarter * k + 1)]) for k in range(1, 4)
    ]
    held = jnp.where(col < 2, piece, got[0] + got[1] + got[2])
    groups = range(0, cols, 4)
    swap = lax.ppermute(held, "col", [p for g in groups for p in ((g, g + 1), (g + 1, g))])
    near = lax.ppermute(held, "col", [p for g in groups for p in ((g, g + 2), (g + 1, g + 3))])
    far = lax.ppermute(held, "col", [p for g in groups for p in ((g, g + 3), (g + 1, g + 2))])
    place = col % 4
    first = jnp.where(place == 0, held, jnp.where(place == 1, swap, jnp.where(place == 2, near, far)))
    second = jnp.where(place == 0, swap, jnp.where(place == 1, held, jnp.where(place == 2, far, near)))
    return jnp.stack([first, second])


def local(matrix, inverses):
    rows, cols = lax.axis_size("row"), lax.axis_size("col")
    size = matrix.shape[0]
    chips = rows // 2
    part = size // chips
    same_core = [[2 * chip + core for chip in range(chips)] for core in range(2)]
    swap_core = [(r, r ^ 1) for r in range(rows)]

    def gather_part(piece):
        copies = jnp.broadcast_to(piece[None], (chips,) + piece.shape)
        return lax.all_to_all(copies, "row", 0, 0, tiled=True, axis_index_groups=same_core)

    with jax.named_scope("panels"):
        held = panel_step(matrix[:, 0, 0, :], 0, cols)
    with jax.named_scope("scatter_rows"):
        dealt = lax.all_to_all(
            matrix, "row", 0, 0, tiled=True, axis_index_groups=same_core
        )[:part, 0]
    dealt, held = lax.optimization_barrier((dealt, held))
    with jax.named_scope("panels"):
        held = panel_step(held, 1, cols)
    with jax.named_scope("gather_rows"):
        own_rows = gather_part(dealt.reshape(part, -1)).reshape(size, -1)
    with jax.named_scope("diagonal"):
        pieces = spread_diagonal(dealt[:, 0, :], cols)
        pieces, held, own_rows = lax.optimization_barrier((pieces, held, own_rows))
    with jax.named_scope("gather_rows"):
        other_rows = lax.ppermute(own_rows, "row", swap_core)
    with jax.named_scope("panels"):
        held = panel_step(held, 2, cols)
    with jax.named_scope("diagonal"):
        mine = gather_part(pieces)
        mine, held = lax.optimization_barrier((mine, held))
    with jax.named_scope("panels"):
        panel = panel_pair(held, cols)
    with jax.named_scope("diagonal"):
        other = lax.ppermute(mine, "row", swap_core)
    square, wide = (size, size), (size, 2 * size)
    with jax.named_scope("upper"):
        inverse0, inverse1, corner, upper0, upper1 = local_call(
            upper_kernel, 5, [square, square, square, wide, wide]
        )(mine, other, own_rows, other_rows, inverses)
    with jax.named_scope("update"):
        (fresh,) = local_call(update_kernel, 8, [wide])(
            held, panel, matrix.reshape(wide), inverse0, inverse1, corner, upper0, upper1
        )
    return fresh.reshape(matrix.shape)


def solution(mesh):
    return jax.shard_map(
        local,
        mesh=mesh,
        in_specs=(P("row", "col", None, None), P()),
        out_specs=P("row", "col", None, None),
        check_vma=False,
    )
```

time: 136 us -> 116 us (0.85)
  matrix products: 18.7 us -> 0 us
  waiting for transfers between devices: 32.2 us -> 21.4 us
  Pallas kernels: 0 us -> 10.6 us
  starting transfers between devices: 67.7 us -> 77.7 us
  local copies, waits for them, and re-layouts: 11 us -> 5.17 us
  other arithmetic: 4.46 us -> 0.24 us
    dot_general x11 -> x0, matrix products: 18.7 us -> none  [the longest x2 6.97 us: refined_inverse(): jnp.dot(approx, 2.0 * identity - product, precision=highest)]
    ppermute x1, starting transfers between devices: 1.91 us -> 15.6 us  [local(): other_rows = lax.ppermute(own_rows, 'row', swap_core)]
    pallas_call x0 -> x2, Pallas kernels: none -> 10.6 us  [the longest x1 6.48 us: local(): local_call(upper_kernel, 5, [square, square, square, wide, wide])]
    ppermute x1, starting transfers between devices: 13.7 us -> 5.87 us  [local(): other = lax.ppermute(mine, 'row', swap_core)]
    ppermute x1, waiting for transfers between devices: 0.7 us -> 6.57 us  [spread_diagonal(): lax.ppermute(held, 'col', [p for g in groups for p in ((g, g + 1), (g + 1...]
    ppermute x1, waiting for transfers between devices: 5.79 us -> 0.01 us  [spread_diagonal(): lax.ppermute(held, 'col', [p for g in groups for p in ((g, g + 3), (g + 1...]
    ppermute x3, waiting for transfers between devices: 15.8 us -> 10.2 us  [panel_step(): got = lax.ppermute(held, 'col', pairs)]
    ppermute x1, starting transfers between devices: 2.1 us -> 5.74 us  [panel_pair(): return lax.ppermute(held, 'col', pairs)]
  transfers between devices with their start and end apart: 15 -> 15, of which waited for: 7 -> 3; matrix products, arithmetic and copies ran while one was open for 13% -> 1% of each run, Pallas kernels for 0% -> 6%
where the time goes in v4:
time: 116 us; the launch traced here: 115 us
  starting transfers between devices  77.7 us (67%)
  waiting for transfers between devices  21.4 us (18%)
  Pallas kernels  10.6 us (9%)
  local copies, waits for them, and re-layouts  5.17 us (4%)
    ppermute x3, starting transfers between devices, panel_step(): got = lax.ppermute(held, 'col', pairs)  18.7 us
    ppermute x1, starting transfers between devices, local(): other_rows = lax.ppermute(own_rows, 'row', swap_core)  15.6 us
    all_to_all x2, starting transfers between devices, gather_part(): lax.all_to_all(copies, 'row', 0, 0, tiled=True, axis_index_groups=same_core)  12.7 us
    ppermute x3, waiting for transfers between devices, panel_step(): got = lax.ppermute(held, 'col', pairs)  10.2 us
    all_to_all x1, starting transfers between devices, local(): lax.all_to_all(matrix, 'row', 0, 0, tiled=True, axis_index_groups=same_core)  7.72 us
    ppermute x1, waiting for transfers between devices, spread_diagonal(): lax.ppermute(held, 'col', [p for g in groups for p in ((g, g + 1), (g + 1...  6.57 us
    pallas_call x1, Pallas kernels, local(): local_call(upper_kernel, 5, [square, square, square, wide, wide])  6.48 us
    ppermute x3, starting transfers between devices, spread_diagonal(): lax.ppermute(piece, 'col', [(0, quarter * k), (1, quarter * k + 1)])  6.26 us
  transfers between devices with their start and end apart: 15, of which 3 were waited for; matrix products, arithmetic and copies ran while one was open for 1% of the time, Pallas kernels for 6%

profile of v4, /device:TPU:1, one launch (start us, length us, event | category | flops | bytes accessed | tf_op | source)
XLA Modules:
  0.0 115.5 jit_solution(6114696700619618654)
XLA Ops:
  0.0 0.0 copy-start.1
  0.0 7.7 %all-to-all-start = ((bf16[512,1,2,512]{3,2,1,0:T(2,128)(2,1)}), bf16[512,1,2,512]{3,2,1,0:T(2,128)(2,1)S(1)}, u32[]{:S(2)}, u32[]{:S(2)}) async-start(bf16[512,1,2,512]{3,2,1,0:T(2,128)(2,1)} %param.2), calls=%async_computation | async-start | bytes 2097152 | tf_op jit(solution)/shard_map/scatter_rows/all_to_all | solution.py:143
  7.7 0.0 copy-done.1
  7.7 0.1 copy.24
  7.9 14.6 %collective-permute-start = (bf16[512,512]{1,0:T(8,128)(2,1)S(1)}, bf16[512,512]{1,0:T(8,128)(2,1)S(1)}, u32[]{:S(2)}, u32[]{:S(2)}) collective-permute-start(bf16[512,512]{1,0:T(8,128)(2,1)S(1)} %bitcast.31), channel_id=1, source_target_pairs={{0,10},{1,7},{16,26},{17,23},{32,42},{33,39},{48,58},{49,55},{64,7... | collective-permute-start | bytes 1572872 | tf_op jit(solution)/shard_map/panels/ppermute | solution.py:100
  22.5 10.2 %collective-permute-done = bf16[512,512]{1,0:T(8,128)(2,1)S(1)} collective-permute-done((bf16[512,512]{1,0:T(8,128)(2,1)S(1)}, bf16[512,512]{1,0:T(8,128)(2,1)S(1)}, u32[]{:S(2)}, u32[]{:S(2)}) %collective-permute-start) | collective-permute-done | bytes 524320 | tf_op jit(solution)/shard_map/panels/ppermute | solution.py:100
  32.7 0.1 broadcast_select_fusion.2
  32.8 0.0 all-to-all-done
  32.9 1.1 broadcast_in_dim.14
  34.0 6.4 %all-to-all-start.1 = ((bf16[16,32,1024]{2,1,0:T(8,128)(2,1)}), bf16[16,32,1024]{2,1,0:T(8,128)(2,1)}, u32[]{:S(2)}, u32[]{:S(2)}) async-start(bf16[16,32,1024]{2,1,0:T(8,128)(2,1)} %broadcast_in_dim.14), calls=%async_computation.1 | async-start | bytes 2097152 | tf_op jit(solution)/shard_map/gather_rows/all_to_all | solution.py:138
  40.4 1.3 %collective-permute-start.1 = (bf16[32,512]{1,0:T(8,128)(2,1)S(1)}, bf16[32,512]{1,0:T(8,128)(2,1)S(1)}, u32[]{:S(2)}, u32[]{:S(2)}) collective-permute-start(bf16[32,512]{1,0:T(8,128)(2,1)S(1)} %slice_bitcast_fusion), channel_id=1, source_target_pairs={{0,4},{1,5},{16,20},{17,21},{32,36},{33,37},{48,52},{49,53},{64,68... | collective-permute-start | bytes 98312 | tf_op jit(solution)/shard_map/diagonal/ppermute | solution.py:115
  41.7 3.7 %collective-permute-start.2 = (bf16[32,512]{1,0:T(8,128)(2,1)S(1)}, bf16[32,512]{1,0:T(8,128)(2,1)S(1)}, u32[]{:S(2)}, u32[]{:S(2)}) collective-permute-start(bf16[32,512]{1,0:T(8,128)(2,1)S(1)} %slice_bitcast_fusion), channel_id=1, source_target_pairs={{0,8},{1,9},{16,24},{17,25},{32,40},{33,41},{48,56},{49,57},{64,72... | collective-permute-start | bytes 98312 | tf_op jit(solution)/shard_map/diagonal/ppermute | solution.py:115
  45.4 1.3 %collective-permute-start.3 = (bf16[32,512]{1,0:T(8,128)(2,1)S(1)}, bf16[32,512]{1,0:T(8,128)(2,1)S(1)}, u32[]{:S(2)}, u32[]{:S(2)}) collective-permute-start(bf16[32,512]{1,0:T(8,128)(2,1)S(1)} %slice_bitcast_fusion), channel_id=1, source_target_pairs={{0,12},{1,13},{16,28},{17,29},{32,44},{33,45},{48,60},{49,61},{64,... | collective-permute-start | bytes 98312 | tf_op jit(solution)/shard_map/diagonal/ppermute | solution.py:115
  46.7 1.3 %collective-permute-start.7 = (bf16[512,512]{1,0:T(8,128)(2,1)S(1)}, bf16[512,512]{1,0:T(8,128)(2,1)S(1)}, u32[]{:S(2)}, u32[]{:S(2)}) collective-permute-start(bf16[512,512]{1,0:T(8,128)(2,1)S(1)} %broadcast_select_fusion.2), channel_id=1, source_target_pairs={{0,4},{10,6},{1,13},{7,11},{16,20},{26,22},{17,29},{23,27},{32,36}... | collective-permute-start | bytes 1572872 | tf_op jit(solution)/shard_map/panels/ppermute | solution.py:100
  48.0 0.0 collective-permute-done.1
  48.0 0.0 collective-permute-done.2
  48.0 0.0 collective-permute-done.3
  48.1 2.6 %collective-permute-start.4 = (bf16[32,512]{1,0:T(8,128)(2,1)S(1)}, bf16[32,512]{1,0:T(8,128)(2,1)S(1)}, u32[]{:S(2)}, u32[]{:S(2)}) collective-permute-start(bf16[32,512]{1,0:T(8,128)(2,1)S(1)} %add_select_fusion), channel_id=1, source_target_pairs={{0,1},{1,0},{4,5},{5,4},{8,9},{9,8},{12,13},{13,12},{16,17},{17,16... | collective-permute-start | bytes 98312 | tf_op jit(solution)/shard_map/diagonal/ppermute | solution.py:119
  50.7 1.3 %collective-permute-start.5 = (bf16[32,512]{1,0:T(8,128)(2,1)S(1)}, bf16[32,512]{1,0:T(8,128)(2,1)S(1)}, u32[]{:S(2)}, u32[]{:S(2)}) collective-permute-start(bf16[32,512]{1,0:T(8,128)(2,1)S(1)} %add_select_fusion), channel_id=1, source_target_pairs={{0,2},{1,3},{4,6},{5,7},{8,10},{9,11},{12,14},{13,15},{16,18},{17,... | collective-permute-start | bytes 98312 | tf_op jit(solution)/shard_map/diagonal/ppermute | solution.py:120
  52.0 1.3 %collective-permute-start.6 = (bf16[32,512]{1,0:T(8,128)(2,1)S(1)}, bf16[32,512]{1,0:T(8,128)(2,1)S(1)}, u32[]{:S(2)}, u32[]{:S(2)}) collective-permute-start(bf16[32,512]{1,0:T(8,128)(2,1)S(1)} %add_select_fusion), channel_id=1, source_target_pairs={{0,3},{1,2},{4,7},{5,6},{8,11},{9,10},{12,15},{13,14},{16,19},{17,... | collective-permute-start | bytes 98312 | tf_op jit(solution)/shard_map/diagonal/ppermute | solution.py:121
  53.3 6.6 %collective-permute-done.4 = bf16[32,512]{1,0:T(8,128)(2,1)S(1)} collective-permute-done((bf16[32,512]{1,0:T(8,128)(2,1)S(1)}, bf16[32,512]{1,0:T(8,128)(2,1)S(1)}, u32[]{:S(2)}, u32[]{:S(2)}) %collective-permute-start.4) | collective-permute-done | bytes 32800 | tf_op jit(solution)/shard_map/diagonal/ppermute | solution.py:119
  59.9 0.0 collective-permute-done.5
  59.9 0.0 collective-permute-done.6
  60.0 0.0 collective-permute-done.7
  60.0 0.1 broadcast_select_fusion.1
  60.0 0.0 all-to-all-done.1
  60.0 1.1 broadcast_in_dim.15
  61.1 6.2 %all-to-all-start.2 = ((bf16[16,2,32,512]{3,2,1,0:T(8,128)(2,1)}), bf16[16,2,32,512]{3,2,1,0:T(8,128)(2,1)S(1)}, u32[]{:S(2)}, u32[]{:S(2)}) async-start(bf16[16,2,32,512]{3,2,1,0:T(8,128)(2,1)} %broadcast_in_dim.15), calls=%async_computation.2 | async-start | bytes 2097152 | tf_op jit(solution)/shard_map/diagonal/all_to_all | solution.py:138
  67.4 2.8 %collective-permute-start.8 = (bf16[512,512]{1,0:T(8,128)(2,1)S(1)}, bf16[512,512]{1,0:T(8,128)(2,1)}, u32[]{:S(2)}, u32[]{:S(2)}) collective-permute-start(bf16[512,512]{1,0:T(8,128)(2,1)S(1)} %broadcast_select_fusion.1), channel_id=1, source_target_pairs={{0,14},{4,2},{6,8},{10,12},{1,3},{13,15},{11,9},{7,5},{16,30},{20,... | collective-permute-start | bytes 1572872 | tf_op jit(solution)/shard_map/panels/ppermute | solution.py:100
  70.2 15.6 %collective-permute-start.11 = (bf16[512,1024]{1,0:T(8,128)(2,1)}, bf16[512,1024]{1,0:T(8,128)(2,1)}, u32[]{:S(2)}, u32[]{:S(2)}) collective-permute-start(bf16[512,1024]{1,0:T(8,128)(2,1)} %bitcast.5.own_rows), channel_id=1, source_target_pairs={{0,16},{16,0},{32,48},{48,32},{64,80},{80,64},{96,112},{112,96},{1... | collective-permute-start | bytes 3145736 | tf_op jit(solution)/shard_map/gather_rows/ppermute | solution.py:155
  85.8 0.0 collective-permute-done.8
  85.8 0.1 broadcast_select_fusion.held
  85.9 0.0 all-to-all-done.2.own_diag
  85.9 5.9 %collective-permute-start.10 = (bf16[16,2,32,512]{3,2,1,0:T(8,128)(2,1)S(1)}, bf16[16,2,32,512]{3,2,1,0:T(8,128)(2,1)S(1)}, u32[]{:S(2)}, u32[]{:S(2)}) collective-permute-start(bf16[16,2,32,512]{3,2,1,0:T(8,128)(2,1)S(1)} %all-to-all-done.2.own_diag), channel_id=1, source_target_pairs={{0,16},{16,0},{32,48},{48,32},{64,80},{80,64},{96,112},{112,96},{1... | collective-permute-start | bytes 3145736 | tf_op jit(solution)/shard_map/diagonal/ppermute | solution.py:164
  91.7 5.7 %collective-permute-start.9 = (bf16[512,512]{1,0:T(8,128)(2,1)S(1)}, bf16[512,512]{1,0:T(8,128)(2,1)S(1)}, u32[]{:S(2)}, u32[]{:S(2)}) collective-permute-start(bf16[512,512]{1,0:T(8,128)(2,1)S(1)} %broadcast_select_fusion.held), channel_id=1, source_target_pairs={{0,15},{1,2},{2,1},{3,4},{4,3},{5,6},{6,5},{7,8},{8,7},{9,10},{10,... | collective-permute-start | bytes 1572872 | tf_op jit(solution)/shard_map/panels/ppermute | solution.py:108
  97.5 0.2 copy.19
  97.7 0.0 collective-permute-done.11.other_rows
  97.8 0.0 collective-permute-done.10.other_diag
  97.8 6.5 %upper.1 = (bf16[512,512]{1,0:T(8,128)(2,1)S(1)}, bf16[512,512]{1,0:T(8,128)(2,1)S(1)}, bf16[512,512]{1,0:T(8,128)(2,1)S(1)}, bf16[512,1024]{1,0:T(8,128)(2,1)S(1)}, bf16[512,1024]{1,0:T(8,128)(2,1)S(1)}) custom-call(bf16[16,2,32,512]{3,2,1,0:T(8,128)(2,1)S(1)} %all-to-all-done.2.own_diag, bf16[16,2,32,512]{3,2,1,0:T(8,128)(2,1)S(1)} %collective-permute-done.10.other_diag, ...), custom_call_target="tpu_custom_call" | custom-call | tf_op jit(solution)/shard_map/upper/pallas_call | solution.py:167
  104.3 0.0 copy-start
  104.3 1.0 copy-done
  105.2 4.5 %collective-permute-done.9.other = bf16[512,512]{1,0:T(8,128)(2,1)S(1)} collective-permute-done((bf16[512,512]{1,0:T(8,128)(2,1)S(1)}, bf16[512,512]{1,0:T(8,128)(2,1)S(1)}, u32[]{:S(2)}, u32[]{:S(2)}) %collective-permute-start.9) | collective-permute-done | bytes 524320 | tf_op jit(solution)/shard_map/panels/ppermute | solution.py:108
  109.8 4.1 %update.1 = bf16[512,1024]{1,0:T(8,128)(2,1)S(1)} custom-call(bf16[512,512]{1,0:T(8,128)(2,1)S(1)} %broadcast_select_fusion.held, bf16[512,512]{1,0:T(8,128)(2,1)S(1)} %collective-permute-done.9.other, bf16[512,1024]{1,0:T(8,128)(2,1)S(1)} %bitcast.24, bf16[512,512]{1,0:T(8,128)(2,1)S(1)} %get-tuple-element.24.inverse0, ...), custom_call_target="tpu_custom_call" | custom-call | tf_op jit(solution)/shard_map/update/pallas_call | solution.py:171
  113.9 1.6 %reshape.28 = bf16[512,1,2,512]{3,2,0,1:T(2,128)(2,1)} reshape(bf16[512,1024]{1,0:T(8,128)(2,1)S(1)} %update.1) | data formatting | bytes 2097152 | tf_op jit(solution)/shard_map/reshape | solution.py:174
  (7 shorter events, 0.1 us)
Async XLA Ops:
  0.0 7.7 %copy-start.1 = (bf16[512,1,2,512]{3,2,1,0:T(2,128)(2,1)S(1)}, bf16[512,1,2,512]{3,2,1,0:T(2,128)(2,1)}, u32[]{:S(2)}) copy-start(bf16[512,1,2,512]{3,2,1,0:T(2,128)(2,1)} %param.2) | copy-start | bytes 3145732
  0.0 32.8 %all-to-all-start = ((bf16[512,1,2,512]{3,2,1,0:T(2,128)(2,1)}), bf16[512,1,2,512]{3,2,1,0:T(2,128)(2,1)S(1)}, u32[]{:S(2)}, u32[]{:S(2)}) async-start(bf16[512,1,2,512]{3,2,1,0:T(2,128)(2,1)} %param.2), calls=%async_computation | async-start | bytes 2097152 | tf_op jit(solution)/shard_map/scatter_rows/all_to_all | solution.py:143
  7.9 24.8 %collective-permute-start = (bf16[512,512]{1,0:T(8,128)(2,1)S(1)}, bf16[512,512]{1,0:T(8,128)(2,1)S(1)}, u32[]{:S(2)}, u32[]{:S(2)}) collective-permute-start(bf16[512,512]{1,0:T(8,128)(2,1)S(1)} %bitcast.31), channel_id=1, source_target_pairs={{0,10},{1,7},{16,26},{17,23},{32,42},{33,39},{48,58},{49,55},{64,7... | collective-permute-start | bytes 1572872 | tf_op jit(solution)/shard_map/panels/ppermute | solution.py:100
  34.0 26.1 %all-to-all-start.1 = ((bf16[16,32,1024]{2,1,0:T(8,128)(2,1)}), bf16[16,32,1024]{2,1,0:T(8,128)(2,1)}, u32[]{:S(2)}, u32[]{:S(2)}) async-start(bf16[16,32,1024]{2,1,0:T(8,128)(2,1)} %broadcast_in_dim.14), calls=%async_computation.1 | async-start | bytes 2097152 | tf_op jit(solution)/shard_map/gather_rows/all_to_all | solution.py:138
  40.4 7.6 %collective-permute-start.1 = (bf16[32,512]{1,0:T(8,128)(2,1)S(1)}, bf16[32,512]{1,0:T(8,128)(2,1)S(1)}, u32[]{:S(2)}, u32[]{:S(2)}) collective-permute-start(bf16[32,512]{1,0:T(8,128)(2,1)S(1)} %slice_bitcast_fusion), channel_id=1, source_target_pairs={{0,4},{1,5},{16,20},{17,21},{32,36},{33,37},{48,52},{49,53},{64,68... | collective-permute-start | bytes 98312 | tf_op jit(solution)/shard_map/diagonal/ppermute | solution.py:115
  41.7 6.3 %collective-permute-start.2 = (bf16[32,512]{1,0:T(8,128)(2,1)S(1)}, bf16[32,512]{1,0:T(8,128)(2,1)S(1)}, u32[]{:S(2)}, u32[]{:S(2)}) collective-permute-start(bf16[32,512]{1,0:T(8,128)(2,1)S(1)} %slice_bitcast_fusion), channel_id=1, source_target_pairs={{0,8},{1,9},{16,24},{17,25},{32,40},{33,41},{48,56},{49,57},{64,72... | collective-permute-start | bytes 98312 | tf_op jit(solution)/shard_map/diagonal/ppermute | solution.py:115
  45.4 2.7 %collective-permute-start.3 = (bf16[32,512]{1,0:T(8,128)(2,1)S(1)}, bf16[32,512]{1,0:T(8,128)(2,1)S(1)}, u32[]{:S(2)}, u32[]{:S(2)}) collective-permute-start(bf16[32,512]{1,0:T(8,128)(2,1)S(1)} %slice_bitcast_fusion), channel_id=1, source_target_pairs={{0,12},{1,13},{16,28},{17,29},{32,44},{33,45},{48,60},{49,61},{64,... | collective-permute-start | bytes 98312 | tf_op jit(solution)/shard_map/diagonal/ppermute | solution.py:115
  46.7 13.3 %collective-permute-start.7 = (bf16[512,512]{1,0:T(8,128)(2,1)S(1)}, bf16[512,512]{1,0:T(8,128)(2,1)S(1)}, u32[]{:S(2)}, u32[]{:S(2)}) collective-permute-start(bf16[512,512]{1,0:T(8,128)(2,1)S(1)} %broadcast_select_fusion.2), channel_id=1, source_target_pairs={{0,4},{10,6},{1,13},{7,11},{16,20},{26,22},{17,29},{23,27},{32,36}... | collective-permute-start | bytes 1572872 | tf_op jit(solution)/shard_map/panels/ppermute | solution.py:100
  48.1 11.9 %collective-permute-start.4 = (bf16[32,512]{1,0:T(8,128)(2,1)S(1)}, bf16[32,512]{1,0:T(8,128)(2,1)S(1)}, u32[]{:S(2)}, u32[]{:S(2)}) collective-permute-start(bf16[32,512]{1,0:T(8,128)(2,1)S(1)} %add_select_fusion), channel_id=1, source_target_pairs={{0,1},{1,0},{4,5},{5,4},{8,9},{9,8},{12,13},{13,12},{16,17},{17,16... | collective-permute-start | bytes 98312 | tf_op jit(solution)/shard_map/diagonal/ppermute | solution.py:119
  50.7 9.2 %collective-permute-start.5 = (bf16[32,512]{1,0:T(8,128)(2,1)S(1)}, bf16[32,512]{1,0:T(8,128)(2,1)S(1)}, u32[]{:S(2)}, u32[]{:S(2)}) collective-permute-start(bf16[32,512]{1,0:T(8,128)(2,1)S(1)} %add_select_fusion), channel_id=1, source_target_pairs={{0,2},{1,3},{4,6},{5,7},{8,10},{9,11},{12,14},{13,15},{16,18},{17,... | collective-permute-start | bytes 98312 | tf_op jit(solution)/shard_map/diagonal/ppermute | solution.py:120
  52.0 7.9 %collective-permute-start.6 = (bf16[32,512]{1,0:T(8,128)(2,1)S(1)}, bf16[32,512]{1,0:T(8,128)(2,1)S(1)}, u32[]{:S(2)}, u32[]{:S(2)}) collective-permute-start(bf16[32,512]{1,0:T(8,128)(2,1)S(1)} %add_select_fusion), channel_id=1, source_target_pairs={{0,3},{1,2},{4,7},{5,6},{8,11},{9,10},{12,15},{13,14},{16,19},{17,... | collective-permute-start | bytes 98312 | tf_op jit(solution)/shard_map/diagonal/ppermute | solution.py:121
  61.1 24.7 %all-to-all-start.2 = ((bf16[16,2,32,512]{3,2,1,0:T(8,128)(2,1)}), bf16[16,2,32,512]{3,2,1,0:T(8,128)(2,1)S(1)}, u32[]{:S(2)}, u32[]{:S(2)}) async-start(bf16[16,2,32,512]{3,2,1,0:T(8,128)(2,1)} %broadcast_in_dim.15), calls=%async_computation.2 | async-start | bytes 2097152 | tf_op jit(solution)/shard_map/diagonal/all_to_all | solution.py:138
  67.4 18.4 %collective-permute-start.8 = (bf16[512,512]{1,0:T(8,128)(2,1)S(1)}, bf16[512,512]{1,0:T(8,128)(2,1)}, u32[]{:S(2)}, u32[]{:S(2)}) collective-permute-start(bf16[512,512]{1,0:T(8,128)(2,1)S(1)} %broadcast_select_fusion.1), channel_id=1, source_target_pairs={{0,14},{4,2},{6,8},{10,12},{1,3},{13,15},{11,9},{7,5},{16,30},{20,... | collective-permute-start | bytes 1572872 | tf_op jit(solution)/shard_map/panels/ppermute | solution.py:100
  70.2 27.6 %collective-permute-start.11 = (bf16[512,1024]{1,0:T(8,128)(2,1)}, bf16[512,1024]{1,0:T(8,128)(2,1)}, u32[]{:S(2)}, u32[]{:S(2)}) collective-permute-start(bf16[512,1024]{1,0:T(8,128)(2,1)} %bitcast.5.own_rows), channel_id=1, source_target_pairs={{0,16},{16,0},{32,48},{48,32},{64,80},{80,64},{96,112},{112,96},{1... | collective-permute-start | bytes 3145736 | tf_op jit(solution)/shard_map/gather_rows/ppermute | solution.py:155
  85.9 11.9 %collective-permute-start.10 = (bf16[16,2,32,512]{3,2,1,0:T(8,128)(2,1)S(1)}, bf16[16,2,32,512]{3,2,1,0:T(8,128)(2,1)S(1)}, u32[]{:S(2)}, u32[]{:S(2)}) collective-permute-start(bf16[16,2,32,512]{3,2,1,0:T(8,128)(2,1)S(1)} %all-to-all-done.2.own_diag), channel_id=1, source_target_pairs={{0,16},{16,0},{32,48},{48,32},{64,80},{80,64},{96,112},{112,96},{1... | collective-permute-start | bytes 3145736 | tf_op jit(solution)/shard_map/diagonal/ppermute | solution.py:164
  91.7 18.0 %collective-permute-start.9 = (bf16[512,512]{1,0:T(8,128)(2,1)S(1)}, bf16[512,512]{1,0:T(8,128)(2,1)S(1)}, u32[]{:S(2)}, u32[]{:S(2)}) collective-permute-start(bf16[512,512]{1,0:T(8,128)(2,1)S(1)} %broadcast_select_fusion.held), channel_id=1, source_target_pairs={{0,15},{1,2},{2,1},{3,4},{4,3},{5,6},{6,5},{7,8},{8,7},{9,10},{10,... | collective-permute-start | bytes 1572872 | tf_op jit(solution)/shard_map/panels/ppermute | solution.py:108
  104.3 1.0 copy-start

commit v5 on v4

v5 whole, which is shorter than its diff:
```python
import jax
import jax.numpy as jnp
from jax import lax
from jax.experimental import pallas as pl
from jax.experimental.pallas import tpu as pltpu
from jax.sharding import PartitionSpec as P

whole = pl.BlockSpec(memory_space=pltpu.VMEM)
params = pltpu.CompilerParams(vmem_limit_bytes=32 * 1024 * 1024)


def product(left, right):
    return jnp.dot(left, right, preferred_element_type=jnp.float32)


def two_parts(value):
    high = value.astype(jnp.bfloat16)
    return high, (value - high.astype(jnp.float32)).astype(jnp.bfloat16)


def refined_inverse(diagonal, approx):
    size = diagonal.shape[0]
    high, low = two_parts(approx)
    row_ids = lax.broadcasted_iota(jnp.int32, (size, size), 0)
    col_ids = lax.broadcasted_iota(jnp.int32, (size, size), 1)
    twice = jnp.where(row_ids == col_ids, 2.0, 0.0)
    rest_high, rest_low = two_parts(twice - (product(diagonal, high) + product(diagonal, low)))
    small = product(high, rest_low) + product(low, rest_high)
    return (product(high, rest_high) + small).astype(jnp.bfloat16)


def finish_kernel(
    own_diag, other_diag, approx, own_rows, other_rows, held, other, block, out,
    upper0_ref, raw1_ref, panel0_ref, panel1_ref, block_ref, sems,
):
    row, col = lax.axis_index("row"), lax.axis_index("col")
    first, even = row % 2 == 0, col % 2 == 0
    size = out.shape[0]

    def fetch(source, target, index):
        return pltpu.make_async_copy(source, target, sems.at[index])

    @pl.when(first)
    def _():
        fetch(own_rows, upper0_ref, 0).start()
        fetch(other_rows, raw1_ref, 1).start()

    @pl.when(jnp.logical_not(first))
    def _():
        fetch(other_rows, upper0_ref, 0).start()
        fetch(own_rows, raw1_ref, 1).start()

    @pl.when(even)
    def _():
        fetch(held, panel0_ref, 2).start()
        fetch(other, panel1_ref, 3).start()

    @pl.when(jnp.logical_not(even))
    def _():
        fetch(other, panel0_ref, 2).start()
        fetch(held, panel1_ref, 3).start()

    fetch(block, block_ref, 4).start()

    def corner(top, side):
        own, exchanged = own_diag[:, side], other_diag[:, side]
        picked = jnp.where(first, own, exchanged) if top else jnp.where(first, exchanged, own)
        return picked.reshape(size, size)

    inverse0 = refined_inverse(corner(True, 0), approx[0])
    right = corner(True, 1)
    lower10 = product(corner(False, 0), inverse0).astype(jnp.bfloat16)
    upper11 = corner(False, 1).astype(jnp.float32) - product(lower10, right)
    inverse1 = refined_inverse(upper11.astype(jnp.bfloat16), approx[1])
    fetch(own_rows, upper0_ref, 0).wait()
    fetch(own_rows, raw1_ref, 1).wait()
    upper0 = upper0_ref[...]
    upper1 = raw1_ref[...].astype(jnp.float32) - product(lower10, upper0)
    upper1 = upper1.astype(jnp.bfloat16)
    fetch(held, panel0_ref, 2).wait()
    fetch(held, panel1_ref, 3).wait()
    fetch(block, block_ref, 4).wait()
    half = size // 2
    for part in range(2):
        rows = pl.ds(part * half, half)
        lower0 = product(panel0_ref[rows], inverse0).astype(jnp.bfloat16)
        rest = panel1_ref[rows].astype(jnp.float32) - product(lower0, right)
        rest_high, rest_low = two_parts(rest)
        lower1 = product(rest_high, inverse1) + product(rest_low, inverse1)
        lower1 = lower1.astype(jnp.bfloat16)
        used0 = jnp.where(row > 0, lower0, jnp.zeros_like(lower0))
        used1 = jnp.where(row > 1, lower1, jnp.zeros_like(lower1))
        fresh = block_ref[rows].astype(jnp.float32) - product(used0, upper0)
        out[rows] = (fresh - product(used1, upper1)).astype(jnp.bfloat16)

        @pl.when((col == 0) & (row > 0))
        def _():
            out[rows, pl.ds(0, size)] = lower0

        @pl.when((col == 1) & (row > 1))
        def _():
            out[rows, pl.ds(0, size)] = lower1


def panel_step(held, level, cols):
    tree = [[(0, 10)], [(0, 4), (10, 6)], [(0, 14), (4, 2), (6, 8), (10, 12)]][level]
    pairs = tree + [((1 - s) % cols, (1 - t) % cols) for s, t in tree]
    got = lax.ppermute(held, "col", pairs)
    col = lax.axis_index("col")
    arrives = jnp.any(jnp.stack([col == t for _, t in pairs]))
    return jnp.where(arrives, got, held)


def panel_pair(held, cols):
    pairs = [(s, (s - 1) % cols) if s % 2 == 0 else (s, (s + 1) % cols) for s in range(cols)]
    return lax.ppermute(held, "col", pairs)


def deal_rows(block, chips):
    chip, side = lax.axis_index("row") // 2, 4
    lanes = chips // side
    part = block.shape[0] // lanes
    got = [
        lax.ppermute(
            block[k * part : (k + 1) * part], "row", [(c, 2 * side * k + c) for c in range(2)]
        )
        for k in range(1, lanes)
    ]
    quarter = jnp.where(chip // side == 0, block[:part], sum(got[1:], got[0]))
    small = part // side
    got = [
        lax.ppermute(
            quarter[k * small : (k + 1) * small],
            "row",
            [(2 * side * y + c, 2 * (side * y + k) + c) for y in range(lanes) for c in range(2)],
        )
        for k in range(1, side)
    ]
    return jnp.where(chip % side == 0, quarter[:small], sum(got[1:], got[0]))


def spread_far(piece, cols):
    quarter = cols // 4
    got = [
        lax.ppermute(piece, "col", [(0, quarter * k), (1, quarter * k + 1)]) for k in range(1, 4)
    ]
    return jnp.where(lax.axis_index("col") < 2, piece, got[0] + got[1] + got[2])


def spread_near(held, cols):
    groups = range(0, cols, 4)
    swap = lax.ppermute(held, "col", [p for g in groups for p in ((g, g + 1), (g + 1, g))])
    near = lax.ppermute(held, "col", [p for g in groups for p in ((g, g + 2), (g + 1, g + 3))])
    far = lax.ppermute(held, "col", [p for g in groups for p in ((g, g + 3), (g + 1, g + 2))])
    place = lax.axis_index("col") % 4
    first = jnp.where(place == 0, held, jnp.where(place == 1, swap, jnp.where(place == 2, near, far)))
    second = jnp.where(place == 0, swap, jnp.where(place == 1, held, jnp.where(place == 2, far, near)))
    return jnp.stack([first, second])


def local(matrix, inverses):
    rows, cols = lax.axis_size("row"), lax.axis_size("col")
    size = matrix.shape[0]
    chips = rows // 2
    part = size // chips
    same_core = [[2 * chip + core for chip in range(chips)] for core in range(2)]
    swap_core = [(r, r ^ 1) for r in range(rows)]

    def gather_part(piece):
        copies = jnp.broadcast_to(piece[None], (chips,) + piece.shape)
        return lax.all_to_all(copies, "row", 0, 0, tiled=True, axis_index_groups=same_core)

    with jax.named_scope("panels"):
        held = panel_step(matrix[:, 0, 0, :], 0, cols)
    with jax.named_scope("scatter_rows"):
        dealt = lax.all_to_all(
            matrix, "row", 0, 0, tiled=True, axis_index_groups=same_core
        )[:part, 0]
    first_dealt = dealt
    with jax.named_scope("panels"):
        held = panel_step(held, 1, cols)
    dealt, held = lax.optimization_barrier((dealt, held))
    with jax.named_scope("gather_rows"):
        own_rows = gather_part(first_dealt.reshape(part, -1)).reshape(size, -1)
    with jax.named_scope("diagonal"):
        piece = spread_far(dealt[:, 0, :], cols)
    piece, own_rows, held = lax.optimization_barrier((piece, own_rows, held))
    with jax.named_scope("panels"):
        held = panel_step(held, 2, cols)
    with jax.named_scope("diagonal"):
        pieces = spread_near(piece, cols)
    pieces, held = lax.optimization_barrier((pieces, held))
    with jax.named_scope("gather_rows"):
        other_rows = lax.ppermute(own_rows, "row", swap_core)
    with jax.named_scope("diagonal"):
        mine = gather_part(pieces)
    with jax.named_scope("panels"):
        panel = panel_pair(held, cols)
    mine, panel = lax.optimization_barrier((mine, panel))
    late, mine = lax.optimization_barrier((matrix, mine))
    with jax.named_scope("diagonal"):
        other = lax.ppermute(mine, "row", swap_core)
    wide = (size, 2 * size)
    with jax.named_scope("finish"):
        fresh = pl.pallas_call(
            finish_kernel,
            out_shape=jax.ShapeDtypeStruct(wide, jnp.bfloat16),
            in_specs=[whole] * 3 + [pl.BlockSpec(memory_space=pl.ANY)] * 5,
            out_specs=whole,
            scratch_shapes=[pltpu.VMEM(wide, jnp.bfloat16)] * 2
            + [pltpu.VMEM((size, size), jnp.bfloat16)] * 2
            + [pltpu.VMEM(wide, jnp.bfloat16), pltpu.SemaphoreType.DMA((5,))],
            compiler_params=params,
        )(mine, other, inverses, own_rows, other_rows, held, panel, late.reshape(wide))
    return fresh.reshape(matrix.shape)


def solution(mesh):
    return jax.shard_map(
        local,
        mesh=mesh,
        in_specs=(P("row", "col", None, None), P()),
        out_specs=P("row", "col", None, None),
        check_vma=False,
    )
```

time: 116 us -> 111 us (0.957)
  starting transfers between devices: 77.7 us -> 61.5 us
  waiting for transfers between devices: 21.4 us -> 30.8 us
  local copies, waits for them, and re-layouts: 5.17 us -> 9.68 us
  Pallas kernels: 10.6 us -> 7.57 us
    ppermute x1, starting transfers between devices: 15.6 us -> 4.83 us  [local(): other_rows = lax.ppermute(own_rows, 'row', swap_core)]
    all_to_all x1, waiting for transfers between devices: 0.01 us -> 10.5 us  [local(): lax.all_to_all(matrix, 'row', 0, 0, tiled=True, axis_index_groups=same_core)]
    all_to_all x2, waiting for transfers between devices: 0.01 us -> 7.93 us  [gather_part(): lax.all_to_all(copies, 'row', 0, 0, tiled=True, axis_index_groups=same_core)]
    ppermute x3, waiting for transfers between devices: 10.2 us -> 3.76 us  [panel_step(): got = lax.ppermute(held, 'col', pairs)]
    all_to_all x2, starting transfers between devices: 12.7 us -> 7.92 us  [gather_part(): lax.all_to_all(copies, 'row', 0, 0, tiled=True, axis_index_groups=same_core)]
    unnamed x7 -> x16, local copies, waits for them, and re-layouts: 1.34 us -> 5.82 us
    ppermute x1, starting transfers between devices: 5.74 us -> 9.71 us  [panel_pair(): return lax.ppermute(held, 'col', pairs)]
    ppermute x6, waiting for transfers between devices: 6.59 us -> 3.1 us  [the longest x1 2.11 us: spread_near(): lax.ppermute(held, 'col', [p for g in groups for p in ((g, g + 1), (g + 1...]
  transfers between devices with their start and end apart: 15 -> 15, of which waited for: 3 -> 7; matrix products, arithmetic and copies ran while one was open for 1% -> 3% of each run, Pallas kernels for 6% -> 0%
where the time goes in v5:
time: 111 us; the launch traced here: 110 us
  starting transfers between devices  61.5 us (55%)
  waiting for transfers between devices  30.8 us (28%)
  local copies, waits for them, and re-layouts  9.68 us (9%)
  Pallas kernels  7.57 us (7%)
    ppermute x3, starting transfers between devices, panel_step(): got = lax.ppermute(held, 'col', pairs)  18 us
    all_to_all x1, waiting for transfers between devices, local(): lax.all_to_all(matrix, 'row', 0, 0, tiled=True, axis_index_groups=same_core)  10.5 us
    ppermute x1, starting transfers between devices, panel_pair(): return lax.ppermute(held, 'col', pairs)  9.71 us
    all_to_all x2, waiting for transfers between devices, gather_part(): lax.all_to_all(copies, 'row', 0, 0, tiled=True, axis_index_groups=same_core)  7.93 us
    all_to_all x2, starting transfers between devices, gather_part(): lax.all_to_all(copies, 'row', 0, 0, tiled=True, axis_index_groups=same_core)  7.92 us
    pallas_call x1, Pallas kernels, local(): pl.pallas_call(finish_kernel, out_shape=jax.ShapeDtypeStruct(wide, jnp.bf...  7.57 us
    all_to_all x1, starting transfers between devices, local(): lax.all_to_all(matrix, 'row', 0, 0, tiled=True, axis_index_groups=same_core)  6.77 us
    unnamed x16, local copies, waits for them, and re-layouts  5.82 us
  transfers between devices with their start and end apart: 15, of which 7 were waited for; matrix products, arithmetic and copies ran while one was open for 3% of the time, Pallas kernels for 0%

profile of v5, /device:TPU:1, one launch (start us, length us, event | category | flops | bytes accessed | tf_op | source)
XLA Modules:
  0.0 110.2 jit_solution(5459381940083127359)
XLA Ops:
  0.0 0.0 copy-start.5
  0.0 1.4 %copy.25 = bf16[512,1,1,512]{3,0,2,1:T(8,128)(2,1)S(1)} copy(bf16[512,1,1,512]{3,2,1,0:T(2,128)(2,1)} %bitcast.28) | data formatting | bytes 1048576
  1.4 15.4 %collective-permute-start = (bf16[512,512]{1,0:T(8,128)(2,1)S(1)}, bf16[512,512]{1,0:T(8,128)(2,1)S(1)}, u32[]{:S(2)}, u32[]{:S(2)}) collective-permute-start(bf16[512,512]{1,0:T(8,128)(2,1)S(1)} %bitcast.32), channel_id=1, source_target_pairs={{0,10},{1,7},{16,26},{17,23},{32,42},{33,39},{48,58},{49,55},{64,7... | collective-permute-start | bytes 1572872 | tf_op jit(solution)/shard_map/panels/ppermute | solution.py:108
  16.9 6.8 %all-to-all-start = ((bf16[512,1,2,512]{3,2,1,0:T(2,128)(2,1)}), bf16[512,1,2,512]{3,2,1,0:T(2,128)(2,1)S(1)}, u32[]{:S(2)}, u32[]{:S(2)}) async-start(bf16[512,1,2,512]{3,2,1,0:T(2,128)(2,1)} %param.2), calls=%async_computation | async-start | bytes 2097152 | tf_op jit(solution)/shard_map/scatter_rows/all_to_all | solution.py:176
  23.6 3.8 %collective-permute-done = bf16[512,512]{1,0:T(8,128)(2,1)S(1)} collective-permute-done((bf16[512,512]{1,0:T(8,128)(2,1)S(1)}, bf16[512,512]{1,0:T(8,128)(2,1)S(1)}, u32[]{:S(2)}, u32[]{:S(2)}) %collective-permute-start) | collective-permute-done | bytes 524320 | tf_op jit(solution)/shard_map/panels/ppermute | solution.py:108
  27.4 0.0 copy-done.5
  27.4 0.1 broadcast_select_fusion.1
  27.5 1.3 %collective-permute-start.1 = (bf16[512,512]{1,0:T(8,128)(2,1)S(1)}, bf16[512,512]{1,0:T(8,128)(2,1)S(1)}, u32[]{:S(2)}, u32[]{:S(2)}) collective-permute-start(bf16[512,512]{1,0:T(8,128)(2,1)S(1)} %broadcast_select_fusion.1), channel_id=1, source_target_pairs={{0,4},{10,6},{1,13},{7,11},{16,20},{26,22},{17,29},{23,27},{32,36}... | collective-permute-start | bytes 1572872 | tf_op jit(solution)/shard_map/panels/ppermute | solution.py:108
  28.8 10.5 %all-to-all-done = bf16[512,1,2,512]{3,2,1,0:T(2,128)(2,1)S(1)} async-done(((bf16[512,1,2,512]{3,2,1,0:T(2,128)(2,1)}), bf16[512,1,2,512]{3,2,1,0:T(2,128)(2,1)S(1)}, u32[]{:S(2)}, u32[]{:S(2)}) %all-to-all-start) | async-done | bytes 1048608 | tf_op jit(solution)/shard_map/scatter_rows/all_to_all | solution.py:176
  39.4 1.1 broadcast_in_dim.14
  40.5 4.3 %all-to-all-start.1 = ((bf16[16,32,1024]{2,1,0:T(8,128)(2,1)}), bf16[16,32,1024]{2,1,0:T(8,128)(2,1)S(1)}, u32[]{:S(2)}, u32[]{:S(2)}) async-start(bf16[16,32,1024]{2,1,0:T(8,128)(2,1)} %broadcast_in_dim.14), calls=%async_computation.1 | async-start | bytes 2097152 | tf_op jit(solution)/shard_map/gather_rows/all_to_all | solution.py:171
  44.8 0.0 collective-permute-done.1
  44.8 0.1 broadcast_select_fusion.2
  44.9 1.3 %collective-permute-start.4 = (bf16[32,512]{1,0:T(8,128)(2,1)S(1)}, bf16[32,512]{1,0:T(8,128)(2,1)S(1)}, u32[]{:S(2)}, u32[]{:S(2)}) collective-permute-start(bf16[32,512]{1,0:T(8,128)(2,1)S(1)} %slice_bitcast_fusion), channel_id=1, source_target_pairs={{0,12},{1,13},{16,28},{17,29},{32,44},{33,45},{48,60},{49,61},{64,... | collective-permute-start | bytes 98312 | tf_op jit(solution)/shard_map/diagonal/ppermute | solution.py:145
  46.2 1.3 %collective-permute-start.3 = (bf16[32,512]{1,0:T(8,128)(2,1)S(1)}, bf16[32,512]{1,0:T(8,128)(2,1)S(1)}, u32[]{:S(2)}, u32[]{:S(2)}) collective-permute-start(bf16[32,512]{1,0:T(8,128)(2,1)S(1)} %slice_bitcast_fusion), channel_id=1, source_target_pairs={{0,8},{1,9},{16,24},{17,25},{32,40},{33,41},{48,56},{49,57},{64,72... | collective-permute-start | bytes 98312 | tf_op jit(solution)/shard_map/diagonal/ppermute | solution.py:145
  47.5 1.3 %collective-permute-start.2 = (bf16[32,512]{1,0:T(8,128)(2,1)S(1)}, bf16[32,512]{1,0:T(8,128)(2,1)S(1)}, u32[]{:S(2)}, u32[]{:S(2)}) collective-permute-start(bf16[32,512]{1,0:T(8,128)(2,1)S(1)} %slice_bitcast_fusion), channel_id=1, source_target_pairs={{0,4},{1,5},{16,20},{17,21},{32,36},{33,37},{48,52},{49,53},{64,68... | collective-permute-start | bytes 98312 | tf_op jit(solution)/shard_map/diagonal/ppermute | solution.py:145
  48.8 0.0 collective-permute-done.4
  48.8 0.0 collective-permute-done.3
  48.8 1.0 collective-permute-done.2
  49.8 7.9 %all-to-all-done.1 = bf16[16,32,1024]{2,1,0:T(8,128)(2,1)S(1)} async-done(((bf16[16,32,1024]{2,1,0:T(8,128)(2,1)}), bf16[16,32,1024]{2,1,0:T(8,128)(2,1)S(1)}, u32[]{:S(2)}, u32[]{:S(2)}) %all-to-all-start.1) | async-done | bytes 1048608 | tf_op jit(solution)/shard_map/gather_rows/all_to_all | solution.py:171
  57.7 1.3 %collective-permute-start.8 = (bf16[512,512]{1,0:T(8,128)(2,1)S(1)}, bf16[512,512]{1,0:T(8,128)(2,1)S(1)}, u32[]{:S(2)}, u32[]{:S(2)}) collective-permute-start(bf16[512,512]{1,0:T(8,128)(2,1)S(1)} %broadcast_select_fusion.2), channel_id=1, source_target_pairs={{0,14},{4,2},{6,8},{10,12},{1,3},{13,15},{11,9},{7,5},{16,30},{20,... | collective-permute-start | bytes 1572872 | tf_op jit(solution)/shard_map/panels/ppermute | solution.py:108
  59.1 1.3 %collective-permute-start.7 = (bf16[32,512]{1,0:T(8,128)(2,1)S(1)}, bf16[32,512]{1,0:T(8,128)(2,1)S(1)}, u32[]{:S(2)}, u32[]{:S(2)}) collective-permute-start(bf16[32,512]{1,0:T(8,128)(2,1)S(1)} %add_select_fusion), channel_id=1, source_target_pairs={{0,3},{1,2},{4,7},{5,6},{8,11},{9,10},{12,15},{13,14},{16,19},{17,... | collective-permute-start | bytes 98312 | tf_op jit(solution)/shard_map/diagonal/ppermute | solution.py:154
  60.4 1.3 %collective-permute-start.6 = (bf16[32,512]{1,0:T(8,128)(2,1)S(1)}, bf16[32,512]{1,0:T(8,128)(2,1)S(1)}, u32[]{:S(2)}, u32[]{:S(2)}) collective-permute-start(bf16[32,512]{1,0:T(8,128)(2,1)S(1)} %add_select_fusion), channel_id=1, source_target_pairs={{0,2},{1,3},{4,6},{5,7},{8,10},{9,11},{12,14},{13,15},{16,18},{17,... | collective-permute-start | bytes 98312 | tf_op jit(solution)/shard_map/diagonal/ppermute | solution.py:153
  61.7 2.5 %collective-permute-start.5 = (bf16[32,512]{1,0:T(8,128)(2,1)S(1)}, bf16[32,512]{1,0:T(8,128)(2,1)S(1)}, u32[]{:S(2)}, u32[]{:S(2)}) collective-permute-start(bf16[32,512]{1,0:T(8,128)(2,1)S(1)} %add_select_fusion), channel_id=1, source_target_pairs={{0,1},{1,0},{4,5},{5,4},{8,9},{9,8},{12,13},{13,12},{16,17},{17,16... | collective-permute-start | bytes 98312 | tf_op jit(solution)/shard_map/diagonal/ppermute | solution.py:152
  64.2 0.0 collective-permute-done.7
  64.2 0.0 collective-permute-done.6
  64.2 2.1 %collective-permute-done.5 = bf16[32,512]{1,0:T(8,128)(2,1)S(1)} collective-permute-done((bf16[32,512]{1,0:T(8,128)(2,1)S(1)}, bf16[32,512]{1,0:T(8,128)(2,1)S(1)}, u32[]{:S(2)}, u32[]{:S(2)}) %collective-permute-start.5) | collective-permute-done | bytes 32800 | tf_op jit(solution)/shard_map/diagonal/ppermute | solution.py:152
  66.3 0.0 collective-permute-done.8
  66.4 0.1 broadcast_select_fusion.held
  66.4 0.0 copy-start
  66.4 1.1 %broadcast_in_dim.15 = bf16[16,2,32,512]{3,2,1,0:T(8,128)(2,1)} broadcast(bf16[2,32,512]{2,1,0:T(8,128)(2,1)S(1)} %pad_maximum_fusion), dimensions={1,2,3} | broadcast | bytes 1114112 | tf_op jit(solution)/shard_map/diagonal/broadcast_in_dim | solution.py:170
  67.6 3.7 %all-to-all-start.2 = ((bf16[16,2,32,512]{3,2,1,0:T(8,128)(2,1)}), bf16[16,2,32,512]{3,2,1,0:T(8,128)(2,1)S(1)}, u32[]{:S(2)}, u32[]{:S(2)}) async-start(bf16[16,2,32,512]{3,2,1,0:T(8,128)(2,1)} %broadcast_in_dim.15), calls=%async_computation.2 | async-start | bytes 2097152 | tf_op jit(solution)/shard_map/diagonal/all_to_all | solution.py:171
  71.2 9.7 %collective-permute-start.9 = (bf16[512,512]{1,0:T(8,128)(2,1)S(1)}, bf16[512,512]{1,0:T(8,128)(2,1)S(1)}, u32[]{:S(2)}, u32[]{:S(2)}) collective-permute-start(bf16[512,512]{1,0:T(8,128)(2,1)S(1)} %broadcast_select_fusion.held), channel_id=1, source_target_pairs={{0,15},{1,2},{2,1},{3,4},{4,3},{5,6},{6,5},{7,8},{8,7},{9,10},{10,... | collective-permute-start | bytes 1572872 | tf_op jit(solution)/shard_map/panels/ppermute | solution.py:116
  81.0 4.8 %collective-permute-start.11 = (bf16[512,1024]{1,0:T(8,128)(2,1)S(1)}, bf16[512,1024]{1,0:T(8,128)(2,1)}, u32[]{:S(2)}, u32[]{:S(2)}) collective-permute-start(bf16[512,1024]{1,0:T(8,128)(2,1)S(1)} %bitcast.25), channel_id=1, source_target_pairs={{0,16},{16,0},{32,48},{48,32},{64,80},{80,64},{96,112},{112,96},{1... | collective-permute-start | bytes 3145736 | tf_op jit(solution)/shard_map/gather_rows/ppermute | solution.py:194
  85.8 4.7 %collective-permute-done.9.other = bf16[512,512]{1,0:T(8,128)(2,1)S(1)} collective-permute-done((bf16[512,512]{1,0:T(8,128)(2,1)S(1)}, bf16[512,512]{1,0:T(8,128)(2,1)S(1)}, u32[]{:S(2)}, u32[]{:S(2)}) %collective-permute-start.9) | collective-permute-done | bytes 524320 | tf_op jit(solution)/shard_map/panels/ppermute | solution.py:116
  90.5 0.0 copy-start.3
  90.5 0.8 copy-done.3
  91.3 0.0 all-to-all-done.2.own_diag
  91.3 5.3 %collective-permute-start.10 = (bf16[16,2,32,512]{3,2,1,0:T(8,128)(2,1)S(1)}, bf16[16,2,32,512]{3,2,1,0:T(8,128)(2,1)S(1)}, u32[]{:S(2)}, u32[]{:S(2)}) collective-permute-start(bf16[16,2,32,512]{3,2,1,0:T(8,128)(2,1)S(1)} %all-to-all-done.2.own_diag), channel_id=1, source_target_pairs={{0,16},{16,0},{32,48},{48,32},{64,80},{80,64},{96,112},{112,96},{1... | collective-permute-start | bytes 3145736 | tf_op jit(solution)/shard_map/diagonal/ppermute | solution.py:202
  96.7 1.5 %copy.20 = bf16[64,8,2,512]{3,1,2,0:T(8,128)(2,1)S(1)} copy(bf16[64,8,2,512]{3,2,1,0:T(2,128)(2,1)} %bitcast.29) | data formatting | bytes 2097152
  98.1 0.0 copy-done
  98.1 0.0 collective-permute-done.11.other_rows
  98.2 0.8 collective-permute-done.10.other_diag
  98.9 0.0 copy-done.2
  98.9 1.0 copy-done.1
  100.0 1.0 copy-done.4
  101.0 7.6 %finish.1 = bf16[512,1024]{1,0:T(8,128)(2,1)S(1)} custom-call(bf16[16,2,32,512]{3,2,1,0:T(8,128)(2,1)S(1)} %all-to-all-done.2.own_diag, bf16[16,2,32,512]{3,2,1,0:T(8,128)(2,1)S(1)} %collective-permute-done.10.other_diag, f32[2,512,512]{2,1,0:T(8,128)S(1)} %copy-done.2, bf16[512,1024]{1,0:T(8,128)(2,1)S(1)} %bitcast.26, ...), custom_call_target="tpu_custom_call" | custom-call | tf_op jit(solution)/shard_map/finish/pallas_call | solution.py:205
  108.6 1.6 %reshape.27 = bf16[512,1,2,512]{3,2,0,1:T(2,128)(2,1)} reshape(bf16[512,1024]{1,0:T(8,128)(2,1)S(1)} %finish.1) | data formatting | bytes 2097152 | tf_op jit(solution)/shard_map/reshape | solution.py:215
  (10 shorter events, 0.1 us)
Async XLA Ops:
  0.0 27.4 %copy-start.5 = (bf16[512,1,2,512]{3,2,1,0:T(2,128)(2,1)S(1)}, bf16[512,1,2,512]{3,2,1,0:T(2,128)(2,1)}, u32[]{:S(2)}) copy-start(bf16[512,1,2,512]{3,2,1,0:T(2,128)(2,1)} %param.2) | copy-start | bytes 3145732
  1.4 26.0 %collective-permute-start = (bf16[512,512]{1,0:T(8,128)(2,1)S(1)}, bf16[512,512]{1,0:T(8,128)(2,1)S(1)}, u32[]{:S(2)}, u32[]{:S(2)}) collective-permute-start(bf16[512,512]{1,0:T(8,128)(2,1)S(1)} %bitcast.32), channel_id=1, source_target_pairs={{0,10},{1,7},{16,26},{17,23},{32,42},{33,39},{48,58},{49,55},{64,7... | collective-permute-start | bytes 1572872 | tf_op jit(solution)/shard_map/panels/ppermute | solution.py:108
  16.9 22.5 %all-to-all-start = ((bf16[512,1,2,512]{3,2,1,0:T(2,128)(2,1)}), bf16[512,1,2,512]{3,2,1,0:T(2,128)(2,1)S(1)}, u32[]{:S(2)}, u32[]{:S(2)}) async-start(bf16[512,1,2,512]{3,2,1,0:T(2,128)(2,1)} %param.2), calls=%async_computation | async-start | bytes 2097152 | tf_op jit(solution)/shard_map/scatter_rows/all_to_all | solution.py:176
  27.5 17.3 %collective-permute-start.1 = (bf16[512,512]{1,0:T(8,128)(2,1)S(1)}, bf16[512,512]{1,0:T(8,128)(2,1)S(1)}, u32[]{:S(2)}, u32[]{:S(2)}) collective-permute-start(bf16[512,512]{1,0:T(8,128)(2,1)S(1)} %broadcast_select_fusion.1), channel_id=1, source_target_pairs={{0,4},{10,6},{1,13},{7,11},{16,20},{26,22},{17,29},{23,27},{32,36}... | collective-permute-start | bytes 1572872 | tf_op jit(solution)/shard_map/panels/ppermute | solution.py:108
  40.5 17.2 %all-to-all-start.1 = ((bf16[16,32,1024]{2,1,0:T(8,128)(2,1)}), bf16[16,32,1024]{2,1,0:T(8,128)(2,1)S(1)}, u32[]{:S(2)}, u32[]{:S(2)}) async-start(bf16[16,32,1024]{2,1,0:T(8,128)(2,1)} %broadcast_in_dim.14), calls=%async_computation.1 | async-start | bytes 2097152 | tf_op jit(solution)/shard_map/gather_rows/all_to_all | solution.py:171
  44.9 3.9 %collective-permute-start.4 = (bf16[32,512]{1,0:T(8,128)(2,1)S(1)}, bf16[32,512]{1,0:T(8,128)(2,1)S(1)}, u32[]{:S(2)}, u32[]{:S(2)}) collective-permute-start(bf16[32,512]{1,0:T(8,128)(2,1)S(1)} %slice_bitcast_fusion), channel_id=1, source_target_pairs={{0,12},{1,13},{16,28},{17,29},{32,44},{33,45},{48,60},{49,61},{64,... | collective-permute-start | bytes 98312 | tf_op jit(solution)/shard_map/diagonal/ppermute | solution.py:145
  46.2 2.6 %collective-permute-start.3 = (bf16[32,512]{1,0:T(8,128)(2,1)S(1)}, bf16[32,512]{1,0:T(8,128)(2,1)S(1)}, u32[]{:S(2)}, u32[]{:S(2)}) collective-permute-start(bf16[32,512]{1,0:T(8,128)(2,1)S(1)} %slice_bitcast_fusion), channel_id=1, source_target_pairs={{0,8},{1,9},{16,24},{17,25},{32,40},{33,41},{48,56},{49,57},{64,72... | collective-permute-start | bytes 98312 | tf_op jit(solution)/shard_map/diagonal/ppermute | solution.py:145
  47.5 2.3 %collective-permute-start.2 = (bf16[32,512]{1,0:T(8,128)(2,1)S(1)}, bf16[32,512]{1,0:T(8,128)(2,1)S(1)}, u32[]{:S(2)}, u32[]{:S(2)}) collective-permute-start(bf16[32,512]{1,0:T(8,128)(2,1)S(1)} %slice_bitcast_fusion), channel_id=1, source_target_pairs={{0,4},{1,5},{16,20},{17,21},{32,36},{33,37},{48,52},{49,53},{64,68... | collective-permute-start | bytes 98312 | tf_op jit(solution)/shard_map/diagonal/ppermute | solution.py:145
  57.7 8.6 %collective-permute-start.8 = (bf16[512,512]{1,0:T(8,128)(2,1)S(1)}, bf16[512,512]{1,0:T(8,128)(2,1)S(1)}, u32[]{:S(2)}, u32[]{:S(2)}) collective-permute-start(bf16[512,512]{1,0:T(8,128)(2,1)S(1)} %broadcast_select_fusion.2), channel_id=1, source_target_pairs={{0,14},{4,2},{6,8},{10,12},{1,3},{13,15},{11,9},{7,5},{16,30},{20,... | collective-permute-start | bytes 1572872 | tf_op jit(solution)/shard_map/panels/ppermute | solution.py:108
  59.1 5.1 %collective-permute-start.7 = (bf16[32,512]{1,0:T(8,128)(2,1)S(1)}, bf16[32,512]{1,0:T(8,128)(2,1)S(1)}, u32[]{:S(2)}, u32[]{:S(2)}) collective-permute-start(bf16[32,512]{1,0:T(8,128)(2,1)S(1)} %add_select_fusion), channel_id=1, source_target_pairs={{0,3},{1,2},{4,7},{5,6},{8,11},{9,10},{12,15},{13,14},{16,19},{17,... | collective-permute-start | bytes 98312 | tf_op jit(solution)/shard_map/diagonal/ppermute | solution.py:154
  60.4 3.8 %collective-permute-start.6 = (bf16[32,512]{1,0:T(8,128)(2,1)S(1)}, bf16[32,512]{1,0:T(8,128)(2,1)S(1)}, u32[]{:S(2)}, u32[]{:S(2)}) collective-permute-start(bf16[32,512]{1,0:T(8,128)(2,1)S(1)} %add_select_fusion), channel_id=1, source_target_pairs={{0,2},{1,3},{4,6},{5,7},{8,10},{9,11},{12,14},{13,15},{16,18},{17,... | collective-permute-start | bytes 98312 | tf_op jit(solution)/shard_map/diagonal/ppermute | solution.py:153
  61.7 4.7 %collective-permute-start.5 = (bf16[32,512]{1,0:T(8,128)(2,1)S(1)}, bf16[32,512]{1,0:T(8,128)(2,1)S(1)}, u32[]{:S(2)}, u32[]{:S(2)}) collective-permute-start(bf16[32,512]{1,0:T(8,128)(2,1)S(1)} %add_select_fusion), channel_id=1, source_target_pairs={{0,1},{1,0},{4,5},{5,4},{8,9},{9,8},{12,13},{13,12},{16,17},{17,16... | collective-permute-start | bytes 98312 | tf_op jit(solution)/shard_map/diagonal/ppermute | solution.py:152
  66.4 31.7 %copy-start = (bf16[512,512]{1,0:T(8,128)(2,1)}, bf16[512,512]{1,0:T(8,128)(2,1)S(1)}, u32[]{:S(2)}) copy-start(bf16[512,512]{1,0:T(8,128)(2,1)S(1)} %broadcast_select_fusion.held) | copy-start | bytes 1572868
  67.6 23.8 %all-to-all-start.2 = ((bf16[16,2,32,512]{3,2,1,0:T(8,128)(2,1)}), bf16[16,2,32,512]{3,2,1,0:T(8,128)(2,1)S(1)}, u32[]{:S(2)}, u32[]{:S(2)}) async-start(bf16[16,2,32,512]{3,2,1,0:T(8,128)(2,1)} %broadcast_in_dim.15), calls=%async_computation.2 | async-start | bytes 2097152 | tf_op jit(solution)/shard_map/diagonal/all_to_all | solution.py:171
  71.2 19.3 %collective-permute-start.9 = (bf16[512,512]{1,0:T(8,128)(2,1)S(1)}, bf16[512,512]{1,0:T(8,128)(2,1)S(1)}, u32[]{:S(2)}, u32[]{:S(2)}) collective-permute-start(bf16[512,512]{1,0:T(8,128)(2,1)S(1)} %broadcast_select_fusion.held), channel_id=1, source_target_pairs={{0,15},{1,2},{2,1},{3,4},{4,3},{5,6},{6,5},{7,8},{8,7},{9,10},{10,... | collective-permute-start | bytes 1572872 | tf_op jit(solution)/shard_map/panels/ppermute | solution.py:116
  81.0 17.2 %collective-permute-start.11 = (bf16[512,1024]{1,0:T(8,128)(2,1)S(1)}, bf16[512,1024]{1,0:T(8,128)(2,1)}, u32[]{:S(2)}, u32[]{:S(2)}) collective-permute-start(bf16[512,1024]{1,0:T(8,128)(2,1)S(1)} %bitcast.25), channel_id=1, source_target_pairs={{0,16},{16,0},{32,48},{48,32},{64,80},{80,64},{96,112},{112,96},{1... | collective-permute-start | bytes 3145736 | tf_op jit(solution)/shard_map/gather_rows/ppermute | solution.py:194
  90.5 0.8 copy-start.3
  91.3 7.6 %copy-start.2 = (f32[2,512,512]{2,1,0:T(8,128)S(1)}, f32[2,512,512]{2,1,0:T(8,128)}, u32[]{:S(2)}) copy-start(f32[2,512,512]{2,1,0:T(8,128)} %approx.1) | copy-start | bytes 6291460
  91.3 7.6 %collective-permute-start.10 = (bf16[16,2,32,512]{3,2,1,0:T(8,128)(2,1)S(1)}, bf16[16,2,32,512]{3,2,1,0:T(8,128)(2,1)S(1)}, u32[]{:S(2)}, u32[]{:S(2)}) collective-permute-start(bf16[16,2,32,512]{3,2,1,0:T(8,128)(2,1)S(1)} %all-to-all-done.2.own_diag), channel_id=1, source_target_pairs={{0,16},{16,0},{32,48},{48,32},{64,80},{80,64},{96,112},{112,96},{1... | collective-permute-start | bytes 3145736 | tf_op jit(solution)/shard_map/diagonal/ppermute | solution.py:202
  98.9 1.0 copy-start.1
  100.0 1.0 copy-start.4

commit v6 on v5

--- a/solution.py
+++ b/solution.py
@@ -103,7 +103,7 @@
 
 
 def panel_step(held, level, cols):
-    tree = [[(0, 10)], [(0, 4), (10, 6)], [(0, 14), (4, 2), (6, 8), (10, 12)]][level]
+    tree = [[(0, 10)], [(0, 12), (10, 4)], [(0, 2), (4, 6), (10, 8), (12, 14)]][level]
     pairs = tree + [((1 - s) % cols, (1 - t) % cols) for s, t in tree]
     got = lax.ppermute(held, "col", pairs)
     col = lax.axis_index("col")
@@ -179,17 +179,16 @@
     first_dealt = dealt
     with jax.named_scope("panels"):
         held = panel_step(held, 1, cols)
-    dealt, held = lax.optimization_barrier((dealt, held))
     with jax.named_scope("gather_rows"):
         own_rows = gather_part(first_dealt.reshape(part, -1)).reshape(size, -1)
     with jax.named_scope("diagonal"):
         piece = spread_far(dealt[:, 0, :], cols)
-    piece, own_rows, held = lax.optimization_barrier((piece, own_rows, held))
+    piece, held = lax.optimization_barrier((piece, held))
     with jax.named_scope("panels"):
         held = panel_step(held, 2, cols)
     with jax.named_scope("diagonal"):
         pieces = spread_near(piece, cols)
-    pieces, held = lax.optimization_barrier((pieces, held))
+    pieces, held, own_rows = lax.optimization_barrier((pieces, held, own_rows))
     with jax.named_scope("gather_rows"):
         other_rows = lax.ppermute(own_rows, "row", swap_core)
     with jax.named_scope("diagonal"):

time: 111 us -> 109 us (0.982)
  waiting for transfers between devices: 30.8 us -> 27.7 us
  starting transfers between devices: 61.5 us -> 64.5 us
  local copies, waits for them, and re-layouts: 9.68 us -> 8.32 us
    all_to_all x1, waiting for transfers between devices: 10.5 us -> 0.01 us  [local(): lax.all_to_all(matrix, 'row', 0, 0, tiled=True, axis_index_groups=same_core)]
    ppermute x3, waiting for transfers between devices: 3.76 us -> 10.2 us  [panel_step(): got = lax.ppermute(held, 'col', pairs)]
    all_to_all x2, waiting for transfers between devices: 7.93 us -> 2.13 us  [gather_part(): lax.all_to_all(copies, 'row', 0, 0, tiled=True, axis_index_groups=same_core)]
    ppermute x1, waiting for transfers between devices: 0.01 us -> 4.56 us  [spread_near(): lax.ppermute(held, 'col', [p for g in groups for p in ((g, g + 3), (g + 1...]
    ppermute x1, waiting for transfers between devices: 4.74 us -> 8.55 us  [panel_pair(): return lax.ppermute(held, 'col', pairs)]
    ppermute x3, starting transfers between devices: 3.87 us -> 6.99 us  [spread_far(): lax.ppermute(piece, 'col', [(0, quarter * k), (1, quarter * k + 1)])]
    ppermute x1, starting transfers between devices: 9.71 us -> 12.4 us  [panel_pair(): return lax.ppermute(held, 'col', pairs)]
    ppermute x1, starting transfers between devices: 5.31 us -> 3.37 us  [local(): other = lax.ppermute(mine, 'row', swap_core)]
where the time goes in v6:
time: 109 us
  starting transfers between devices  64.5 us (59%)
  waiting for transfers between devices  27.7 us (25%)
  local copies, waits for them, and re-layouts  8.32 us (8%)
  Pallas kernels  7.57 us (7%)
    ppermute x3, starting transfers between devices, panel_step(): got = lax.ppermute(held, 'col', pairs)  17.2 us
    ppermute x1, starting transfers between devices, panel_pair(): return lax.ppermute(held, 'col', pairs)  12.4 us
    ppermute x3, waiting for transfers between devices, panel_step(): got = lax.ppermute(held, 'col', pairs)  10.2 us
    all_to_all x2, starting transfers between devices, gather_part(): lax.all_to_all(copies, 'row', 0, 0, tiled=True, axis_index_groups=same_core)  8.56 us
    ppermute x1, waiting for transfers between devices, panel_pair(): return lax.ppermute(held, 'col', pairs)  8.55 us
    all_to_all x1, starting transfers between devices, local(): lax.all_to_all(matrix, 'row', 0, 0, tiled=True, axis_index_groups=same_core)  7.72 us
    pallas_call x1, Pallas kernels, local(): pl.pallas_call(finish_kernel, out_shape=jax.ShapeDtypeStruct(wide, jnp.bf...  7.57 us
    ppermute x3, starting transfers between devices, spread_far(): lax.ppermute(piece, 'col', [(0, quarter * k), (1, quarter * k + 1)])  6.99 us
  transfers between devices with their start and end apart: 15, of which 7 were waited for; matrix products, arithmetic and copies ran while one was open for 3% of the time, Pallas kernels for 0%

profile of v6, /device:TPU:1, one launch (start us, length us, event | category | flops | bytes accessed | tf_op | source)
XLA Modules:
  0.0 108.7 jit_solution(4334443788975616216)
XLA Ops:
  0.0 0.0 copy-start.5
  0.0 7.7 %all-to-all-start = ((bf16[512,1,2,512]{3,2,1,0:T(2,128)(2,1)}), bf16[512,1,2,512]{3,2,1,0:T(2,128)(2,1)S(1)}, u32[]{:S(2)}, u32[]{:S(2)}) async-start(bf16[512,1,2,512]{3,2,1,0:T(2,128)(2,1)} %param.2), calls=%async_computation | async-start | bytes 2097152 | tf_op jit(solution)/shard_map/scatter_rows/all_to_all | solution.py:176
  7.7 0.0 copy-done.5
  7.7 0.1 copy.25
  7.9 14.6 %collective-permute-start.3 = (bf16[512,512]{1,0:T(8,128)(2,1)S(1)}, bf16[512,512]{1,0:T(8,128)(2,1)S(1)}, u32[]{:S(2)}, u32[]{:S(2)}) collective-permute-start(bf16[512,512]{1,0:T(8,128)(2,1)S(1)} %bitcast.32), channel_id=1, source_target_pairs={{0,10},{1,7},{16,26},{17,23},{32,42},{33,39},{48,58},{49,55},{64,7... | collective-permute-start | bytes 1572872 | tf_op jit(solution)/shard_map/panels/ppermute | solution.py:108
  22.5 10.2 %collective-permute-done.3 = bf16[512,512]{1,0:T(8,128)(2,1)S(1)} collective-permute-done((bf16[512,512]{1,0:T(8,128)(2,1)S(1)}, bf16[512,512]{1,0:T(8,128)(2,1)S(1)}, u32[]{:S(2)}, u32[]{:S(2)}) %collective-permute-start.3) | collective-permute-done | bytes 524320 | tf_op jit(solution)/shard_map/panels/ppermute | solution.py:108
  32.7 0.1 broadcast_select_fusion.1
  32.8 1.3 %collective-permute-start.4 = (bf16[512,512]{1,0:T(8,128)(2,1)S(1)}, bf16[512,512]{1,0:T(8,128)(2,1)S(1)}, u32[]{:S(2)}, u32[]{:S(2)}) collective-permute-start(bf16[512,512]{1,0:T(8,128)(2,1)S(1)} %broadcast_select_fusion.1), channel_id=1, source_target_pairs={{0,12},{10,4},{1,5},{7,13},{16,28},{26,20},{17,21},{23,29},{32,44}... | collective-permute-start | bytes 1572872 | tf_op jit(solution)/shard_map/panels/ppermute | solution.py:108
  34.1 0.0 all-to-all-done
  34.2 2.1 %collective-permute-start.2 = (bf16[32,512]{1,0:T(8,128)(2,1)S(1)}, bf16[32,512]{1,0:T(8,128)(2,1)S(1)}, u32[]{:S(2)}, u32[]{:S(2)}) collective-permute-start(bf16[32,512]{1,0:T(8,128)(2,1)S(1)} %slice_bitcast_fusion), channel_id=1, source_target_pairs={{0,12},{1,13},{16,28},{17,29},{32,44},{33,45},{48,60},{49,61},{64,... | collective-permute-start | bytes 98312 | tf_op jit(solution)/shard_map/diagonal/ppermute | solution.py:145
  36.3 3.7 %collective-permute-start.1 = (bf16[32,512]{1,0:T(8,128)(2,1)S(1)}, bf16[32,512]{1,0:T(8,128)(2,1)S(1)}, u32[]{:S(2)}, u32[]{:S(2)}) collective-permute-start(bf16[32,512]{1,0:T(8,128)(2,1)S(1)} %slice_bitcast_fusion), channel_id=1, source_target_pairs={{0,8},{1,9},{16,24},{17,25},{32,40},{33,41},{48,56},{49,57},{64,72... | collective-permute-start | bytes 98312 | tf_op jit(solution)/shard_map/diagonal/ppermute | solution.py:145
  39.9 1.3 %collective-permute-start = (bf16[32,512]{1,0:T(8,128)(2,1)S(1)}, bf16[32,512]{1,0:T(8,128)(2,1)S(1)}, u32[]{:S(2)}, u32[]{:S(2)}) collective-permute-start(bf16[32,512]{1,0:T(8,128)(2,1)S(1)} %slice_bitcast_fusion), channel_id=1, source_target_pairs={{0,4},{1,5},{16,20},{17,21},{32,36},{33,37},{48,52},{49,53},{64,68... | collective-permute-start | bytes 98312 | tf_op jit(solution)/shard_map/diagonal/ppermute | solution.py:145
  41.2 1.1 %broadcast_in_dim.14 = bf16[16,32,1024]{2,1,0:T(8,128)(2,1)} broadcast(bf16[32,1024]{1,0:T(8,128)(2,1)S(1)} %bitcast.33), dimensions={1,2} | broadcast | bytes 1114112 | tf_op jit(solution)/shard_map/gather_rows/broadcast_in_dim | solution.py:170
  42.3 4.2 %all-to-all-start.1 = ((bf16[16,32,1024]{2,1,0:T(8,128)(2,1)}), bf16[16,32,1024]{2,1,0:T(8,128)(2,1)S(1)}, u32[]{:S(2)}, u32[]{:S(2)}) async-start(bf16[16,32,1024]{2,1,0:T(8,128)(2,1)} %broadcast_in_dim.14), calls=%async_computation.1 | async-start | bytes 2097152 | tf_op jit(solution)/shard_map/gather_rows/all_to_all | solution.py:171
  46.5 0.0 collective-permute-done.2
  46.6 0.0 collective-permute-done.1
  46.6 0.0 collective-permute-done
  46.6 0.0 collective-permute-done.4
  46.6 0.1 broadcast_select_fusion.2
  46.7 1.3 %collective-permute-start.8 = (bf16[512,512]{1,0:T(8,128)(2,1)S(1)}, bf16[512,512]{1,0:T(8,128)(2,1)S(1)}, u32[]{:S(2)}, u32[]{:S(2)}) collective-permute-start(bf16[512,512]{1,0:T(8,128)(2,1)S(1)} %broadcast_select_fusion.2), channel_id=1, source_target_pairs={{0,2},{4,6},{10,8},{12,14},{1,15},{13,11},{7,9},{5,3},{16,18},{20,... | collective-permute-start | bytes 1572872 | tf_op jit(solution)/shard_map/panels/ppermute | solution.py:108
  48.0 1.3 %collective-permute-start.7 = (bf16[32,512]{1,0:T(8,128)(2,1)S(1)}, bf16[32,512]{1,0:T(8,128)(2,1)S(1)}, u32[]{:S(2)}, u32[]{:S(2)}) collective-permute-start(bf16[32,512]{1,0:T(8,128)(2,1)S(1)} %add_select_fusion), channel_id=1, source_target_pairs={{0,3},{1,2},{4,7},{5,6},{8,11},{9,10},{12,15},{13,14},{16,19},{17,... | collective-permute-start | bytes 98312 | tf_op jit(solution)/shard_map/diagonal/ppermute | solution.py:154
  49.3 1.3 %collective-permute-start.6 = (bf16[32,512]{1,0:T(8,128)(2,1)S(1)}, bf16[32,512]{1,0:T(8,128)(2,1)S(1)}, u32[]{:S(2)}, u32[]{:S(2)}) collective-permute-start(bf16[32,512]{1,0:T(8,128)(2,1)S(1)} %add_select_fusion), channel_id=1, source_target_pairs={{0,2},{1,3},{4,6},{5,7},{8,10},{9,11},{12,14},{13,15},{16,18},{17,... | collective-permute-start | bytes 98312 | tf_op jit(solution)/shard_map/diagonal/ppermute | solution.py:153
  50.6 2.6 %collective-permute-start.5 = (bf16[32,512]{1,0:T(8,128)(2,1)S(1)}, bf16[32,512]{1,0:T(8,128)(2,1)S(1)}, u32[]{:S(2)}, u32[]{:S(2)}) collective-permute-start(bf16[32,512]{1,0:T(8,128)(2,1)S(1)} %add_select_fusion), channel_id=1, source_target_pairs={{0,1},{1,0},{4,5},{5,4},{8,9},{9,8},{12,13},{13,12},{16,17},{17,16... | collective-permute-start | bytes 98312 | tf_op jit(solution)/shard_map/diagonal/ppermute | solution.py:152
  53.3 4.6 %collective-permute-done.7 = bf16[32,512]{1,0:T(8,128)(2,1)S(1)} collective-permute-done((bf16[32,512]{1,0:T(8,128)(2,1)S(1)}, bf16[32,512]{1,0:T(8,128)(2,1)S(1)}, u32[]{:S(2)}, u32[]{:S(2)}) %collective-permute-start.7) | collective-permute-done | bytes 32800 | tf_op jit(solution)/shard_map/diagonal/ppermute | solution.py:154
  57.9 0.7 collective-permute-done.6
  58.6 0.7 collective-permute-done.5
  59.3 0.0 collective-permute-done.8
  59.3 0.1 broadcast_select_fusion.held
  59.4 0.0 copy-start
  59.4 2.1 %all-to-all-done.1 = bf16[16,32,1024]{2,1,0:T(8,128)(2,1)S(1)} async-done(((bf16[16,32,1024]{2,1,0:T(8,128)(2,1)}), bf16[16,32,1024]{2,1,0:T(8,128)(2,1)S(1)}, u32[]{:S(2)}, u32[]{:S(2)}) %all-to-all-start.1) | async-done | bytes 1048608 | tf_op jit(solution)/shard_map/gather_rows/all_to_all | solution.py:171
  61.5 1.1 %broadcast_in_dim.15 = bf16[16,2,32,512]{3,2,1,0:T(8,128)(2,1)} broadcast(bf16[2,32,512]{2,1,0:T(8,128)(2,1)S(1)} %pad_maximum_fusion), dimensions={1,2,3} | broadcast | bytes 1114112 | tf_op jit(solution)/shard_map/diagonal/broadcast_in_dim | solution.py:170
  62.6 4.4 %all-to-all-start.2 = ((bf16[16,2,32,512]{3,2,1,0:T(8,128)(2,1)}), bf16[16,2,32,512]{3,2,1,0:T(8,128)(2,1)S(1)}, u32[]{:S(2)}, u32[]{:S(2)}) async-start(bf16[16,2,32,512]{3,2,1,0:T(8,128)(2,1)} %broadcast_in_dim.15), calls=%async_computation.2 | async-start | bytes 2097152 | tf_op jit(solution)/shard_map/diagonal/all_to_all | solution.py:171
  67.0 12.4 %collective-permute-start.9 = (bf16[512,512]{1,0:T(8,128)(2,1)S(1)}, bf16[512,512]{1,0:T(8,128)(2,1)S(1)}, u32[]{:S(2)}, u32[]{:S(2)}) collective-permute-start(bf16[512,512]{1,0:T(8,128)(2,1)S(1)} %broadcast_select_fusion.held), channel_id=1, source_target_pairs={{0,15},{1,2},{2,1},{3,4},{4,3},{5,6},{6,5},{7,8},{8,7},{9,10},{10,... | collective-permute-start | bytes 1572872 | tf_op jit(solution)/shard_map/panels/ppermute | solution.py:116
  79.4 3.0 %collective-permute-start.11 = (bf16[512,1024]{1,0:T(8,128)(2,1)S(1)}, bf16[512,1024]{1,0:T(8,128)(2,1)}, u32[]{:S(2)}, u32[]{:S(2)}) collective-permute-start(bf16[512,1024]{1,0:T(8,128)(2,1)S(1)} %bitcast.25), channel_id=1, source_target_pairs={{0,16},{16,0},{32,48},{48,32},{64,80},{80,64},{96,112},{112,96},{1... | collective-permute-start | bytes 3145736 | tf_op jit(solution)/shard_map/gather_rows/ppermute | solution.py:193
  82.4 8.6 %collective-permute-done.9.other = bf16[512,512]{1,0:T(8,128)(2,1)S(1)} collective-permute-done((bf16[512,512]{1,0:T(8,128)(2,1)S(1)}, bf16[512,512]{1,0:T(8,128)(2,1)S(1)}, u32[]{:S(2)}, u32[]{:S(2)}) %collective-permute-start.9) | collective-permute-done | bytes 524320 | tf_op jit(solution)/shard_map/panels/ppermute | solution.py:116
  91.0 0.0 copy-start.3
  91.0 0.8 copy-done.3
  91.8 0.0 all-to-all-done.2.own_diag
  91.8 3.4 %collective-permute-start.10 = (bf16[16,2,32,512]{3,2,1,0:T(8,128)(2,1)S(1)}, bf16[16,2,32,512]{3,2,1,0:T(8,128)(2,1)S(1)}, u32[]{:S(2)}, u32[]{:S(2)}) collective-permute-start(bf16[16,2,32,512]{3,2,1,0:T(8,128)(2,1)S(1)} %all-to-all-done.2.own_diag), channel_id=1, source_target_pairs={{0,16},{16,0},{32,48},{48,32},{64,80},{80,64},{96,112},{112,96},{1... | collective-permute-start | bytes 3145736 | tf_op jit(solution)/shard_map/diagonal/ppermute | solution.py:201
  95.1 1.5 %copy.20 = bf16[64,8,2,512]{3,1,2,0:T(8,128)(2,1)S(1)} copy(bf16[64,8,2,512]{3,2,1,0:T(2,128)(2,1)} %bitcast.28) | data formatting | bytes 2097152
  96.6 0.0 copy-done
  96.6 0.0 collective-permute-done.11.other_rows
  96.6 0.8 collective-permute-done.10.other_diag
  97.4 0.0 copy-done.2
  97.4 1.0 copy-done.1
  98.5 1.0 copy-done.4
  99.5 7.6 %finish.1 = bf16[512,1024]{1,0:T(8,128)(2,1)S(1)} custom-call(bf16[16,2,32,512]{3,2,1,0:T(8,128)(2,1)S(1)} %all-to-all-done.2.own_diag, bf16[16,2,32,512]{3,2,1,0:T(8,128)(2,1)S(1)} %collective-permute-done.10.other_diag, f32[2,512,512]{2,1,0:T(8,128)S(1)} %copy-done.2, bf16[512,1024]{1,0:T(8,128)(2,1)S(1)} %bitcast.26, ...), custom_call_target="tpu_custom_call" | custom-call | tf_op jit(solution)/shard_map/finish/pallas_call | solution.py:204
  107.1 1.6 %reshape.27 = bf16[512,1,2,512]{3,2,0,1:T(2,128)(2,1)} reshape(bf16[512,1024]{1,0:T(8,128)(2,1)S(1)} %finish.1) | data formatting | bytes 2097152 | tf_op jit(solution)/shard_map/reshape | solution.py:214
  (10 shorter events, 0.1 us)
Async XLA Ops:
  0.0 7.7 %copy-start.5 = (bf16[512,1,2,512]{3,2,1,0:T(2,128)(2,1)S(1)}, bf16[512,1,2,512]{3,2,1,0:T(2,128)(2,1)}, u32[]{:S(2)}) copy-start(bf16[512,1,2,512]{3,2,1,0:T(2,128)(2,1)} %param.2) | copy-start | bytes 3145732
  0.0 34.1 %all-to-all-start = ((bf16[512,1,2,512]{3,2,1,0:T(2,128)(2,1)}), bf16[512,1,2,512]{3,2,1,0:T(2,128)(2,1)S(1)}, u32[]{:S(2)}, u32[]{:S(2)}) async-start(bf16[512,1,2,512]{3,2,1,0:T(2,128)(2,1)} %param.2), calls=%async_computation | async-start | bytes 2097152 | tf_op jit(solution)/shard_map/scatter_rows/all_to_all | solution.py:176
  7.9 24.8 %collective-permute-start.3 = (bf16[512,512]{1,0:T(8,128)(2,1)S(1)}, bf16[512,512]{1,0:T(8,128)(2,1)S(1)}, u32[]{:S(2)}, u32[]{:S(2)}) collective-permute-start(bf16[512,512]{1,0:T(8,128)(2,1)S(1)} %bitcast.32), channel_id=1, source_target_pairs={{0,10},{1,7},{16,26},{17,23},{32,42},{33,39},{48,58},{49,55},{64,7... | collective-permute-start | bytes 1572872 | tf_op jit(solution)/shard_map/panels/ppermute | solution.py:108
  32.8 13.8 %collective-permute-start.4 = (bf16[512,512]{1,0:T(8,128)(2,1)S(1)}, bf16[512,512]{1,0:T(8,128)(2,1)S(1)}, u32[]{:S(2)}, u32[]{:S(2)}) collective-permute-start(bf16[512,512]{1,0:T(8,128)(2,1)S(1)} %broadcast_select_fusion.1), channel_id=1, source_target_pairs={{0,12},{10,4},{1,5},{7,13},{16,28},{26,20},{17,21},{23,29},{32,44}... | collective-permute-start | bytes 1572872 | tf_op jit(solution)/shard_map/panels/ppermute | solution.py:108
  34.2 12.4 %collective-permute-start.2 = (bf16[32,512]{1,0:T(8,128)(2,1)S(1)}, bf16[32,512]{1,0:T(8,128)(2,1)S(1)}, u32[]{:S(2)}, u32[]{:S(2)}) collective-permute-start(bf16[32,512]{1,0:T(8,128)(2,1)S(1)} %slice_bitcast_fusion), channel_id=1, source_target_pairs={{0,12},{1,13},{16,28},{17,29},{32,44},{33,45},{48,60},{49,61},{64,... | collective-permute-start | bytes 98312 | tf_op jit(solution)/shard_map/diagonal/ppermute | solution.py:145
  36.3 10.3 %collective-permute-start.1 = (bf16[32,512]{1,0:T(8,128)(2,1)S(1)}, bf16[32,512]{1,0:T(8,128)(2,1)S(1)}, u32[]{:S(2)}, u32[]{:S(2)}) collective-permute-start(bf16[32,512]{1,0:T(8,128)(2,1)S(1)} %slice_bitcast_fusion), channel_id=1, source_target_pairs={{0,8},{1,9},{16,24},{17,25},{32,40},{33,41},{48,56},{49,57},{64,72... | collective-permute-start | bytes 98312 | tf_op jit(solution)/shard_map/diagonal/ppermute | solution.py:145
  39.9 6.7 %collective-permute-start = (bf16[32,512]{1,0:T(8,128)(2,1)S(1)}, bf16[32,512]{1,0:T(8,128)(2,1)S(1)}, u32[]{:S(2)}, u32[]{:S(2)}) collective-permute-start(bf16[32,512]{1,0:T(8,128)(2,1)S(1)} %slice_bitcast_fusion), channel_id=1, source_target_pairs={{0,4},{1,5},{16,20},{17,21},{32,36},{33,37},{48,52},{49,53},{64,68... | collective-permute-start | bytes 98312 | tf_op jit(solution)/shard_map/diagonal/ppermute | solution.py:145
  42.3 19.2 %all-to-all-start.1 = ((bf16[16,32,1024]{2,1,0:T(8,128)(2,1)}), bf16[16,32,1024]{2,1,0:T(8,128)(2,1)S(1)}, u32[]{:S(2)}, u32[]{:S(2)}) async-start(bf16[16,32,1024]{2,1,0:T(8,128)(2,1)} %broadcast_in_dim.14), calls=%async_computation.1 | async-start | bytes 2097152 | tf_op jit(solution)/shard_map/gather_rows/all_to_all | solution.py:171
  46.7 12.6 %collective-permute-start.8 = (bf16[512,512]{1,0:T(8,128)(2,1)S(1)}, bf16[512,512]{1,0:T(8,128)(2,1)S(1)}, u32[]{:S(2)}, u32[]{:S(2)}) collective-permute-start(bf16[512,512]{1,0:T(8,128)(2,1)S(1)} %broadcast_select_fusion.2), channel_id=1, source_target_pairs={{0,2},{4,6},{10,8},{12,14},{1,15},{13,11},{7,9},{5,3},{16,18},{20,... | collective-permute-start | bytes 1572872 | tf_op jit(solution)/shard_map/panels/ppermute | solution.py:108
  48.0 9.9 %collective-permute-start.7 = (bf16[32,512]{1,0:T(8,128)(2,1)S(1)}, bf16[32,512]{1,0:T(8,128)(2,1)S(1)}, u32[]{:S(2)}, u32[]{:S(2)}) collective-permute-start(bf16[32,512]{1,0:T(8,128)(2,1)S(1)} %add_select_fusion), channel_id=1, source_target_pairs={{0,3},{1,2},{4,7},{5,6},{8,11},{9,10},{12,15},{13,14},{16,19},{17,... | collective-permute-start | bytes 98312 | tf_op jit(solution)/shard_map/diagonal/ppermute | solution.py:154
  49.3 9.3 %collective-permute-start.6 = (bf16[32,512]{1,0:T(8,128)(2,1)S(1)}, bf16[32,512]{1,0:T(8,128)(2,1)S(1)}, u32[]{:S(2)}, u32[]{:S(2)}) collective-permute-start(bf16[32,512]{1,0:T(8,128)(2,1)S(1)} %add_select_fusion), channel_id=1, source_target_pairs={{0,2},{1,3},{4,6},{5,7},{8,10},{9,11},{12,14},{13,15},{16,18},{17,... | collective-permute-start | bytes 98312 | tf_op jit(solution)/shard_map/diagonal/ppermute | solution.py:153
  50.6 8.7 %collective-permute-start.5 = (bf16[32,512]{1,0:T(8,128)(2,1)S(1)}, bf16[32,512]{1,0:T(8,128)(2,1)S(1)}, u32[]{:S(2)}, u32[]{:S(2)}) collective-permute-start(bf16[32,512]{1,0:T(8,128)(2,1)S(1)} %add_select_fusion), channel_id=1, source_target_pairs={{0,1},{1,0},{4,5},{5,4},{8,9},{9,8},{12,13},{13,12},{16,17},{17,16... | collective-permute-start | bytes 98312 | tf_op jit(solution)/shard_map/diagonal/ppermute | solution.py:152
  59.4 37.2 %copy-start = (bf16[512,512]{1,0:T(8,128)(2,1)}, bf16[512,512]{1,0:T(8,128)(2,1)S(1)}, u32[]{:S(2)}) copy-start(bf16[512,512]{1,0:T(8,128)(2,1)S(1)} %broadcast_select_fusion.held) | copy-start | bytes 1572868
  62.6 29.2 %all-to-all-start.2 = ((bf16[16,2,32,512]{3,2,1,0:T(8,128)(2,1)}), bf16[16,2,32,512]{3,2,1,0:T(8,128)(2,1)S(1)}, u32[]{:S(2)}, u32[]{:S(2)}) async-start(bf16[16,2,32,512]{3,2,1,0:T(8,128)(2,1)} %broadcast_in_dim.15), calls=%async_computation.2 | async-start | bytes 2097152 | tf_op jit(solution)/shard_map/diagonal/all_to_all | solution.py:171
  67.0 24.0 %collective-permute-start.9 = (bf16[512,512]{1,0:T(8,128)(2,1)S(1)}, bf16[512,512]{1,0:T(8,128)(2,1)S(1)}, u32[]{:S(2)}, u32[]{:S(2)}) collective-permute-start(bf16[512,512]{1,0:T(8,128)(2,1)S(1)} %broadcast_select_fusion.held), channel_id=1, source_target_pairs={{0,15},{1,2},{2,1},{3,4},{4,3},{5,6},{6,5},{7,8},{8,7},{9,10},{10,... | collective-permute-start | bytes 1572872 | tf_op jit(solution)/shard_map/panels/ppermute | solution.py:116
  79.4 17.2 %collective-permute-start.11 = (bf16[512,1024]{1,0:T(8,128)(2,1)S(1)}, bf16[512,1024]{1,0:T(8,128)(2,1)}, u32[]{:S(2)}, u32[]{:S(2)}) collective-permute-start(bf16[512,1024]{1,0:T(8,128)(2,1)S(1)} %bitcast.25), channel_id=1, source_target_pairs={{0,16},{16,0},{32,48},{48,32},{64,80},{80,64},{96,112},{112,96},{1... | collective-permute-start | bytes 3145736 | tf_op jit(solution)/shard_map/gather_rows/ppermute | solution.py:193
  91.0 0.8 copy-start.3
  91.8 5.6 %copy-start.2 = (f32[2,512,512]{2,1,0:T(8,128)S(1)}, f32[2,512,512]{2,1,0:T(8,128)}, u32[]{:S(2)}) copy-start(f32[2,512,512]{2,1,0:T(8,128)} %approx.1) | copy-start | bytes 6291460
  91.8 5.6 %collective-permute-start.10 = (bf16[16,2,32,512]{3,2,1,0:T(8,128)(2,1)S(1)}, bf16[16,2,32,512]{3,2,1,0:T(8,128)(2,1)S(1)}, u32[]{:S(2)}, u32[]{:S(2)}) collective-permute-start(bf16[16,2,32,512]{3,2,1,0:T(8,128)(2,1)S(1)} %all-to-all-done.2.own_diag), channel_id=1, source_target_pairs={{0,16},{16,0},{32,48},{48,32},{64,80},{80,64},{96,112},{112,96},{1... | collective-permute-start | bytes 3145736 | tf_op jit(solution)/shard_map/diagonal/ppermute | solution.py:201
  97.4 1.0 copy-start.1
  98.5 1.0 copy-start.4

commit v7 on v6

--- a/solution.py
+++ b/solution.py
@@ -184,15 +184,15 @@
     with jax.named_scope("diagonal"):
         piece = spread_far(dealt[:, 0, :], cols)
     piece, held = lax.optimization_barrier((piece, held))
-    with jax.named_scope("panels"):
-        held = panel_step(held, 2, cols)
     with jax.named_scope("diagonal"):
         pieces = spread_near(piece, cols)
-    pieces, held, own_rows = lax.optimization_barrier((pieces, held, own_rows))
+    pieces, own_rows = lax.optimization_barrier((pieces, own_rows))
     with jax.named_scope("gather_rows"):
         other_rows = lax.ppermute(own_rows, "row", swap_core)
     with jax.named_scope("diagonal"):
         mine = gather_part(pieces)
+    with jax.named_scope("panels"):
+        held = panel_step(held, 2, cols)
     with jax.named_scope("panels"):
         panel = panel_pair(held, cols)
     mine, panel = lax.optimization_barrier((mine, panel))

time: 109 us -> 104 us (0.954)
  the two profiles are of different devices: /device:TPU:1 before, /device:TPU:259 now
where the time goes in v7:
time: 104 us; the launch traced here: 103 us
  starting transfers between devices  56.2 us (54%)
  waiting for transfers between devices  28.3 us (27%)
  local copies, waits for them, and re-layouts  10.8 us (10%)
  Pallas kernels  7.59 us (7%)
    ppermute x1, starting transfers between devices, local(): other_rows = lax.ppermute(own_rows, 'row', swap_core)  15 us
    all_to_all x1, waiting for transfers between devices, local(): lax.all_to_all(matrix, 'row', 0, 0, tiled=True, axis_index_groups=same_core)  13.3 us
    all_to_all x2, starting transfers between devices, gather_part(): lax.all_to_all(copies, 'row', 0, 0, tiled=True, axis_index_groups=same_core)  11.9 us
    ppermute x3, waiting for transfers between devices, spread_far(): lax.ppermute(piece, 'col', [(0, quarter * k), (1, quarter * k + 1)])  11.4 us
    ppermute x1, starting transfers between devices, local(): other = lax.ppermute(mine, 'row', swap_core)  9.67 us
    pallas_call x1, Pallas kernels, local(): pl.pallas_call(finish_kernel, out_shape=jax.ShapeDtypeStruct(wide, jnp.bf...  7.59 us
    all_to_all x1, starting transfers between devices, local(): lax.all_to_all(matrix, 'row', 0, 0, tiled=True, axis_index_groups=same_core)  7.05 us
    unnamed x20, local copies, waits for them, and re-layouts  6.98 us
  transfers between devices with their start and end apart: 15, of which 4 were waited for; matrix products, arithmetic and copies ran while one was open for 4% of the time, Pallas kernels for 0%

profile of v7, /device:TPU:259, one launch (start us, length us, event | category | flops | bytes accessed | tf_op | source)
XLA Modules:
  0.0 103.5 jit_solution(16508072868968132465)
XLA Ops:
  0.0 7.0 %all-to-all-start = ((bf16[512,1,2,512]{3,2,1,0:T(2,128)(2,1)}), bf16[512,1,2,512]{3,2,1,0:T(2,128)(2,1)S(1)}, u32[]{:S(2)}, u32[]{:S(2)}) async-start(bf16[512,1,2,512]{3,2,1,0:T(2,128)(2,1)} %param.2), calls=%async_computation | async-start | bytes 2097152 | tf_op jit(solution)/shard_map/scatter_rows/all_to_all | solution.py:176
  7.1 0.1 copy.25
  7.2 0.7 collective-permute-start.3
  7.9 0.0 collective-permute-done.3
  7.9 0.1 broadcast_select_fusion.1
  8.0 0.7 collective-permute-start.4
  8.7 13.3 %all-to-all-done = bf16[512,1,2,512]{3,2,1,0:T(2,128)(2,1)S(1)} async-done(((bf16[512,1,2,512]{3,2,1,0:T(2,128)(2,1)}), bf16[512,1,2,512]{3,2,1,0:T(2,128)(2,1)S(1)}, u32[]{:S(2)}, u32[]{:S(2)}) %all-to-all-start) | async-done | bytes 1048608 | tf_op jit(solution)/shard_map/scatter_rows/all_to_all | solution.py:176
  22.1 1.1 %broadcast_in_dim.14 = bf16[16,32,1024]{2,1,0:T(8,128)(2,1)} broadcast(bf16[32,1024]{1,0:T(8,128)(2,1)S(1)} %bitcast.33), dimensions={1,2} | broadcast | bytes 1114112 | tf_op jit(solution)/shard_map/gather_rows/broadcast_in_dim | solution.py:170
  23.1 5.3 %all-to-all-start.1 = ((bf16[16,32,1024]{2,1,0:T(8,128)(2,1)}), bf16[16,32,1024]{2,1,0:T(8,128)(2,1)S(1)}, u32[]{:S(2)}, u32[]{:S(2)}) async-start(bf16[16,32,1024]{2,1,0:T(8,128)(2,1)} %broadcast_in_dim.14), calls=%async_computation.1 | async-start | bytes 2097152 | tf_op jit(solution)/shard_map/gather_rows/all_to_all | solution.py:171
  28.4 0.7 collective-permute-start.2
  29.1 1.3 %collective-permute-start.1 = (bf16[32,512]{1,0:T(8,128)(2,1)S(1)}, bf16[32,512]{1,0:T(8,128)(2,1)S(1)}, u32[]{:S(2)}, u32[]{:S(2)}) collective-permute-start(bf16[32,512]{1,0:T(8,128)(2,1)S(1)} %slice_bitcast_fusion), channel_id=1, source_target_pairs={{0,8},{1,9},{16,24},{17,25},{32,40},{33,41},{48,56},{49,57},{64,72... | collective-permute-start | bytes 98312 | tf_op jit(solution)/shard_map/diagonal/ppermute | solution.py:145
  30.4 0.7 collective-permute-start
  31.1 0.0 collective-permute-done.2
  31.1 11.4 %collective-permute-done.1 = bf16[32,512]{1,0:T(8,128)(2,1)S(1)} collective-permute-done((bf16[32,512]{1,0:T(8,128)(2,1)S(1)}, bf16[32,512]{1,0:T(8,128)(2,1)S(1)}, u32[]{:S(2)}, u32[]{:S(2)}) %collective-permute-start.1) | collective-permute-done | bytes 32800 | tf_op jit(solution)/shard_map/diagonal/ppermute | solution.py:145
  42.5 0.0 collective-permute-done
  42.5 0.0 collective-permute-done.4
  42.5 0.1 broadcast_select_fusion.2
  42.6 1.3 %collective-permute-start.7 = (bf16[32,512]{1,0:T(8,128)(2,1)S(1)}, bf16[32,512]{1,0:T(8,128)(2,1)S(1)}, u32[]{:S(2)}, u32[]{:S(2)}) collective-permute-start(bf16[32,512]{1,0:T(8,128)(2,1)S(1)} %add_select_fusion), channel_id=1, source_target_pairs={{0,3},{1,2},{4,7},{5,6},{8,11},{9,10},{12,15},{13,14},{16,19},{17,... | collective-permute-start | bytes 98312 | tf_op jit(solution)/shard_map/diagonal/ppermute | solution.py:154
  43.9 1.3 %collective-permute-start.6 = (bf16[32,512]{1,0:T(8,128)(2,1)S(1)}, bf16[32,512]{1,0:T(8,128)(2,1)S(1)}, u32[]{:S(2)}, u32[]{:S(2)}) collective-permute-start(bf16[32,512]{1,0:T(8,128)(2,1)S(1)} %add_select_fusion), channel_id=1, source_target_pairs={{0,2},{1,3},{4,6},{5,7},{8,10},{9,11},{12,14},{13,15},{16,18},{17,... | collective-permute-start | bytes 98312 | tf_op jit(solution)/shard_map/diagonal/ppermute | solution.py:153
  45.2 2.8 %collective-permute-start.5 = (bf16[32,512]{1,0:T(8,128)(2,1)S(1)}, bf16[32,512]{1,0:T(8,128)(2,1)S(1)}, u32[]{:S(2)}, u32[]{:S(2)}) collective-permute-start(bf16[32,512]{1,0:T(8,128)(2,1)S(1)} %add_select_fusion), channel_id=1, source_target_pairs={{0,1},{1,0},{4,5},{5,4},{8,9},{9,8},{12,13},{13,12},{16,17},{17,16... | collective-permute-start | bytes 98312 | tf_op jit(solution)/shard_map/diagonal/ppermute | solution.py:152
  48.0 1.3 %collective-permute-start.8 = (bf16[512,512]{1,0:T(8,128)(2,1)S(1)}, bf16[512,512]{1,0:T(8,128)(2,1)S(1)}, u32[]{:S(2)}, u32[]{:S(2)}) collective-permute-start(bf16[512,512]{1,0:T(8,128)(2,1)S(1)} %broadcast_select_fusion.2), channel_id=1, source_target_pairs={{0,2},{4,6},{10,8},{12,14},{1,15},{13,11},{7,9},{5,3},{16,18},{20,... | collective-permute-start | bytes 1572872 | tf_op jit(solution)/shard_map/panels/ppermute | solution.py:108
  49.3 0.0 collective-permute-done.7
  49.3 0.0 collective-permute-done.6
  49.3 0.6 collective-permute-done.5
  49.9 0.0 all-to-all-done.1
  49.9 1.1 %broadcast_in_dim.15 = bf16[16,2,32,512]{3,2,1,0:T(8,128)(2,1)} broadcast(bf16[2,32,512]{2,1,0:T(8,128)(2,1)S(1)} %pad_maximum_fusion), dimensions={1,2,3} | broadcast | bytes 1114112 | tf_op jit(solution)/shard_map/diagonal/broadcast_in_dim | solution.py:170
  51.0 6.7 %all-to-all-start.2 = ((bf16[16,2,32,512]{3,2,1,0:T(8,128)(2,1)}), bf16[16,2,32,512]{3,2,1,0:T(8,128)(2,1)S(1)}, u32[]{:S(2)}, u32[]{:S(2)}) async-start(bf16[16,2,32,512]{3,2,1,0:T(8,128)(2,1)} %broadcast_in_dim.15), calls=%async_computation.2 | async-start | bytes 2097152 | tf_op jit(solution)/shard_map/diagonal/all_to_all | solution.py:171
  57.6 3.1 %collective-permute-done.8 = bf16[512,512]{1,0:T(8,128)(2,1)S(1)} collective-permute-done((bf16[512,512]{1,0:T(8,128)(2,1)S(1)}, bf16[512,512]{1,0:T(8,128)(2,1)S(1)}, u32[]{:S(2)}, u32[]{:S(2)}) %collective-permute-start.8) | collective-permute-done | bytes 524320 | tf_op jit(solution)/shard_map/panels/ppermute | solution.py:108
  60.7 0.1 broadcast_select_fusion.held
  60.7 2.0 %collective-permute-start.9 = (bf16[512,512]{1,0:T(8,128)(2,1)S(1)}, bf16[512,512]{1,0:T(8,128)(2,1)S(1)}, u32[]{:S(2)}, u32[]{:S(2)}) collective-permute-start(bf16[512,512]{1,0:T(8,128)(2,1)S(1)} %broadcast_select_fusion.held), channel_id=1, source_target_pairs={{0,15},{1,2},{2,1},{3,4},{4,3},{5,6},{6,5},{7,8},{8,7},{9,10},{10,... | collective-permute-start | bytes 1572872 | tf_op jit(solution)/shard_map/panels/ppermute | solution.py:116
  62.7 0.8 copy-done
  63.5 15.0 %collective-permute-start.11 = (bf16[512,1024]{1,0:T(8,128)(2,1)S(1)}, bf16[512,1024]{1,0:T(8,128)(2,1)S(1)}, u32[]{:S(2)}, u32[]{:S(2)}) collective-permute-start(bf16[512,1024]{1,0:T(8,128)(2,1)S(1)} %bitcast.25), channel_id=1, source_target_pairs={{0,16},{16,0},{32,48},{48,32},{64,80},{80,64},{96,112},{112,96},{1... | collective-permute-start | bytes 3145736 | tf_op jit(solution)/shard_map/gather_rows/ppermute | solution.py:191
  78.5 0.0 collective-permute-done.9.other
  78.5 0.0 copy-start.5
  78.5 0.8 copy-done.5
  79.3 0.0 all-to-all-done.2.own_diag
  79.3 9.7 %collective-permute-start.10 = (bf16[16,2,32,512]{3,2,1,0:T(8,128)(2,1)S(1)}, bf16[16,2,32,512]{3,2,1,0:T(8,128)(2,1)S(1)}, u32[]{:S(2)}, u32[]{:S(2)}) collective-permute-start(bf16[16,2,32,512]{3,2,1,0:T(8,128)(2,1)S(1)} %all-to-all-done.2.own_diag), channel_id=1, source_target_pairs={{0,16},{16,0},{32,48},{48,32},{64,80},{80,64},{96,112},{112,96},{1... | collective-permute-start | bytes 3145736 | tf_op jit(solution)/shard_map/diagonal/ppermute | solution.py:201
  89.0 1.5 %copy.20 = bf16[64,8,2,512]{3,1,2,0:T(8,128)(2,1)S(1)} copy(bf16[64,8,2,512]{3,2,1,0:T(2,128)(2,1)} %bitcast.28) | data formatting | bytes 2097152
  90.5 0.0 collective-permute-done.11.other_rows
  90.5 0.0 copy-start.3
  90.5 1.0 copy-done.3
  91.5 0.0 collective-permute-done.10.other_diag
  91.5 0.0 copy-done.1
  91.5 0.0 copy-start.2
  91.5 1.6 %copy-done.2 = f32[2,512,512]{2,1,0:T(8,128)S(1)} copy-done((f32[2,512,512]{2,1,0:T(8,128)S(1)}, f32[2,512,512]{2,1,0:T(8,128)}, u32[]{:S(2)}) %copy-start.2) | copy-done | bytes 2097176
  93.1 1.2 %copy-done.4 = bf16[512,1024]{1,0:T(8,128)(2,1)S(1)} copy-done((bf16[512,1024]{1,0:T(8,128)(2,1)S(1)}, bf16[512,1024]{1,0:T(8,128)(2,1)}, u32[]{:S(2)}) %copy-start.4) | copy-done | bytes 1048600
  94.3 7.6 %finish.1 = bf16[512,1024]{1,0:T(8,128)(2,1)S(1)} custom-call(bf16[16,2,32,512]{3,2,1,0:T(8,128)(2,1)S(1)} %all-to-all-done.2.own_diag, bf16[16,2,32,512]{3,2,1,0:T(8,128)(2,1)S(1)} %collective-permute-done.10.other_diag, f32[2,512,512]{2,1,0:T(8,128)S(1)} %copy-done.2, bf16[512,1024]{1,0:T(8,128)(2,1)S(1)} %bitcast.26, bf16[512,1024]{1,0:T(8,128)(2,1)S(1)} %copy-done.4, ...), custom_call_target="tpu_custom_call" | custom-call | tf_op jit(solution)/shard_map/finish/pallas_call | solution.py:204
  101.9 1.6 %reshape.27 = bf16[512,1,2,512]{3,2,0,1:T(2,128)(2,1)} reshape(bf16[512,1024]{1,0:T(8,128)(2,1)S(1)} %finish.1) | data formatting | bytes 2097152 | tf_op jit(solution)/shard_map/reshape | solution.py:214
  (14 shorter events, 0.1 us)
Async XLA Ops:
  0.0 7.1 %copy-start.7 = (bf16[512,1,2,512]{3,2,1,0:T(2,128)(2,1)S(1)}, bf16[512,1,2,512]{3,2,1,0:T(2,128)(2,1)}, u32[]{:S(2)}) copy-start(bf16[512,1,2,512]{3,2,1,0:T(2,128)(2,1)} %param.2) | copy-start | bytes 3145732
  0.0 22.0 %all-to-all-start = ((bf16[512,1,2,512]{3,2,1,0:T(2,128)(2,1)}), bf16[512,1,2,512]{3,2,1,0:T(2,128)(2,1)S(1)}, u32[]{:S(2)}, u32[]{:S(2)}) async-start(bf16[512,1,2,512]{3,2,1,0:T(2,128)(2,1)} %param.2), calls=%async_computation | async-start | bytes 2097152 | tf_op jit(solution)/shard_map/scatter_rows/all_to_all | solution.py:176
  7.2 0.7 collective-permute-start.3
  8.0 34.5 %collective-permute-start.4 = (bf16[512,512]{1,0:T(8,128)(2,1)S(1)}, bf16[512,512]{1,0:T(8,128)(2,1)S(1)}, u32[]{:S(2)}, u32[]{:S(2)}) collective-permute-start(bf16[512,512]{1,0:T(8,128)(2,1)S(1)} %broadcast_select_fusion.1), channel_id=1, source_target_pairs={{0,12},{10,4},{1,5},{7,13},{16,28},{26,20},{17,21},{23,29},{32,44}... | collective-permute-start | bytes 1572872 | tf_op jit(solution)/shard_map/panels/ppermute | solution.py:108
  23.1 26.7 %all-to-all-start.1 = ((bf16[16,32,1024]{2,1,0:T(8,128)(2,1)}), bf16[16,32,1024]{2,1,0:T(8,128)(2,1)S(1)}, u32[]{:S(2)}, u32[]{:S(2)}) async-start(bf16[16,32,1024]{2,1,0:T(8,128)(2,1)} %broadcast_in_dim.14), calls=%async_computation.1 | async-start | bytes 2097152 | tf_op jit(solution)/shard_map/gather_rows/all_to_all | solution.py:171
  28.4 2.7 %collective-permute-start.2 = (bf16[32,512]{1,0:T(8,128)(2,1)S(1)}, bf16[32,512]{1,0:T(8,128)(2,1)S(1)}, u32[]{:S(2)}, u32[]{:S(2)}) collective-permute-start(bf16[32,512]{1,0:T(8,128)(2,1)S(1)} %slice_bitcast_fusion), channel_id=1, source_target_pairs={{0,12},{1,13},{16,28},{17,29},{32,44},{33,45},{48,60},{49,61},{64,... | collective-permute-start | bytes 98312 | tf_op jit(solution)/shard_map/diagonal/ppermute | solution.py:145
  29.1 13.4 %collective-permute-start.1 = (bf16[32,512]{1,0:T(8,128)(2,1)S(1)}, bf16[32,512]{1,0:T(8,128)(2,1)S(1)}, u32[]{:S(2)}, u32[]{:S(2)}) collective-permute-start(bf16[32,512]{1,0:T(8,128)(2,1)S(1)} %slice_bitcast_fusion), channel_id=1, source_target_pairs={{0,8},{1,9},{16,24},{17,25},{32,40},{33,41},{48,56},{49,57},{64,72... | collective-permute-start | bytes 98312 | tf_op jit(solution)/shard_map/diagonal/ppermute | solution.py:145
  30.4 12.1 %collective-permute-start = (bf16[32,512]{1,0:T(8,128)(2,1)S(1)}, bf16[32,512]{1,0:T(8,128)(2,1)S(1)}, u32[]{:S(2)}, u32[]{:S(2)}) collective-permute-start(bf16[32,512]{1,0:T(8,128)(2,1)S(1)} %slice_bitcast_fusion), channel_id=1, source_target_pairs={{0,4},{1,5},{16,20},{17,21},{32,36},{33,37},{48,52},{49,53},{64,68... | collective-permute-start | bytes 98312 | tf_op jit(solution)/shard_map/diagonal/ppermute | solution.py:145
  42.6 6.7 %collective-permute-start.7 = (bf16[32,512]{1,0:T(8,128)(2,1)S(1)}, bf16[32,512]{1,0:T(8,128)(2,1)S(1)}, u32[]{:S(2)}, u32[]{:S(2)}) collective-permute-start(bf16[32,512]{1,0:T(8,128)(2,1)S(1)} %add_select_fusion), channel_id=1, source_target_pairs={{0,3},{1,2},{4,7},{5,6},{8,11},{9,10},{12,15},{13,14},{16,19},{17,... | collective-permute-start | bytes 98312 | tf_op jit(solution)/shard_map/diagonal/ppermute | solution.py:154
  43.9 5.4 %collective-permute-start.6 = (bf16[32,512]{1,0:T(8,128)(2,1)S(1)}, bf16[32,512]{1,0:T(8,128)(2,1)S(1)}, u32[]{:S(2)}, u32[]{:S(2)}) collective-permute-start(bf16[32,512]{1,0:T(8,128)(2,1)S(1)} %add_select_fusion), channel_id=1, source_target_pairs={{0,2},{1,3},{4,6},{5,7},{8,10},{9,11},{12,14},{13,15},{16,18},{17,... | collective-permute-start | bytes 98312 | tf_op jit(solution)/shard_map/diagonal/ppermute | solution.py:153
  45.2 4.7 %collective-permute-start.5 = (bf16[32,512]{1,0:T(8,128)(2,1)S(1)}, bf16[32,512]{1,0:T(8,128)(2,1)S(1)}, u32[]{:S(2)}, u32[]{:S(2)}) collective-permute-start(bf16[32,512]{1,0:T(8,128)(2,1)S(1)} %add_select_fusion), channel_id=1, source_target_pairs={{0,1},{1,0},{4,5},{5,4},{8,9},{9,8},{12,13},{13,12},{16,17},{17,16... | collective-permute-start | bytes 98312 | tf_op jit(solution)/shard_map/diagonal/ppermute | solution.py:152
  48.0 12.7 %collective-permute-start.8 = (bf16[512,512]{1,0:T(8,128)(2,1)S(1)}, bf16[512,512]{1,0:T(8,128)(2,1)S(1)}, u32[]{:S(2)}, u32[]{:S(2)}) collective-permute-start(bf16[512,512]{1,0:T(8,128)(2,1)S(1)} %broadcast_select_fusion.2), channel_id=1, source_target_pairs={{0,2},{4,6},{10,8},{12,14},{1,15},{13,11},{7,9},{5,3},{16,18},{20,... | collective-permute-start | bytes 1572872 | tf_op jit(solution)/shard_map/panels/ppermute | solution.py:108
  51.0 28.3 %all-to-all-start.2 = ((bf16[16,2,32,512]{3,2,1,0:T(8,128)(2,1)}), bf16[16,2,32,512]{3,2,1,0:T(8,128)(2,1)S(1)}, u32[]{:S(2)}, u32[]{:S(2)}) async-start(bf16[16,2,32,512]{3,2,1,0:T(8,128)(2,1)} %broadcast_in_dim.15), calls=%async_computation.2 | async-start | bytes 2097152 | tf_op jit(solution)/shard_map/diagonal/all_to_all | solution.py:171
  60.7 17.8 %collective-permute-start.9 = (bf16[512,512]{1,0:T(8,128)(2,1)S(1)}, bf16[512,512]{1,0:T(8,128)(2,1)S(1)}, u32[]{:S(2)}, u32[]{:S(2)}) collective-permute-start(bf16[512,512]{1,0:T(8,128)(2,1)S(1)} %broadcast_select_fusion.held), channel_id=1, source_target_pairs={{0,15},{1,2},{2,1},{3,4},{4,3},{5,6},{6,5},{7,8},{8,7},{9,10},{10,... | collective-permute-start | bytes 1572872 | tf_op jit(solution)/shard_map/panels/ppermute | solution.py:116
  62.7 0.8 copy-start
  63.5 26.9 %collective-permute-start.11 = (bf16[512,1024]{1,0:T(8,128)(2,1)S(1)}, bf16[512,1024]{1,0:T(8,128)(2,1)S(1)}, u32[]{:S(2)}, u32[]{:S(2)}) collective-permute-start(bf16[512,1024]{1,0:T(8,128)(2,1)S(1)} %bitcast.25), channel_id=1, source_target_pairs={{0,16},{16,0},{32,48},{48,32},{64,80},{80,64},{96,112},{112,96},{1... | collective-permute-start | bytes 3145736 | tf_op jit(solution)/shard_map/gather_rows/ppermute | solution.py:191
  78.5 0.8 copy-start.5
  79.3 12.1 %copy-start.1 = (bf16[512,512]{1,0:T(8,128)(2,1)S(1)}, bf16[512,512]{1,0:T(8,128)(2,1)}, u32[]{:S(2)}) copy-start(bf16[512,512]{1,0:T(8,128)(2,1)} %copy-done) | copy-start | bytes 1572868
  79.3 12.1 %copy-start.6 = (bf16[512,512]{1,0:T(8,128)(2,1)S(1)}, bf16[512,512]{1,0:T(8,128)(2,1)}, u32[]{:S(2)}) copy-start(bf16[512,512]{1,0:T(8,128)(2,1)} %copy-done.5) | copy-start | bytes 1572868
  79.3 12.1 %collective-permute-start.10 = (bf16[16,2,32,512]{3,2,1,0:T(8,128)(2,1)S(1)}, bf16[16,2,32,512]{3,2,1,0:T(8,128)(2,1)S(1)}, u32[]{:S(2)}, u32[]{:S(2)}) collective-permute-start(bf16[16,2,32,512]{3,2,1,0:T(8,128)(2,1)S(1)} %all-to-all-done.2.own_diag), channel_id=1, source_target_pairs={{0,16},{16,0},{32,48},{48,32},{64,80},{80,64},{96,112},{112,96},{1... | collective-permute-start | bytes 3145736 | tf_op jit(solution)/shard_map/diagonal/ppermute | solution.py:201
  90.5 1.0 copy-start.3
  91.5 1.6 %copy-start.2 = (f32[2,512,512]{2,1,0:T(8,128)S(1)}, f32[2,512,512]{2,1,0:T(8,128)}, u32[]{:S(2)}) copy-start(f32[2,512,512]{2,1,0:T(8,128)} %approx.1) | copy-start | bytes 6291460
  93.1 1.2 %copy-start.4 = (bf16[512,1024]{1,0:T(8,128)(2,1)S(1)}, bf16[512,1024]{1,0:T(8,128)(2,1)}, u32[]{:S(2)}) copy-start(bf16[512,1024]{1,0:T(8,128)(2,1)} %copy-done.3) | copy-start | bytes 3145732

commit v8 on v7

--- a/solution.py
+++ b/solution.py
@@ -183,10 +183,9 @@
         own_rows = gather_part(first_dealt.reshape(part, -1)).reshape(size, -1)
     with jax.named_scope("diagonal"):
         piece = spread_far(dealt[:, 0, :], cols)
-    piece, held = lax.optimization_barrier((piece, held))
     with jax.named_scope("diagonal"):
         pieces = spread_near(piece, cols)
-    pieces, own_rows = lax.optimization_barrier((pieces, own_rows))
+    pieces, own_rows, held = lax.optimization_barrier((pieces, own_rows, held))
     with jax.named_scope("gather_rows"):
         other_rows = lax.ppermute(own_rows, "row", swap_core)
     with jax.named_scope("diagonal"):

time: 104 us -> 103 us (level)
  the two profiles are of different devices: /device:TPU:259 before, /device:TPU:1 now
where the time goes in v8:
time: 103 us; the launch traced here: 102 us
  starting transfers between devices  64.9 us (63%)
  waiting for transfers between devices  21.4 us (21%)
  Pallas kernels  7.57 us (7%)
  local copies, waits for them, and re-layouts  7.52 us (7%)
    ppermute x3, starting transfers between devices, panel_step(): got = lax.ppermute(held, 'col', pairs)  18.8 us
    ppermute x3, waiting for transfers between devices, panel_step(): got = lax.ppermute(held, 'col', pairs)  11.9 us
    all_to_all x2, starting transfers between devices, gather_part(): lax.all_to_all(copies, 'row', 0, 0, tiled=True, axis_index_groups=same_core)  10.7 us
    all_to_all x1, starting transfers between devices, local(): lax.all_to_all(matrix, 'row', 0, 0, tiled=True, axis_index_groups=same_core)  7.72 us
    pallas_call x1, Pallas kernels, local(): pl.pallas_call(finish_kernel, out_shape=jax.ShapeDtypeStruct(wide, jnp.bf...  7.57 us
    ppermute x1, starting transfers between devices, panel_pair(): return lax.ppermute(held, 'col', pairs)  6.9 us
    ppermute x1, starting transfers between devices, local(): other = lax.ppermute(mine, 'row', swap_core)  5.91 us
    ppermute x1, starting transfers between devices, local(): other_rows = lax.ppermute(own_rows, 'row', swap_core)  5.56 us
  transfers between devices with their start and end apart: 15, of which 7 were waited for; matrix products, arithmetic and copies ran while one was open for 4% of the time, Pallas kernels for 0%

profile of v8, /device:TPU:1, one launch (start us, length us, event | category | flops | bytes accessed | tf_op | source)
XLA Modules:
  0.0 102.0 jit_solution(11931401715139764654)
XLA Ops:
  0.0 0.0 copy-start.5
  0.0 7.7 %all-to-all-start = ((bf16[512,1,2,512]{3,2,1,0:T(2,128)(2,1)}), bf16[512,1,2,512]{3,2,1,0:T(2,128)(2,1)S(1)}, u32[]{:S(2)}, u32[]{:S(2)}) async-start(bf16[512,1,2,512]{3,2,1,0:T(2,128)(2,1)} %param.2), calls=%async_computation | async-start | bytes 2097152 | tf_op jit(solution)/shard_map/scatter_rows/all_to_all | solution.py:176
  7.7 0.0 copy-done.5
  7.7 0.1 copy.25
  7.9 14.6 %collective-permute-start.6 = (bf16[512,512]{1,0:T(8,128)(2,1)S(1)}, bf16[512,512]{1,0:T(8,128)(2,1)S(1)}, u32[]{:S(2)}, u32[]{:S(2)}) collective-permute-start(bf16[512,512]{1,0:T(8,128)(2,1)S(1)} %bitcast.32), channel_id=1, source_target_pairs={{0,10},{1,7},{16,26},{17,23},{32,42},{33,39},{48,58},{49,55},{64,7... | collective-permute-start | bytes 1572872 | tf_op jit(solution)/shard_map/panels/ppermute | solution.py:108
  22.5 10.2 %collective-permute-done.6 = bf16[512,512]{1,0:T(8,128)(2,1)S(1)} collective-permute-done((bf16[512,512]{1,0:T(8,128)(2,1)S(1)}, bf16[512,512]{1,0:T(8,128)(2,1)S(1)}, u32[]{:S(2)}, u32[]{:S(2)}) %collective-permute-start.6) | collective-permute-done | bytes 524320 | tf_op jit(solution)/shard_map/panels/ppermute | solution.py:108
  32.7 0.1 broadcast_select_fusion.1
  32.8 2.1 %collective-permute-start.7 = (bf16[512,512]{1,0:T(8,128)(2,1)S(1)}, bf16[512,512]{1,0:T(8,128)(2,1)}, u32[]{:S(2)}, u32[]{:S(2)}) collective-permute-start(bf16[512,512]{1,0:T(8,128)(2,1)S(1)} %broadcast_select_fusion.1), channel_id=1, source_target_pairs={{0,12},{10,4},{1,5},{7,13},{16,28},{26,20},{17,21},{23,29},{32,44}... | collective-permute-start | bytes 1572872 | tf_op jit(solution)/shard_map/panels/ppermute | solution.py:108
  34.9 0.0 all-to-all-done
  35.0 1.1 %broadcast_in_dim.14 = bf16[16,32,1024]{2,1,0:T(8,128)(2,1)} broadcast(bf16[32,1024]{1,0:T(8,128)(2,1)S(1)} %bitcast.33), dimensions={1,2} | broadcast | bytes 1114112 | tf_op jit(solution)/shard_map/gather_rows/broadcast_in_dim | solution.py:170
  36.1 6.4 %all-to-all-start.1 = ((bf16[16,32,1024]{2,1,0:T(8,128)(2,1)}), bf16[16,32,1024]{2,1,0:T(8,128)(2,1)S(1)}, u32[]{:S(2)}, u32[]{:S(2)}) async-start(bf16[16,32,1024]{2,1,0:T(8,128)(2,1)} %broadcast_in_dim.14), calls=%async_computation.1 | async-start | bytes 2097152 | tf_op jit(solution)/shard_map/gather_rows/all_to_all | solution.py:171
  42.4 1.3 %collective-permute-start.2 = (bf16[32,512]{1,0:T(8,128)(2,1)S(1)}, bf16[32,512]{1,0:T(8,128)(2,1)S(1)}, u32[]{:S(2)}, u32[]{:S(2)}) collective-permute-start(bf16[32,512]{1,0:T(8,128)(2,1)S(1)} %slice_bitcast_fusion), channel_id=1, source_target_pairs={{0,12},{1,13},{16,28},{17,29},{32,44},{33,45},{48,60},{49,61},{64,... | collective-permute-start | bytes 98312 | tf_op jit(solution)/shard_map/diagonal/ppermute | solution.py:145
  43.7 1.5 %collective-permute-start.1 = (bf16[32,512]{1,0:T(8,128)(2,1)S(1)}, bf16[32,512]{1,0:T(8,128)(2,1)S(1)}, u32[]{:S(2)}, u32[]{:S(2)}) collective-permute-start(bf16[32,512]{1,0:T(8,128)(2,1)S(1)} %slice_bitcast_fusion), channel_id=1, source_target_pairs={{0,8},{1,9},{16,24},{17,25},{32,40},{33,41},{48,56},{49,57},{64,72... | collective-permute-start | bytes 98312 | tf_op jit(solution)/shard_map/diagonal/ppermute | solution.py:145
  45.2 1.3 %collective-permute-start = (bf16[32,512]{1,0:T(8,128)(2,1)S(1)}, bf16[32,512]{1,0:T(8,128)(2,1)S(1)}, u32[]{:S(2)}, u32[]{:S(2)}) collective-permute-start(bf16[32,512]{1,0:T(8,128)(2,1)S(1)} %slice_bitcast_fusion), channel_id=1, source_target_pairs={{0,4},{1,5},{16,20},{17,21},{32,36},{33,37},{48,52},{49,53},{64,68... | collective-permute-start | bytes 98312 | tf_op jit(solution)/shard_map/diagonal/ppermute | solution.py:145
  46.6 0.0 collective-permute-done.2
  46.6 0.0 collective-permute-done.1
  46.6 1.0 collective-permute-done
  47.6 1.3 %collective-permute-start.5 = (bf16[32,512]{1,0:T(8,128)(2,1)S(1)}, bf16[32,512]{1,0:T(8,128)(2,1)S(1)}, u32[]{:S(2)}, u32[]{:S(2)}) collective-permute-start(bf16[32,512]{1,0:T(8,128)(2,1)S(1)} %add_select_fusion), channel_id=1, source_target_pairs={{0,3},{1,2},{4,7},{5,6},{8,11},{9,10},{12,15},{13,14},{16,19},{17,... | collective-permute-start | bytes 98312 | tf_op jit(solution)/shard_map/diagonal/ppermute | solution.py:154
  48.9 1.3 %collective-permute-start.4 = (bf16[32,512]{1,0:T(8,128)(2,1)S(1)}, bf16[32,512]{1,0:T(8,128)(2,1)S(1)}, u32[]{:S(2)}, u32[]{:S(2)}) collective-permute-start(bf16[32,512]{1,0:T(8,128)(2,1)S(1)} %add_select_fusion), channel_id=1, source_target_pairs={{0,2},{1,3},{4,6},{5,7},{8,10},{9,11},{12,14},{13,15},{16,18},{17,... | collective-permute-start | bytes 98312 | tf_op jit(solution)/shard_map/diagonal/ppermute | solution.py:153
  50.1 2.6 %collective-permute-start.3 = (bf16[32,512]{1,0:T(8,128)(2,1)S(1)}, bf16[32,512]{1,0:T(8,128)(2,1)S(1)}, u32[]{:S(2)}, u32[]{:S(2)}) collective-permute-start(bf16[32,512]{1,0:T(8,128)(2,1)S(1)} %add_select_fusion), channel_id=1, source_target_pairs={{0,1},{1,0},{4,5},{5,4},{8,9},{9,8},{12,13},{13,12},{16,17},{17,16... | collective-permute-start | bytes 98312 | tf_op jit(solution)/shard_map/diagonal/ppermute | solution.py:152
  52.8 0.0 collective-permute-done.7
  52.8 0.1 broadcast_select_fusion.2
  52.9 0.0 collective-permute-done.5
  52.9 0.0 collective-permute-done.4
  52.9 2.2 %collective-permute-done.3 = bf16[32,512]{1,0:T(8,128)(2,1)S(1)} collective-permute-done((bf16[32,512]{1,0:T(8,128)(2,1)S(1)}, bf16[32,512]{1,0:T(8,128)(2,1)S(1)}, u32[]{:S(2)}, u32[]{:S(2)}) %collective-permute-start.3) | collective-permute-done | bytes 32800 | tf_op jit(solution)/shard_map/diagonal/ppermute | solution.py:152
  55.1 2.3 %all-to-all-done.1 = bf16[16,32,1024]{2,1,0:T(8,128)(2,1)S(1)} async-done(((bf16[16,32,1024]{2,1,0:T(8,128)(2,1)}), bf16[16,32,1024]{2,1,0:T(8,128)(2,1)S(1)}, u32[]{:S(2)}, u32[]{:S(2)}) %all-to-all-start.1) | async-done | bytes 1048608 | tf_op jit(solution)/shard_map/gather_rows/all_to_all | solution.py:171
  57.4 2.1 %collective-permute-start.8 = (bf16[512,512]{1,0:T(8,128)(2,1)S(1)}, bf16[512,512]{1,0:T(8,128)(2,1)}, u32[]{:S(2)}, u32[]{:S(2)}) collective-permute-start(bf16[512,512]{1,0:T(8,128)(2,1)S(1)} %broadcast_select_fusion.2), channel_id=1, source_target_pairs={{0,2},{4,6},{10,8},{12,14},{1,15},{13,11},{7,9},{5,3},{16,18},{20,... | collective-permute-start | bytes 1572872 | tf_op jit(solution)/shard_map/panels/ppermute | solution.py:108
  59.5 1.1 %broadcast_in_dim.15 = bf16[16,2,32,512]{3,2,1,0:T(8,128)(2,1)} broadcast(bf16[2,32,512]{2,1,0:T(8,128)(2,1)S(1)} %pad_maximum_fusion), dimensions={1,2,3} | broadcast | bytes 1114112 | tf_op jit(solution)/shard_map/diagonal/broadcast_in_dim | solution.py:170
  60.6 4.4 %all-to-all-start.2 = ((bf16[16,2,32,512]{3,2,1,0:T(8,128)(2,1)}), bf16[16,2,32,512]{3,2,1,0:T(8,128)(2,1)S(1)}, u32[]{:S(2)}, u32[]{:S(2)}) async-start(bf16[16,2,32,512]{3,2,1,0:T(8,128)(2,1)} %broadcast_in_dim.15), calls=%async_computation.2 | async-start | bytes 2097152 | tf_op jit(solution)/shard_map/diagonal/all_to_all | solution.py:171
  65.0 1.6 %collective-permute-done.8 = bf16[512,512]{1,0:T(8,128)(2,1)} collective-permute-done((bf16[512,512]{1,0:T(8,128)(2,1)S(1)}, bf16[512,512]{1,0:T(8,128)(2,1)}, u32[]{:S(2)}, u32[]{:S(2)}) %collective-permute-start.8) | collective-permute-done | bytes 524320 | tf_op jit(solution)/shard_map/panels/ppermute | solution.py:108
  66.7 0.1 broadcast_select_fusion.held
  66.7 0.0 copy-start
  66.8 6.9 %collective-permute-start.9 = (bf16[512,512]{1,0:T(8,128)(2,1)S(1)}, bf16[512,512]{1,0:T(8,128)(2,1)S(1)}, u32[]{:S(2)}, u32[]{:S(2)}) collective-permute-start(bf16[512,512]{1,0:T(8,128)(2,1)S(1)} %broadcast_select_fusion.held), channel_id=1, source_target_pairs={{0,15},{1,2},{2,1},{3,4},{4,3},{5,6},{6,5},{7,8},{8,7},{9,10},{10,... | collective-permute-start | bytes 1572872 | tf_op jit(solution)/shard_map/panels/ppermute | solution.py:116
  73.7 5.6 %collective-permute-start.11 = (bf16[512,1024]{1,0:T(8,128)(2,1)S(1)}, bf16[512,1024]{1,0:T(8,128)(2,1)}, u32[]{:S(2)}, u32[]{:S(2)}) collective-permute-start(bf16[512,1024]{1,0:T(8,128)(2,1)S(1)} %bitcast.25), channel_id=1, source_target_pairs={{0,16},{16,0},{32,48},{48,32},{64,80},{80,64},{96,112},{112,96},{1... | collective-permute-start | bytes 3145736 | tf_op jit(solution)/shard_map/gather_rows/ppermute | solution.py:190
  79.2 0.0 all-to-all-done.2.own_diag
  79.2 0.0 copy-start.2
  79.2 3.3 %collective-permute-done.9.other = bf16[512,512]{1,0:T(8,128)(2,1)S(1)} collective-permute-done((bf16[512,512]{1,0:T(8,128)(2,1)S(1)}, bf16[512,512]{1,0:T(8,128)(2,1)S(1)}, u32[]{:S(2)}, u32[]{:S(2)}) %collective-permute-start.9) | collective-permute-done | bytes 524320 | tf_op jit(solution)/shard_map/panels/ppermute | solution.py:116
  82.5 5.9 %collective-permute-start.10 = (bf16[16,2,32,512]{3,2,1,0:T(8,128)(2,1)S(1)}, bf16[16,2,32,512]{3,2,1,0:T(8,128)(2,1)S(1)}, u32[]{:S(2)}, u32[]{:S(2)}) collective-permute-start(bf16[16,2,32,512]{3,2,1,0:T(8,128)(2,1)S(1)} %all-to-all-done.2.own_diag), channel_id=1, source_target_pairs={{0,16},{16,0},{32,48},{48,32},{64,80},{80,64},{96,112},{112,96},{1... | collective-permute-start | bytes 3145736 | tf_op jit(solution)/shard_map/diagonal/ppermute | solution.py:200
  88.4 1.5 %copy.20 = bf16[64,8,2,512]{3,1,2,0:T(8,128)(2,1)S(1)} copy(bf16[64,8,2,512]{3,2,1,0:T(2,128)(2,1)} %bitcast.28) | data formatting | bytes 2097152
  89.9 0.0 collective-permute-done.11.other_rows
  89.9 0.8 collective-permute-done.10.other_diag
  90.7 0.0 copy-done
  90.7 0.0 copy-done.3
  90.7 0.0 copy-done.2
  90.7 1.0 %copy-done.1 = bf16[512,512]{1,0:T(8,128)(2,1)S(1)} copy-done((bf16[512,512]{1,0:T(8,128)(2,1)S(1)}, bf16[512,512]{1,0:T(8,128)(2,1)}, u32[]{:S(2)}) %copy-start.1) | copy-done | bytes 524312
  91.8 1.0 %copy-done.4 = bf16[512,512]{1,0:T(8,128)(2,1)S(1)} copy-done((bf16[512,512]{1,0:T(8,128)(2,1)S(1)}, bf16[512,512]{1,0:T(8,128)(2,1)}, u32[]{:S(2)}) %copy-start.4) | copy-done | bytes 524312
  92.8 7.6 %finish.1 = bf16[512,1024]{1,0:T(8,128)(2,1)S(1)} custom-call(bf16[16,2,32,512]{3,2,1,0:T(8,128)(2,1)S(1)} %all-to-all-done.2.own_diag, bf16[16,2,32,512]{3,2,1,0:T(8,128)(2,1)S(1)} %collective-permute-done.10.other_diag, f32[2,512,512]{2,1,0:T(8,128)S(1)} %copy-done.2, bf16[512,1024]{1,0:T(8,128)(2,1)S(1)} %bitcast.26, ...), custom_call_target="tpu_custom_call" | custom-call | tf_op jit(solution)/shard_map/finish/pallas_call | solution.py:203
  100.4 1.6 %reshape.27 = bf16[512,1,2,512]{3,2,0,1:T(2,128)(2,1)} reshape(bf16[512,1024]{1,0:T(8,128)(2,1)S(1)} %finish.1) | data formatting | bytes 2097152 | tf_op jit(solution)/shard_map/reshape | solution.py:213
  (10 shorter events, 0.1 us)
Async XLA Ops:
  0.0 7.7 %copy-start.5 = (bf16[512,1,2,512]{3,2,1,0:T(2,128)(2,1)S(1)}, bf16[512,1,2,512]{3,2,1,0:T(2,128)(2,1)}, u32[]{:S(2)}) copy-start(bf16[512,1,2,512]{3,2,1,0:T(2,128)(2,1)} %param.2) | copy-start | bytes 3145732
  0.0 34.9 %all-to-all-start = ((bf16[512,1,2,512]{3,2,1,0:T(2,128)(2,1)}), bf16[512,1,2,512]{3,2,1,0:T(2,128)(2,1)S(1)}, u32[]{:S(2)}, u32[]{:S(2)}) async-start(bf16[512,1,2,512]{3,2,1,0:T(2,128)(2,1)} %param.2), calls=%async_computation | async-start | bytes 2097152 | tf_op jit(solution)/shard_map/scatter_rows/all_to_all | solution.py:176
  7.9 24.8 %collective-permute-start.6 = (bf16[512,512]{1,0:T(8,128)(2,1)S(1)}, bf16[512,512]{1,0:T(8,128)(2,1)S(1)}, u32[]{:S(2)}, u32[]{:S(2)}) collective-permute-start(bf16[512,512]{1,0:T(8,128)(2,1)S(1)} %bitcast.32), channel_id=1, source_target_pairs={{0,10},{1,7},{16,26},{17,23},{32,42},{33,39},{48,58},{49,55},{64,7... | collective-permute-start | bytes 1572872 | tf_op jit(solution)/shard_map/panels/ppermute | solution.py:108
  32.8 20.0 %collective-permute-start.7 = (bf16[512,512]{1,0:T(8,128)(2,1)S(1)}, bf16[512,512]{1,0:T(8,128)(2,1)}, u32[]{:S(2)}, u32[]{:S(2)}) collective-permute-start(bf16[512,512]{1,0:T(8,128)(2,1)S(1)} %broadcast_select_fusion.1), channel_id=1, source_target_pairs={{0,12},{10,4},{1,5},{7,13},{16,28},{26,20},{17,21},{23,29},{32,44}... | collective-permute-start | bytes 1572872 | tf_op jit(solution)/shard_map/panels/ppermute | solution.py:108
  36.1 21.4 %all-to-all-start.1 = ((bf16[16,32,1024]{2,1,0:T(8,128)(2,1)}), bf16[16,32,1024]{2,1,0:T(8,128)(2,1)S(1)}, u32[]{:S(2)}, u32[]{:S(2)}) async-start(bf16[16,32,1024]{2,1,0:T(8,128)(2,1)} %broadcast_in_dim.14), calls=%async_computation.1 | async-start | bytes 2097152 | tf_op jit(solution)/shard_map/gather_rows/all_to_all | solution.py:171
  42.4 4.1 %collective-permute-start.2 = (bf16[32,512]{1,0:T(8,128)(2,1)S(1)}, bf16[32,512]{1,0:T(8,128)(2,1)S(1)}, u32[]{:S(2)}, u32[]{:S(2)}) collective-permute-start(bf16[32,512]{1,0:T(8,128)(2,1)S(1)} %slice_bitcast_fusion), channel_id=1, source_target_pairs={{0,12},{1,13},{16,28},{17,29},{32,44},{33,45},{48,60},{49,61},{64,... | collective-permute-start | bytes 98312 | tf_op jit(solution)/shard_map/diagonal/ppermute | solution.py:145
  43.7 2.8 %collective-permute-start.1 = (bf16[32,512]{1,0:T(8,128)(2,1)S(1)}, bf16[32,512]{1,0:T(8,128)(2,1)S(1)}, u32[]{:S(2)}, u32[]{:S(2)}) collective-permute-start(bf16[32,512]{1,0:T(8,128)(2,1)S(1)} %slice_bitcast_fusion), channel_id=1, source_target_pairs={{0,8},{1,9},{16,24},{17,25},{32,40},{33,41},{48,56},{49,57},{64,72... | collective-permute-start | bytes 98312 | tf_op jit(solution)/shard_map/diagonal/ppermute | solution.py:145
  45.2 2.3 %collective-permute-start = (bf16[32,512]{1,0:T(8,128)(2,1)S(1)}, bf16[32,512]{1,0:T(8,128)(2,1)S(1)}, u32[]{:S(2)}, u32[]{:S(2)}) collective-permute-start(bf16[32,512]{1,0:T(8,128)(2,1)S(1)} %slice_bitcast_fusion), channel_id=1, source_target_pairs={{0,4},{1,5},{16,20},{17,21},{32,36},{33,37},{48,52},{49,53},{64,68... | collective-permute-start | bytes 98312 | tf_op jit(solution)/shard_map/diagonal/ppermute | solution.py:145
  47.6 5.3 %collective-permute-start.5 = (bf16[32,512]{1,0:T(8,128)(2,1)S(1)}, bf16[32,512]{1,0:T(8,128)(2,1)S(1)}, u32[]{:S(2)}, u32[]{:S(2)}) collective-permute-start(bf16[32,512]{1,0:T(8,128)(2,1)S(1)} %add_select_fusion), channel_id=1, source_target_pairs={{0,3},{1,2},{4,7},{5,6},{8,11},{9,10},{12,15},{13,14},{16,19},{17,... | collective-permute-start | bytes 98312 | tf_op jit(solution)/shard_map/diagonal/ppermute | solution.py:154
  48.9 4.1 %collective-permute-start.4 = (bf16[32,512]{1,0:T(8,128)(2,1)S(1)}, bf16[32,512]{1,0:T(8,128)(2,1)S(1)}, u32[]{:S(2)}, u32[]{:S(2)}) collective-permute-start(bf16[32,512]{1,0:T(8,128)(2,1)S(1)} %add_select_fusion), channel_id=1, source_target_pairs={{0,2},{1,3},{4,6},{5,7},{8,10},{9,11},{12,14},{13,15},{16,18},{17,... | collective-permute-start | bytes 98312 | tf_op jit(solution)/shard_map/diagonal/ppermute | solution.py:153
  50.1 5.0 %collective-permute-start.3 = (bf16[32,512]{1,0:T(8,128)(2,1)S(1)}, bf16[32,512]{1,0:T(8,128)(2,1)S(1)}, u32[]{:S(2)}, u32[]{:S(2)}) collective-permute-start(bf16[32,512]{1,0:T(8,128)(2,1)S(1)} %add_select_fusion), channel_id=1, source_target_pairs={{0,1},{1,0},{4,5},{5,4},{8,9},{9,8},{12,13},{13,12},{16,17},{17,16... | collective-permute-start | bytes 98312 | tf_op jit(solution)/shard_map/diagonal/ppermute | solution.py:152
  57.4 9.3 %collective-permute-start.8 = (bf16[512,512]{1,0:T(8,128)(2,1)S(1)}, bf16[512,512]{1,0:T(8,128)(2,1)}, u32[]{:S(2)}, u32[]{:S(2)}) collective-permute-start(bf16[512,512]{1,0:T(8,128)(2,1)S(1)} %broadcast_select_fusion.2), channel_id=1, source_target_pairs={{0,2},{4,6},{10,8},{12,14},{1,15},{13,11},{7,9},{5,3},{16,18},{20,... | collective-permute-start | bytes 1572872 | tf_op jit(solution)/shard_map/panels/ppermute | solution.py:108
  60.6 18.6 %all-to-all-start.2 = ((bf16[16,2,32,512]{3,2,1,0:T(8,128)(2,1)}), bf16[16,2,32,512]{3,2,1,0:T(8,128)(2,1)S(1)}, u32[]{:S(2)}, u32[]{:S(2)}) async-start(bf16[16,2,32,512]{3,2,1,0:T(8,128)(2,1)} %broadcast_in_dim.15), calls=%async_computation.2 | async-start | bytes 2097152 | tf_op jit(solution)/shard_map/diagonal/all_to_all | solution.py:171
  66.7 24.0 %copy-start = (bf16[512,512]{1,0:T(8,128)(2,1)}, bf16[512,512]{1,0:T(8,128)(2,1)S(1)}, u32[]{:S(2)}) copy-start(bf16[512,512]{1,0:T(8,128)(2,1)S(1)} %broadcast_select_fusion.held) | copy-start | bytes 1572868
  66.8 15.8 %collective-permute-start.9 = (bf16[512,512]{1,0:T(8,128)(2,1)S(1)}, bf16[512,512]{1,0:T(8,128)(2,1)S(1)}, u32[]{:S(2)}, u32[]{:S(2)}) collective-permute-start(bf16[512,512]{1,0:T(8,128)(2,1)S(1)} %broadcast_select_fusion.held), channel_id=1, source_target_pairs={{0,15},{1,2},{2,1},{3,4},{4,3},{5,6},{6,5},{7,8},{8,7},{9,10},{10,... | collective-permute-start | bytes 1572872 | tf_op jit(solution)/shard_map/panels/ppermute | solution.py:116
  73.7 16.2 %collective-permute-start.11 = (bf16[512,1024]{1,0:T(8,128)(2,1)S(1)}, bf16[512,1024]{1,0:T(8,128)(2,1)}, u32[]{:S(2)}, u32[]{:S(2)}) collective-permute-start(bf16[512,1024]{1,0:T(8,128)(2,1)S(1)} %bitcast.25), channel_id=1, source_target_pairs={{0,16},{16,0},{32,48},{48,32},{64,80},{80,64},{96,112},{112,96},{1... | collective-permute-start | bytes 3145736 | tf_op jit(solution)/shard_map/gather_rows/ppermute | solution.py:190
  79.2 11.5 %copy-start.2 = (f32[2,512,512]{2,1,0:T(8,128)S(1)}, f32[2,512,512]{2,1,0:T(8,128)}, u32[]{:S(2)}) copy-start(f32[2,512,512]{2,1,0:T(8,128)} %approx.1) | copy-start | bytes 6291460
  82.5 8.2 %copy-start.3 = (bf16[512,512]{1,0:T(8,128)(2,1)}, bf16[512,512]{1,0:T(8,128)(2,1)S(1)}, u32[]{:S(2)}) copy-start(bf16[512,512]{1,0:T(8,128)(2,1)S(1)} %collective-permute-done.9.other) | copy-start | bytes 1572868
  82.5 8.2 %collective-permute-start.10 = (bf16[16,2,32,512]{3,2,1,0:T(8,128)(2,1)S(1)}, bf16[16,2,32,512]{3,2,1,0:T(8,128)(2,1)S(1)}, u32[]{:S(2)}, u32[]{:S(2)}) collective-permute-start(bf16[16,2,32,512]{3,2,1,0:T(8,128)(2,1)S(1)} %all-to-all-done.2.own_diag), channel_id=1, source_target_pairs={{0,16},{16,0},{32,48},{48,32},{64,80},{80,64},{96,112},{112,96},{1... | collective-permute-start | bytes 3145736 | tf_op jit(solution)/shard_map/diagonal/ppermute | solution.py:200
  90.7 1.0 %copy-start.1 = (bf16[512,512]{1,0:T(8,128)(2,1)S(1)}, bf16[512,512]{1,0:T(8,128)(2,1)}, u32[]{:S(2)}) copy-start(bf16[512,512]{1,0:T(8,128)(2,1)} %copy-done) | copy-start | bytes 1572868
  91.7 1.0 %copy-start.4 = (bf16[512,512]{1,0:T(8,128)(2,1)S(1)}, bf16[512,512]{1,0:T(8,128)(2,1)}, u32[]{:S(2)}) copy-start(bf16[512,512]{1,0:T(8,128)(2,1)} %copy-done.3) | copy-start | bytes 1572868

commit v9 on v8

--- a/solution.py
+++ b/solution.py
@@ -80,8 +80,8 @@
     fetch(held, panel0_ref, 2).wait()
     fetch(held, panel1_ref, 3).wait()
     fetch(block, block_ref, 4).wait()
-    half = size // 2
-    for part in range(2):
+    half = size
+    for part in range(1):
         rows = pl.ds(part * half, half)
         lower0 = product(panel0_ref[rows], inverse0).astype(jnp.bfloat16)
         rest = panel1_ref[rows].astype(jnp.float32) - product(lower0, right)

time: 103 us -> 102 us (level)
  no operation moved by 1% of the time
where the time goes in v9:
time: 102 us; the launch traced here: 101 us
  starting transfers between devices  64.9 us (64%)
  waiting for transfers between devices  21.4 us (21%)
  local copies, waits for them, and re-layouts  7.52 us (7%)
  Pallas kernels  7.09 us (7%)
    ppermute x3, starting transfers between devices, panel_step(): got = lax.ppermute(held, 'col', pairs)  18.8 us
    ppermute x3, waiting for transfers between devices, panel_step(): got = lax.ppermute(held, 'col', pairs)  11.9 us
    all_to_all x2, starting transfers between devices, gather_part(): lax.all_to_all(copies, 'row', 0, 0, tiled=True, axis_index_groups=same_core)  10.7 us
    all_to_all x1, starting transfers between devices, local(): lax.all_to_all(matrix, 'row', 0, 0, tiled=True, axis_index_groups=same_core)  7.72 us
    pallas_call x1, Pallas kernels, local(): pl.pallas_call(finish_kernel, out_shape=jax.ShapeDtypeStruct(wide, jnp.bf...  7.09 us
    ppermute x1, starting transfers between devices, panel_pair(): return lax.ppermute(held, 'col', pairs)  6.9 us
    ppermute x1, starting transfers between devices, local(): other = lax.ppermute(mine, 'row', swap_core)  5.91 us
    ppermute x1, starting transfers between devices, local(): other_rows = lax.ppermute(own_rows, 'row', swap_core)  5.56 us
  transfers between devices with their start and end apart: 15, of which 7 were waited for; matrix products, arithmetic and copies ran while one was open for 4% of the time, Pallas kernels for 0%

profile of v9, /device:TPU:1, one launch (start us, length us, event | category | flops | bytes accessed | tf_op | source)
XLA Modules:
  0.0 101.5 jit_solution(15628596994172365574)
XLA Ops:
  0.0 0.0 copy-start.5
  0.0 7.7 %all-to-all-start = ((bf16[512,1,2,512]{3,2,1,0:T(2,128)(2,1)}), bf16[512,1,2,512]{3,2,1,0:T(2,128)(2,1)S(1)}, u32[]{:S(2)}, u32[]{:S(2)}) async-start(bf16[512,1,2,512]{3,2,1,0:T(2,128)(2,1)} %param.2), calls=%async_computation | async-start | bytes 2097152 | tf_op jit(solution)/shard_map/scatter_rows/all_to_all | solution.py:176
  7.7 0.0 copy-done.5
  7.7 0.1 copy.25
  7.9 14.6 %collective-permute-start.6 = (bf16[512,512]{1,0:T(8,128)(2,1)S(1)}, bf16[512,512]{1,0:T(8,128)(2,1)S(1)}, u32[]{:S(2)}, u32[]{:S(2)}) collective-permute-start(bf16[512,512]{1,0:T(8,128)(2,1)S(1)} %bitcast.32), channel_id=1, source_target_pairs={{0,10},{1,7},{16,26},{17,23},{32,42},{33,39},{48,58},{49,55},{64,7... | collective-permute-start | bytes 1572872 | tf_op jit(solution)/shard_map/panels/ppermute | solution.py:108
  22.5 10.2 %collective-permute-done.6 = bf16[512,512]{1,0:T(8,128)(2,1)S(1)} collective-permute-done((bf16[512,512]{1,0:T(8,128)(2,1)S(1)}, bf16[512,512]{1,0:T(8,128)(2,1)S(1)}, u32[]{:S(2)}, u32[]{:S(2)}) %collective-permute-start.6) | collective-permute-done | bytes 524320 | tf_op jit(solution)/shard_map/panels/ppermute | solution.py:108
  32.7 0.1 broadcast_select_fusion.1
  32.8 2.1 %collective-permute-start.7 = (bf16[512,512]{1,0:T(8,128)(2,1)S(1)}, bf16[512,512]{1,0:T(8,128)(2,1)}, u32[]{:S(2)}, u32[]{:S(2)}) collective-permute-start(bf16[512,512]{1,0:T(8,128)(2,1)S(1)} %broadcast_select_fusion.1), channel_id=1, source_target_pairs={{0,12},{10,4},{1,5},{7,13},{16,28},{26,20},{17,21},{23,29},{32,44}... | collective-permute-start | bytes 1572872 | tf_op jit(solution)/shard_map/panels/ppermute | solution.py:108
  34.9 0.0 all-to-all-done
  35.0 1.1 %broadcast_in_dim.14 = bf16[16,32,1024]{2,1,0:T(8,128)(2,1)} broadcast(bf16[32,1024]{1,0:T(8,128)(2,1)S(1)} %bitcast.33), dimensions={1,2} | broadcast | bytes 1114112 | tf_op jit(solution)/shard_map/gather_rows/broadcast_in_dim | solution.py:170
  36.1 6.4 %all-to-all-start.1 = ((bf16[16,32,1024]{2,1,0:T(8,128)(2,1)}), bf16[16,32,1024]{2,1,0:T(8,128)(2,1)S(1)}, u32[]{:S(2)}, u32[]{:S(2)}) async-start(bf16[16,32,1024]{2,1,0:T(8,128)(2,1)} %broadcast_in_dim.14), calls=%async_computation.1 | async-start | bytes 2097152 | tf_op jit(solution)/shard_map/gather_rows/all_to_all | solution.py:171
  42.4 1.3 %collective-permute-start.2 = (bf16[32,512]{1,0:T(8,128)(2,1)S(1)}, bf16[32,512]{1,0:T(8,128)(2,1)S(1)}, u32[]{:S(2)}, u32[]{:S(2)}) collective-permute-start(bf16[32,512]{1,0:T(8,128)(2,1)S(1)} %slice_bitcast_fusion), channel_id=1, source_target_pairs={{0,12},{1,13},{16,28},{17,29},{32,44},{33,45},{48,60},{49,61},{64,... | collective-permute-start | bytes 98312 | tf_op jit(solution)/shard_map/diagonal/ppermute | solution.py:145
  43.7 1.5 %collective-permute-start.1 = (bf16[32,512]{1,0:T(8,128)(2,1)S(1)}, bf16[32,512]{1,0:T(8,128)(2,1)S(1)}, u32[]{:S(2)}, u32[]{:S(2)}) collective-permute-start(bf16[32,512]{1,0:T(8,128)(2,1)S(1)} %slice_bitcast_fusion), channel_id=1, source_target_pairs={{0,8},{1,9},{16,24},{17,25},{32,40},{33,41},{48,56},{49,57},{64,72... | collective-permute-start | bytes 98312 | tf_op jit(solution)/shard_map/diagonal/ppermute | solution.py:145
  45.2 1.3 %collective-permute-start = (bf16[32,512]{1,0:T(8,128)(2,1)S(1)}, bf16[32,512]{1,0:T(8,128)(2,1)S(1)}, u32[]{:S(2)}, u32[]{:S(2)}) collective-permute-start(bf16[32,512]{1,0:T(8,128)(2,1)S(1)} %slice_bitcast_fusion), channel_id=1, source_target_pairs={{0,4},{1,5},{16,20},{17,21},{32,36},{33,37},{48,52},{49,53},{64,68... | collective-permute-start | bytes 98312 | tf_op jit(solution)/shard_map/diagonal/ppermute | solution.py:145
  46.6 0.0 collective-permute-done.2
  46.6 0.0 collective-permute-done.1
  46.6 1.0 collective-permute-done
  47.6 1.3 %collective-permute-start.5 = (bf16[32,512]{1,0:T(8,128)(2,1)S(1)}, bf16[32,512]{1,0:T(8,128)(2,1)S(1)}, u32[]{:S(2)}, u32[]{:S(2)}) collective-permute-start(bf16[32,512]{1,0:T(8,128)(2,1)S(1)} %add_select_fusion), channel_id=1, source_target_pairs={{0,3},{1,2},{4,7},{5,6},{8,11},{9,10},{12,15},{13,14},{16,19},{17,... | collective-permute-start | bytes 98312 | tf_op jit(solution)/shard_map/diagonal/ppermute | solution.py:154
  48.9 1.3 %collective-permute-start.4 = (bf16[32,512]{1,0:T(8,128)(2,1)S(1)}, bf16[32,512]{1,0:T(8,128)(2,1)S(1)}, u32[]{:S(2)}, u32[]{:S(2)}) collective-permute-start(bf16[32,512]{1,0:T(8,128)(2,1)S(1)} %add_select_fusion), channel_id=1, source_target_pairs={{0,2},{1,3},{4,6},{5,7},{8,10},{9,11},{12,14},{13,15},{16,18},{17,... | collective-permute-start | bytes 98312 | tf_op jit(solution)/shard_map/diagonal/ppermute | solution.py:153
  50.1 2.6 %collective-permute-start.3 = (bf16[32,512]{1,0:T(8,128)(2,1)S(1)}, bf16[32,512]{1,0:T(8,128)(2,1)S(1)}, u32[]{:S(2)}, u32[]{:S(2)}) collective-permute-start(bf16[32,512]{1,0:T(8,128)(2,1)S(1)} %add_select_fusion), channel_id=1, source_target_pairs={{0,1},{1,0},{4,5},{5,4},{8,9},{9,8},{12,13},{13,12},{16,17},{17,16... | collective-permute-start | bytes 98312 | tf_op jit(solution)/shard_map/diagonal/ppermute | solution.py:152
  52.8 0.0 collective-permute-done.7
  52.8 0.1 broadcast_select_fusion.2
  52.9 0.0 collective-permute-done.5
  52.9 0.0 collective-permute-done.4
  52.9 2.2 %collective-permute-done.3 = bf16[32,512]{1,0:T(8,128)(2,1)S(1)} collective-permute-done((bf16[32,512]{1,0:T(8,128)(2,1)S(1)}, bf16[32,512]{1,0:T(8,128)(2,1)S(1)}, u32[]{:S(2)}, u32[]{:S(2)}) %collective-permute-start.3) | collective-permute-done | bytes 32800 | tf_op jit(solution)/shard_map/diagonal/ppermute | solution.py:152
  55.1 2.3 %all-to-all-done.1 = bf16[16,32,1024]{2,1,0:T(8,128)(2,1)S(1)} async-done(((bf16[16,32,1024]{2,1,0:T(8,128)(2,1)}), bf16[16,32,1024]{2,1,0:T(8,128)(2,1)S(1)}, u32[]{:S(2)}, u32[]{:S(2)}) %all-to-all-start.1) | async-done | bytes 1048608 | tf_op jit(solution)/shard_map/gather_rows/all_to_all | solution.py:171
  57.4 2.1 %collective-permute-start.8 = (bf16[512,512]{1,0:T(8,128)(2,1)S(1)}, bf16[512,512]{1,0:T(8,128)(2,1)}, u32[]{:S(2)}, u32[]{:S(2)}) collective-permute-start(bf16[512,512]{1,0:T(8,128)(2,1)S(1)} %broadcast_select_fusion.2), channel_id=1, source_target_pairs={{0,2},{4,6},{10,8},{12,14},{1,15},{13,11},{7,9},{5,3},{16,18},{20,... | collective-permute-start | bytes 1572872 | tf_op jit(solution)/shard_map/panels/ppermute | solution.py:108
  59.5 1.1 %broadcast_in_dim.15 = bf16[16,2,32,512]{3,2,1,0:T(8,128)(2,1)} broadcast(bf16[2,32,512]{2,1,0:T(8,128)(2,1)S(1)} %pad_maximum_fusion), dimensions={1,2,3} | broadcast | bytes 1114112 | tf_op jit(solution)/shard_map/diagonal/broadcast_in_dim | solution.py:170
  60.6 4.4 %all-to-all-start.2 = ((bf16[16,2,32,512]{3,2,1,0:T(8,128)(2,1)}), bf16[16,2,32,512]{3,2,1,0:T(8,128)(2,1)S(1)}, u32[]{:S(2)}, u32[]{:S(2)}) async-start(bf16[16,2,32,512]{3,2,1,0:T(8,128)(2,1)} %broadcast_in_dim.15), calls=%async_computation.2 | async-start | bytes 2097152 | tf_op jit(solution)/shard_map/diagonal/all_to_all | solution.py:171
  65.0 1.6 %collective-permute-done.8 = bf16[512,512]{1,0:T(8,128)(2,1)} collective-permute-done((bf16[512,512]{1,0:T(8,128)(2,1)S(1)}, bf16[512,512]{1,0:T(8,128)(2,1)}, u32[]{:S(2)}, u32[]{:S(2)}) %collective-permute-start.8) | collective-permute-done | bytes 524320 | tf_op jit(solution)/shard_map/panels/ppermute | solution.py:108
  66.7 0.1 broadcast_select_fusion.held
  66.7 0.0 copy-start
  66.8 6.9 %collective-permute-start.9 = (bf16[512,512]{1,0:T(8,128)(2,1)S(1)}, bf16[512,512]{1,0:T(8,128)(2,1)S(1)}, u32[]{:S(2)}, u32[]{:S(2)}) collective-permute-start(bf16[512,512]{1,0:T(8,128)(2,1)S(1)} %broadcast_select_fusion.held), channel_id=1, source_target_pairs={{0,15},{1,2},{2,1},{3,4},{4,3},{5,6},{6,5},{7,8},{8,7},{9,10},{10,... | collective-permute-start | bytes 1572872 | tf_op jit(solution)/shard_map/panels/ppermute | solution.py:116
  73.7 5.6 %collective-permute-start.11 = (bf16[512,1024]{1,0:T(8,128)(2,1)S(1)}, bf16[512,1024]{1,0:T(8,128)(2,1)}, u32[]{:S(2)}, u32[]{:S(2)}) collective-permute-start(bf16[512,1024]{1,0:T(8,128)(2,1)S(1)} %bitcast.25), channel_id=1, source_target_pairs={{0,16},{16,0},{32,48},{48,32},{64,80},{80,64},{96,112},{112,96},{1... | collective-permute-start | bytes 3145736 | tf_op jit(solution)/shard_map/gather_rows/ppermute | solution.py:190
  79.2 0.0 all-to-all-done.2.own_diag
  79.2 0.0 copy-start.2
  79.2 3.3 %collective-permute-done.9.other = bf16[512,512]{1,0:T(8,128)(2,1)S(1)} collective-permute-done((bf16[512,512]{1,0:T(8,128)(2,1)S(1)}, bf16[512,512]{1,0:T(8,128)(2,1)S(1)}, u32[]{:S(2)}, u32[]{:S(2)}) %collective-permute-start.9) | collective-permute-done | bytes 524320 | tf_op jit(solution)/shard_map/panels/ppermute | solution.py:116
  82.5 5.9 %collective-permute-start.10 = (bf16[16,2,32,512]{3,2,1,0:T(8,128)(2,1)S(1)}, bf16[16,2,32,512]{3,2,1,0:T(8,128)(2,1)S(1)}, u32[]{:S(2)}, u32[]{:S(2)}) collective-permute-start(bf16[16,2,32,512]{3,2,1,0:T(8,128)(2,1)S(1)} %all-to-all-done.2.own_diag), channel_id=1, source_target_pairs={{0,16},{16,0},{32,48},{48,32},{64,80},{80,64},{96,112},{112,96},{1... | collective-permute-start | bytes 3145736 | tf_op jit(solution)/shard_map/diagonal/ppermute | solution.py:200
  88.4 1.5 %copy.20 = bf16[64,8,2,512]{3,1,2,0:T(8,128)(2,1)S(1)} copy(bf16[64,8,2,512]{3,2,1,0:T(2,128)(2,1)} %bitcast.28) | data formatting | bytes 2097152
  89.9 0.0 collective-permute-done.11.other_rows
  89.9 0.8 collective-permute-done.10.other_diag
  90.7 0.0 copy-done
  90.7 0.0 copy-done.3
  90.7 0.0 copy-done.2
  90.7 1.0 %copy-done.1 = bf16[512,512]{1,0:T(8,128)(2,1)S(1)} copy-done((bf16[512,512]{1,0:T(8,128)(2,1)S(1)}, bf16[512,512]{1,0:T(8,128)(2,1)}, u32[]{:S(2)}) %copy-start.1) | copy-done | bytes 524312
  91.8 1.0 %copy-done.4 = bf16[512,512]{1,0:T(8,128)(2,1)S(1)} copy-done((bf16[512,512]{1,0:T(8,128)(2,1)S(1)}, bf16[512,512]{1,0:T(8,128)(2,1)}, u32[]{:S(2)}) %copy-start.4) | copy-done | bytes 524312
  92.8 7.1 %finish.1 = bf16[512,1024]{1,0:T(8,128)(2,1)S(1)} custom-call(bf16[16,2,32,512]{3,2,1,0:T(8,128)(2,1)S(1)} %all-to-all-done.2.own_diag, bf16[16,2,32,512]{3,2,1,0:T(8,128)(2,1)S(1)} %collective-permute-done.10.other_diag, f32[2,512,512]{2,1,0:T(8,128)S(1)} %copy-done.2, bf16[512,1024]{1,0:T(8,128)(2,1)S(1)} %bitcast.26, ...), custom_call_target="tpu_custom_call" | custom-call | tf_op jit(solution)/shard_map/finish/pallas_call | solution.py:203
  99.9 1.6 %reshape.27 = bf16[512,1,2,512]{3,2,0,1:T(2,128)(2,1)} reshape(bf16[512,1024]{1,0:T(8,128)(2,1)S(1)} %finish.1) | data formatting | bytes 2097152 | tf_op jit(solution)/shard_map/reshape | solution.py:213
  (10 shorter events, 0.1 us)
Async XLA Ops:
  0.0 7.7 %copy-start.5 = (bf16[512,1,2,512]{3,2,1,0:T(2,128)(2,1)S(1)}, bf16[512,1,2,512]{3,2,1,0:T(2,128)(2,1)}, u32[]{:S(2)}) copy-start(bf16[512,1,2,512]{3,2,1,0:T(2,128)(2,1)} %param.2) | copy-start | bytes 3145732
  0.0 34.9 %all-to-all-start = ((bf16[512,1,2,512]{3,2,1,0:T(2,128)(2,1)}), bf16[512,1,2,512]{3,2,1,0:T(2,128)(2,1)S(1)}, u32[]{:S(2)}, u32[]{:S(2)}) async-start(bf16[512,1,2,512]{3,2,1,0:T(2,128)(2,1)} %param.2), calls=%async_computation | async-start | bytes 2097152 | tf_op jit(solution)/shard_map/scatter_rows/all_to_all | solution.py:176
  7.9 24.8 %collective-permute-start.6 = (bf16[512,512]{1,0:T(8,128)(2,1)S(1)}, bf16[512,512]{1,0:T(8,128)(2,1)S(1)}, u32[]{:S(2)}, u32[]{:S(2)}) collective-permute-start(bf16[512,512]{1,0:T(8,128)(2,1)S(1)} %bitcast.32), channel_id=1, source_target_pairs={{0,10},{1,7},{16,26},{17,23},{32,42},{33,39},{48,58},{49,55},{64,7... | collective-permute-start | bytes 1572872 | tf_op jit(solution)/shard_map/panels/ppermute | solution.py:108
  32.8 20.0 %collective-permute-start.7 = (bf16[512,512]{1,0:T(8,128)(2,1)S(1)}, bf16[512,512]{1,0:T(8,128)(2,1)}, u32[]{:S(2)}, u32[]{:S(2)}) collective-permute-start(bf16[512,512]{1,0:T(8,128)(2,1)S(1)} %broadcast_select_fusion.1), channel_id=1, source_target_pairs={{0,12},{10,4},{1,5},{7,13},{16,28},{26,20},{17,21},{23,29},{32,44}... | collective-permute-start | bytes 1572872 | tf_op jit(solution)/shard_map/panels/ppermute | solution.py:108
  36.1 21.4 %all-to-all-start.1 = ((bf16[16,32,1024]{2,1,0:T(8,128)(2,1)}), bf16[16,32,1024]{2,1,0:T(8,128)(2,1)S(1)}, u32[]{:S(2)}, u32[]{:S(2)}) async-start(bf16[16,32,1024]{2,1,0:T(8,128)(2,1)} %broadcast_in_dim.14), calls=%async_computation.1 | async-start | bytes 2097152 | tf_op jit(solution)/shard_map/gather_rows/all_to_all | solution.py:171
  42.4 4.1 %collective-permute-start.2 = (bf16[32,512]{1,0:T(8,128)(2,1)S(1)}, bf16[32,512]{1,0:T(8,128)(2,1)S(1)}, u32[]{:S(2)}, u32[]{:S(2)}) collective-permute-start(bf16[32,512]{1,0:T(8,128)(2,1)S(1)} %slice_bitcast_fusion), channel_id=1, source_target_pairs={{0,12},{1,13},{16,28},{17,29},{32,44},{33,45},{48,60},{49,61},{64,... | collective-permute-start | bytes 98312 | tf_op jit(solution)/shard_map/diagonal/ppermute | solution.py:145
  43.7 2.8 %collective-permute-start.1 = (bf16[32,512]{1,0:T(8,128)(2,1)S(1)}, bf16[32,512]{1,0:T(8,128)(2,1)S(1)}, u32[]{:S(2)}, u32[]{:S(2)}) collective-permute-start(bf16[32,512]{1,0:T(8,128)(2,1)S(1)} %slice_bitcast_fusion), channel_id=1, source_target_pairs={{0,8},{1,9},{16,24},{17,25},{32,40},{33,41},{48,56},{49,57},{64,72... | collective-permute-start | bytes 98312 | tf_op jit(solution)/shard_map/diagonal/ppermute | solution.py:145
  45.2 2.3 %collective-permute-start = (bf16[32,512]{1,0:T(8,128)(2,1)S(1)}, bf16[32,512]{1,0:T(8,128)(2,1)S(1)}, u32[]{:S(2)}, u32[]{:S(2)}) collective-permute-start(bf16[32,512]{1,0:T(8,128)(2,1)S(1)} %slice_bitcast_fusion), channel_id=1, source_target_pairs={{0,4},{1,5},{16,20},{17,21},{32,36},{33,37},{48,52},{49,53},{64,68... | collective-permute-start | bytes 98312 | tf_op jit(solution)/shard_map/diagonal/ppermute | solution.py:145
  47.6 5.3 %collective-permute-start.5 = (bf16[32,512]{1,0:T(8,128)(2,1)S(1)}, bf16[32,512]{1,0:T(8,128)(2,1)S(1)}, u32[]{:S(2)}, u32[]{:S(2)}) collective-permute-start(bf16[32,512]{1,0:T(8,128)(2,1)S(1)} %add_select_fusion), channel_id=1, source_target_pairs={{0,3},{1,2},{4,7},{5,6},{8,11},{9,10},{12,15},{13,14},{16,19},{17,... | collective-permute-start | bytes 98312 | tf_op jit(solution)/shard_map/diagonal/ppermute | solution.py:154
  48.9 4.1 %collective-permute-start.4 = (bf16[32,512]{1,0:T(8,128)(2,1)S(1)}, bf16[32,512]{1,0:T(8,128)(2,1)S(1)}, u32[]{:S(2)}, u32[]{:S(2)}) collective-permute-start(bf16[32,512]{1,0:T(8,128)(2,1)S(1)} %add_select_fusion), channel_id=1, source_target_pairs={{0,2},{1,3},{4,6},{5,7},{8,10},{9,11},{12,14},{13,15},{16,18},{17,... | collective-permute-start | bytes 98312 | tf_op jit(solution)/shard_map/diagonal/ppermute | solution.py:153
  50.1 5.0 %collective-permute-start.3 = (bf16[32,512]{1,0:T(8,128)(2,1)S(1)}, bf16[32,512]{1,0:T(8,128)(2,1)S(1)}, u32[]{:S(2)}, u32[]{:S(2)}) collective-permute-start(bf16[32,512]{1,0:T(8,128)(2,1)S(1)} %add_select_fusion), channel_id=1, source_target_pairs={{0,1},{1,0},{4,5},{5,4},{8,9},{9,8},{12,13},{13,12},{16,17},{17,16... | collective-permute-start | bytes 98312 | tf_op jit(solution)/shard_map/diagonal/ppermute | solution.py:152
  57.4 9.3 %collective-permute-start.8 = (bf16[512,512]{1,0:T(8,128)(2,1)S(1)}, bf16[512,512]{1,0:T(8,128)(2,1)}, u32[]{:S(2)}, u32[]{:S(2)}) collective-permute-start(bf16[512,512]{1,0:T(8,128)(2,1)S(1)} %broadcast_select_fusion.2), channel_id=1, source_target_pairs={{0,2},{4,6},{10,8},{12,14},{1,15},{13,11},{7,9},{5,3},{16,18},{20,... | collective-permute-start | bytes 1572872 | tf_op jit(solution)/shard_map/panels/ppermute | solution.py:108
  60.6 18.6 %all-to-all-start.2 = ((bf16[16,2,32,512]{3,2,1,0:T(8,128)(2,1)}), bf16[16,2,32,512]{3,2,1,0:T(8,128)(2,1)S(1)}, u32[]{:S(2)}, u32[]{:S(2)}) async-start(bf16[16,2,32,512]{3,2,1,0:T(8,128)(2,1)} %broadcast_in_dim.15), calls=%async_computation.2 | async-start | bytes 2097152 | tf_op jit(solution)/shard_map/diagonal/all_to_all | solution.py:171
  66.7 24.0 %copy-start = (bf16[512,512]{1,0:T(8,128)(2,1)}, bf16[512,512]{1,0:T(8,128)(2,1)S(1)}, u32[]{:S(2)}) copy-start(bf16[512,512]{1,0:T(8,128)(2,1)S(1)} %broadcast_select_fusion.held) | copy-start | bytes 1572868
  66.8 15.8 %collective-permute-start.9 = (bf16[512,512]{1,0:T(8,128)(2,1)S(1)}, bf16[512,512]{1,0:T(8,128)(2,1)S(1)}, u32[]{:S(2)}, u32[]{:S(2)}) collective-permute-start(bf16[512,512]{1,0:T(8,128)(2,1)S(1)} %broadcast_select_fusion.held), channel_id=1, source_target_pairs={{0,15},{1,2},{2,1},{3,4},{4,3},{5,6},{6,5},{7,8},{8,7},{9,10},{10,... | collective-permute-start | bytes 1572872 | tf_op jit(solution)/shard_map/panels/ppermute | solution.py:116
  73.7 16.2 %collective-permute-start.11 = (bf16[512,1024]{1,0:T(8,128)(2,1)S(1)}, bf16[512,1024]{1,0:T(8,128)(2,1)}, u32[]{:S(2)}, u32[]{:S(2)}) collective-permute-start(bf16[512,1024]{1,0:T(8,128)(2,1)S(1)} %bitcast.25), channel_id=1, source_target_pairs={{0,16},{16,0},{32,48},{48,32},{64,80},{80,64},{96,112},{112,96},{1... | collective-permute-start | bytes 3145736 | tf_op jit(solution)/shard_map/gather_rows/ppermute | solution.py:190
  79.2 11.5 %copy-start.2 = (f32[2,512,512]{2,1,0:T(8,128)S(1)}, f32[2,512,512]{2,1,0:T(8,128)}, u32[]{:S(2)}) copy-start(f32[2,512,512]{2,1,0:T(8,128)} %approx.1) | copy-start | bytes 6291460
  82.5 8.2 %copy-start.3 = (bf16[512,512]{1,0:T(8,128)(2,1)}, bf16[512,512]{1,0:T(8,128)(2,1)S(1)}, u32[]{:S(2)}) copy-start(bf16[512,512]{1,0:T(8,128)(2,1)S(1)} %collective-permute-done.9.other) | copy-start | bytes 1572868
  82.5 8.2 %collective-permute-start.10 = (bf16[16,2,32,512]{3,2,1,0:T(8,128)(2,1)S(1)}, bf16[16,2,32,512]{3,2,1,0:T(8,128)(2,1)S(1)}, u32[]{:S(2)}, u32[]{:S(2)}) collective-permute-start(bf16[16,2,32,512]{3,2,1,0:T(8,128)(2,1)S(1)} %all-to-all-done.2.own_diag), channel_id=1, source_target_pairs={{0,16},{16,0},{32,48},{48,32},{64,80},{80,64},{96,112},{112,96},{1... | collective-permute-start | bytes 3145736 | tf_op jit(solution)/shard_map/diagonal/ppermute | solution.py:200
  90.7 1.0 %copy-start.1 = (bf16[512,512]{1,0:T(8,128)(2,1)S(1)}, bf16[512,512]{1,0:T(8,128)(2,1)}, u32[]{:S(2)}) copy-start(bf16[512,512]{1,0:T(8,128)(2,1)} %copy-done) | copy-start | bytes 1572868
  91.7 1.0 %copy-start.4 = (bf16[512,512]{1,0:T(8,128)(2,1)S(1)}, bf16[512,512]{1,0:T(8,128)(2,1)}, u32[]{:S(2)}) copy-start(bf16[512,512]{1,0:T(8,128)(2,1)} %copy-done.3) | copy-start | bytes 1572868
